TPU v7x, 32 devices: a whole 2x2x4 slice. The times are simulated.
32 devices in a mesh: dp: 8 (over z, x), tensor: 4 (over y, core).
Axes of the slice: x: 2, y: 2, z: 4, core: 2. Of those that a mesh axis runs over, the one named last changes fastest.
Arguments:
- layer_in: bfloat16 [2, 4096, 1536], P(None, 'dp'), may hold values from -6 to 6
- short_lengths: int32 [8, 4], P('dp'), may hold values from 1 to 160, 512 in all within a row
- long_lengths: int32 [8, 3], P('dp'), may hold values from 1 to 256, 512 in all within a row
- norm1_gain: float32 [1536], replicated, may hold values from 0.5 to 1.5
- query_weight: bfloat16 [1536, 1536], P(None, 'tensor'), may hold values from -0.15625 to 0.15625
- key_weight: bfloat16 [1536, 1536], P(None, 'tensor'), may hold values from -0.15625 to 0.15625
- value_weight: bfloat16 [1536, 1536], P(None, 'tensor'), may hold values from -0.15625 to 0.15625
- lambda_param: float32 [12, 256], P('tensor'), may hold values from -0.12 to 0.12
- sub_gain: float32 [12, 128], P('tensor'), may hold values from 0.5 to 1.5
- out_weight: bfloat16 [1536, 1536], P('tensor'), may hold values from -0.625 to 0.625
- norm2_gain: float32 [1536], replicated, may hold values from 0.5 to 1.5
- gate_weight: bfloat16 [1536, 4096], P(None, 'tensor'), may hold values from -0.15625 to 0.15625
- up_weight: bfloat16 [1536, 4096], P(None, 'tensor'), may hold values from -0.15625 to 0.15625
- down_weight: bfloat16 [4096, 1536], P('tensor'), may hold values from -0.125 to 0.125
- out_cotangent: bfloat16 [2, 4096, 1536], P(None, 'dp'), may hold values from -6 to 6
Outputs:
- layer_out: bfloat16 [2, 4096, 1536], P(None, 'dp')
- grad_in: bfloat16 [2, 4096, 1536], P(None, 'dp')
- grad_norm1: float32 [1536], P('dp')
- grad_query: float32 [1536, 1536], P('dp', 'tensor')
- grad_key: float32 [1536, 1536], P('dp', 'tensor')
- grad_value: float32 [1536, 1536], P('dp', 'tensor')
- grad_lambda: float32 [12, 256], P('tensor', 'dp')
- grad_sub_gain: float32 [12, 128], P('tensor', 'dp')
- grad_out: float32 [1536, 1536], P('tensor', 'dp')
- grad_norm2: float32 [1536], P('dp')
- grad_gate: float32 [1536, 4096], P('dp', 'tensor')
- grad_up: float32 [1536, 4096], P('dp', 'tensor')
- grad_down: float32 [4096, 1536], P('tensor', 'dp')
Inputs may be any that keep to these rules, and one draw needn't show every extreme that they name: `short_lengths`: each row gives, in order, the lengths of the documents packed into one block of 512 rows of micro-batch 0; a row sums to 512. `long_lengths`: each row gives, in order, the lengths of the documents packed into one block of 512 rows of micro-batch 1; a row sums to 512.
All inputs are finite; a program needn't handle non-finite values.
Results may differ from a plain program's by a relative error of at most 0.015.
The roundings to bfloat16 on the way count: a program that leaves them out, or rounds other values in their place, can miss the bound.
Values sent between devices are 32-bit elements; how exact they have to be, the bound alone decides.
A program may use at most 256 MiB of HBM per device.

v0:
```python
import math

import jax
import jax.numpy as jnp
from jax import lax
from jax.sharding import PartitionSpec as P

norm_epsilon = 1e-05
lambda_base = 0.8 - 0.6 * math.exp(-0.3 * 11.0)
rotary_base = 10000.0
floor_score = -60.0


def doc_tables(lengths, row_count):
    doc_ends = jnp.cumsum(lengths, dtype=jnp.int32)
    places = jnp.arange(row_count, dtype=jnp.int32)
    passed = (places[:, None] >= doc_ends[None, :]).astype(jnp.int32)
    segment = jnp.sum(passed, axis=1, dtype=jnp.int32)
    starts = jnp.sum(passed * lengths[None, :], axis=1, dtype=jnp.int32)
    allowed = (segment[:, None] == segment[None, :]) & (places[None, :] <= places[:, None])
    return (places - starts, allowed)


def rotary_tables(position, map_width):
    half_width = map_width // 2
    frequency = rotary_base ** (-2.0 * jnp.arange(half_width, dtype=jnp.float32) / map_width)
    angles = position.astype(jnp.float32)[:, None] * frequency[None, :]
    return (jnp.cos(angles), jnp.sin(angles))


def rotate(values, cosine_table, sine_table):
    half_width = values.shape[-1] // 2
    first_half = values[..., :half_width]
    second_half = values[..., half_width:]
    cos_wide = cosine_table[:, None, None, :]
    sin_wide = sine_table[:, None, None, :]
    return jnp.concatenate(
        [
            first_half * cos_wide - second_half * sin_wide,
            second_half * cos_wide + first_half * sin_wide,
        ],
        axis=-1,
    )


def rotate_back(values, cosine_table, sine_table):
    half_width = values.shape[-1] // 2
    first_half = values[..., :half_width]
    second_half = values[..., half_width:]
    cos_wide = cosine_table[:, None, None, :]
    sin_wide = sine_table[:, None, None, :]
    return jnp.concatenate(
        [
            first_half * cos_wide + second_half * sin_wide,
            second_half * cos_wide - first_half * sin_wide,
        ],
        axis=-1,
    )


def rms_back(incoming, values, inverse_root):
    return inverse_root * incoming - values * inverse_root**3 * jnp.mean(
        incoming * values, axis=-1, keepdims=True
    )


def micro_batch(row_in, row_cot, lengths, weight_set):
    (
        norm1_gain,
        query_weight,
        key_weight,
        value_weight,
        lambda_param,
        sub_gain,
        out_weight,
        norm2_gain,
        gate_weight,
        up_weight,
        down_weight,
    ) = weight_set
    row_count = row_in.shape[0]
    head_count = lambda_param.shape[0]
    map_width = lambda_param.shape[1] // 4
    value_width = sub_gain.shape[1]
    score_scale = map_width ** (-0.5)
    position, allowed = doc_tables(lengths, row_count)
    cosine_table, sine_table = rotary_tables(position, map_width)
    inputs = row_in.astype(jnp.float32)
    root_one = lax.rsqrt(jnp.mean(inputs * inputs, axis=-1, keepdims=True) + norm_epsilon)
    normed_one = (inputs * root_one * norm1_gain).astype(jnp.bfloat16)
    query_raw = jnp.dot(normed_one, query_weight, preferred_element_type=jnp.float32).reshape(
        row_count, head_count, 2, map_width
    )
    query_rows = rotate(query_raw, cosine_table, sine_table).astype(jnp.bfloat16)
    key_raw = jnp.dot(normed_one, key_weight, preferred_element_type=jnp.float32).reshape(
        row_count, head_count, 2, map_width
    )
    key_rows = rotate(key_raw, cosine_table, sine_table).astype(jnp.bfloat16)
    value_rows = (
        jnp.dot(normed_one, value_weight, preferred_element_type=jnp.float32)
        .astype(jnp.bfloat16)
        .reshape(row_count, head_count, value_width)
    )
    lambda_parts = lambda_param.reshape(head_count, 4, map_width)
    first_exp = jnp.exp(jnp.sum(lambda_parts[:, 0] * lambda_parts[:, 1], axis=-1))
    second_exp = jnp.exp(jnp.sum(lambda_parts[:, 2] * lambda_parts[:, 3], axis=-1))
    lambda_head = first_exp - second_exp + lambda_base

    def raw_scores():
        return (
            jnp.einsum("thmd,shmd->hmts", query_rows, key_rows, preferred_element_type=jnp.float32)
            * score_scale
        )

    scores = raw_scores()
    row_max = jnp.max(jnp.where(allowed, scores, floor_score), axis=-1, keepdims=True)
    expanded = jnp.where(allowed, jnp.exp(jnp.where(allowed, scores - row_max, 0.0)), 0.0)
    row_total = jnp.sum(expanded, axis=-1, keepdims=True)
    log_total = row_max + jnp.log(row_total)
    softmax_maps = expanded / row_total
    combined = (softmax_maps[:, 0] - lambda_head[:, None, None] * softmax_maps[:, 1]).astype(
        jnp.bfloat16
    )
    mixed = jnp.einsum("hts,shd->thd", combined, value_rows, preferred_element_type=jnp.float32)
    root_sub = lax.rsqrt(jnp.mean(mixed * mixed, axis=-1, keepdims=True) + norm_epsilon)
    sub_scale = sub_gain * (1.0 - lambda_base)
    heads_out = (
        (mixed * root_sub * sub_scale)
        .astype(jnp.bfloat16)
        .reshape(row_count, head_count * value_width)
    )
    attended = lax.psum(
        jnp.dot(heads_out, out_weight, preferred_element_type=jnp.float32), "tensor"
    )
    middle = inputs + attended
    root_two = lax.rsqrt(jnp.mean(middle * middle, axis=-1, keepdims=True) + norm_epsilon)
    normed_two = (middle * root_two * norm2_gain).astype(jnp.bfloat16)
    gate_pre = jnp.dot(normed_two, gate_weight, preferred_element_type=jnp.float32)
    upward = jnp.dot(normed_two, up_weight, preferred_element_type=jnp.float32)
    sigmoid_gate = jax.nn.sigmoid(gate_pre)
    hidden = (gate_pre * sigmoid_gate * upward).astype(jnp.bfloat16)
    fed = lax.psum(jnp.dot(hidden, down_weight, preferred_element_type=jnp.float32), "tensor")
    layer_rows = (middle + fed).astype(jnp.bfloat16)
    cot_values = row_cot.astype(jnp.float32)
    grad_down_w = jnp.einsum("tf,td->fd", hidden, row_cot, preferred_element_type=jnp.float32)
    grad_hidden = jnp.einsum("td,fd->tf", row_cot, down_weight, preferred_element_type=jnp.float32)
    grad_gate_pre = (
        grad_hidden * upward * sigmoid_gate * (1.0 + gate_pre * (1.0 - sigmoid_gate))
    ).astype(jnp.bfloat16)
    grad_up_pre = (grad_hidden * gate_pre * sigmoid_gate).astype(jnp.bfloat16)
    grad_gate_w = jnp.einsum(
        "td,tf->df", normed_two, grad_gate_pre, preferred_element_type=jnp.float32
    )
    grad_up_w = jnp.einsum("td,tf->df", normed_two, grad_up_pre, preferred_element_type=jnp.float32)
    ffn_partial = jnp.einsum(
        "tf,df->td", grad_gate_pre, gate_weight, preferred_element_type=jnp.float32
    ) + jnp.einsum("tf,df->td", grad_up_pre, up_weight, preferred_element_type=jnp.float32)
    grad_normed_two = lax.psum(ffn_partial, "tensor")
    grad_norm2 = jnp.sum(grad_normed_two * middle * root_two, axis=0)
    grad_middle = cot_values + rms_back(grad_normed_two * norm2_gain, middle, root_two)
    grad_attended = grad_middle.astype(jnp.bfloat16)
    grad_out_w = jnp.einsum(
        "tc,td->cd", heads_out, grad_attended, preferred_element_type=jnp.float32
    )
    grad_heads = jnp.einsum(
        "td,cd->tc", grad_attended, out_weight, preferred_element_type=jnp.float32
    ).reshape(row_count, head_count, value_width)
    grad_sub = jnp.sum(grad_heads * mixed * root_sub, axis=0) * (1.0 - lambda_base)
    grad_mixed = rms_back(grad_heads * sub_scale, mixed, root_sub).astype(jnp.bfloat16)
    maps_again = jnp.where(allowed, jnp.exp(jnp.where(allowed, raw_scores() - log_total, 0.0)), 0.0)
    first_map = maps_again[:, 0]
    second_map = maps_again[:, 1]
    combined_again = (first_map - lambda_head[:, None, None] * second_map).astype(jnp.bfloat16)
    grad_combined = jnp.einsum(
        "thd,shd->hts", grad_mixed, value_rows, preferred_element_type=jnp.float32
    )
    grad_value = (
        jnp.einsum("hts,thd->shd", combined_again, grad_mixed, preferred_element_type=jnp.float32)
        .astype(jnp.bfloat16)
        .reshape(row_count, head_count * value_width)
    )
    grad_lambda_head = -jnp.sum(grad_combined * second_map, axis=(1, 2))
    grad_first = first_map * (
        grad_combined - jnp.sum(grad_combined * first_map, axis=-1, keepdims=True)
    )
    second_in = -lambda_head[:, None, None] * grad_combined
    grad_second = second_map * (second_in - jnp.sum(second_in * second_map, axis=-1, keepdims=True))
    grad_scores = jnp.stack([grad_first, grad_second], axis=1).astype(jnp.bfloat16)
    grad_query_roped = (
        jnp.einsum("hmts,shmd->thmd", grad_scores, key_rows, preferred_element_type=jnp.float32)
        * score_scale
    )
    grad_key_roped = (
        jnp.einsum("hmts,thmd->shmd", grad_scores, query_rows, preferred_element_type=jnp.float32)
        * score_scale
    )
    grad_query = (
        rotate_back(grad_query_roped, cosine_table, sine_table)
        .astype(jnp.bfloat16)
        .reshape(row_count, head_count * 2 * map_width)
    )
    grad_key = (
        rotate_back(grad_key_roped, cosine_table, sine_table)
        .astype(jnp.bfloat16)
        .reshape(row_count, head_count * 2 * map_width)
    )
    grad_query_w = jnp.einsum(
        "td,tc->dc", normed_one, grad_query, preferred_element_type=jnp.float32
    )
    grad_key_w = jnp.einsum("td,tc->dc", normed_one, grad_key, preferred_element_type=jnp.float32)
    grad_value_w = jnp.einsum(
        "td,tc->dc", normed_one, grad_value, preferred_element_type=jnp.float32
    )
    attn_partial = jnp.einsum(
        "tc,dc->td", grad_query, query_weight, preferred_element_type=jnp.float32
    )
    attn_partial = attn_partial + jnp.einsum(
        "tc,dc->td", grad_key, key_weight, preferred_element_type=jnp.float32
    )
    attn_partial = attn_partial + jnp.einsum(
        "tc,dc->td", grad_value, value_weight, preferred_element_type=jnp.float32
    )
    grad_normed_one = lax.psum(attn_partial, "tensor")
    grad_norm1 = jnp.sum(grad_normed_one * inputs * root_one, axis=0)
    grad_rows = (grad_middle + rms_back(grad_normed_one * norm1_gain, inputs, root_one)).astype(
        jnp.bfloat16
    )
    first_scale = (grad_lambda_head * first_exp)[:, None]
    second_scale = (grad_lambda_head * second_exp)[:, None]
    lambda_grad = jnp.stack(
        [
            first_scale * lambda_parts[:, 1],
            first_scale * lambda_parts[:, 0],
            -second_scale * lambda_parts[:, 3],
            -second_scale * lambda_parts[:, 2],
        ],
        axis=1,
    ).reshape(head_count, 4 * map_width)
    row_grads = (
        grad_norm1,
        grad_query_w,
        grad_key_w,
        grad_value_w,
        grad_gate_w,
        grad_up_w,
        grad_norm2,
    )
    col_grads = (grad_out_w, grad_down_w, lambda_grad, grad_sub)
    return (layer_rows, grad_rows, row_grads, col_grads)


def on_device(
    layer_in,
    short_lengths,
    long_lengths,
    norm1_gain,
    query_weight,
    key_weight,
    value_weight,
    lambda_param,
    sub_gain,
    out_weight,
    norm2_gain,
    gate_weight,
    up_weight,
    down_weight,
    out_cotangent,
):
    weight_set = (
        norm1_gain,
        query_weight,
        key_weight,
        value_weight,
        lambda_param,
        sub_gain,
        out_weight,
        norm2_gain,
        gate_weight,
        up_weight,
        down_weight,
    )
    doc_lengths = (short_lengths[0], long_lengths[0])
    out_blocks = []
    grad_blocks = []
    row_total = ()
    col_total = ()
    for batch_index in range(2):
        layer_rows, grad_rows, row_grads, col_grads = micro_batch(
            layer_in[batch_index], out_cotangent[batch_index], doc_lengths[batch_index], weight_set
        )
        row_grads = (
            lax.psum_scatter(row_grads[0], "dp", scatter_dimension=0, tiled=True),
            lax.psum_scatter(row_grads[1], "dp", scatter_dimension=0, tiled=True),
            lax.psum_scatter(row_grads[2], "dp", scatter_dimension=0, tiled=True),
            lax.psum_scatter(row_grads[3], "dp", scatter_dimension=0, tiled=True),
            lax.psum_scatter(row_grads[4], "dp", scatter_dimension=0, tiled=True),
            lax.psum_scatter(row_grads[5], "dp", scatter_dimension=0, tiled=True),
            lax.psum_scatter(row_grads[6], "dp", scatter_dimension=0, tiled=True),
        )
        col_grads = (
            lax.psum_scatter(col_grads[0], "dp", scatter_dimension=1, tiled=True),
            lax.psum_scatter(col_grads[1], "dp", scatter_dimension=1, tiled=True),
            lax.psum_scatter(col_grads[2], "dp", scatter_dimension=1, tiled=True),
            lax.psum_scatter(col_grads[3], "dp", scatter_dimension=1, tiled=True),
        )
        if batch_index == 0:
            row_total = row_grads
            col_total = col_grads
        else:
            row_total = tuple((running + addend for running, addend in zip(row_total, row_grads)))
            col_total = tuple((running + addend for running, addend in zip(col_total, col_grads)))
        out_blocks.append(layer_rows)
        grad_blocks.append(grad_rows)
    return (
        jnp.stack(out_blocks),
        jnp.stack(grad_blocks),
        row_total[0],
        row_total[1],
        row_total[2],
        row_total[3],
        col_total[2],
        col_total[3],
        col_total[0],
        row_total[6],
        row_total[4],
        row_total[5],
        col_total[1],
    )


def solution(mesh):
    return jax.shard_map(
        on_device,
        mesh=mesh,
        in_specs=(
            P(None, "dp", None),
            P("dp", None),
            P("dp", None),
            P(),
            P(None, "tensor"),
            P(None, "tensor"),
            P(None, "tensor"),
            P("tensor", None),
            P("tensor", None),
            P("tensor", None),
            P(),
            P(None, "tensor"),
            P(None, "tensor"),
            P("tensor", None),
            P(None, "dp", None),
        ),
        out_specs=(
            P(None, "dp", None),
            P(None, "dp", None),
            P("dp"),
            P("dp", "tensor"),
            P("dp", "tensor"),
            P("dp", "tensor"),
            P("tensor", "dp"),
            P("tensor", "dp"),
            P("tensor", "dp"),
            P("dp"),
            P("dp", "tensor"),
            P("dp", "tensor"),
            P("tensor", "dp"),
        ),
        check_vma=False,
    )
```

profile of v0, /device:TPU:0, one launch (start us, length us, event | category | flops | bytes accessed | tf_op | source)
XLA Modules:
  0.0 1415.0 jit_solution(13785820956298431993)
XLA Ops:
  37.1 6.4 exponential_select_fusion
  62.8 122.4 %all-reduce.14.cloned.1.call-done = (f32[512,1536]{1,0:T(8,128)}, f32[512,1536]{1,0:T(8,128)}) async-done(((f32[512,1536]{1,0:T(8,128)}, f32[512,1536]{1,0:T(8,128)}), (f32[512,1536]{1,0:T(8,128)}, f32[512,1536]{1,0:T(8,128)})) %all-reduce.14.cloned.1.call-update) | async-done | bytes 6291472 | tf_op jit(solution)/shard_map/psum | solution.py:132
  185.2 4.7 multiply_reduce_fusion.11
  220.9 7.2 exponential_select_fusion.1
  235.1 105.8 %all-reduce.12.cloned.1.call-done = (f32[512,1536]{1,0:T(8,128)}, f32[512,1536]{1,0:T(8,128)}) async-done(((f32[512,1536]{1,0:T(8,128)}, f32[512,1536]{1,0:T(8,128)}), (f32[512,1536]{1,0:T(8,128)}, f32[512,1536]{1,0:T(8,128)})) %all-reduce.12.cloned.1.call-update) | async-done | bytes 6291472 | tf_op jit(solution)/shard_map/psum | solution.py:158
  340.9 6.2 multiply_reduce_fusion.1
  358.9 4.7 fusion.3
  371.0 4.6 fusion.160
  375.6 4.8 multiply_reduce_fusion.3
  380.4 5.8 fusion.118
  391.9 5.6 fusion.121
  449.6 4.6 convolution_add_fusion.1
  458.0 4.7 convolution_add_fusion.2
  474.5 56.0 %reduce-scatter.28.cloned.1.call-done = f32[32,3]{1,0:T(8,128)} async-done(((f32[256,3]{1,0:T(8,128)}), f32[32,3]{1,0:T(8,128)}) %reduce-scatter.28.cloned.1.call-update) | async-done | bytes 400
  531.9 222.6 %all-reduce.10.cloned.1.call-done = (f32[512,1536]{1,0:T(8,128)}, f32[512,1536]{1,0:T(8,128)}, f32[512,1536]{1,0:T(8,128)}, f32[512,1536]{1,0:T(8,128)}) async-done(((f32[512,1536]{1,0:T(8,128)}, f32[512,1536]{1,0:T(8,128)}, f32[512,1536]{1,0:T(8,128)}, f32[512,1536]{1,0:T(8,128)}), (f32[512,1536]{1,0:T(8,128)}, f32[512,1536]{1,0:T(8,128)}, f32[512,1536]{1,0:T(8,128)}, ...) | async-done | bytes 12582928 | tf_op jit(solution)/shard_map/psum | solution.py:142
  758.4 37.5 %all-reduce.2 = (f32[1536]{0:T(1024)S(1)}, f32[1536]{0:T(1024)S(1)}) all-reduce(f32[1536]{0:T(1024)S(1)} %add.310, f32[1536]{0:T(1024)S(1)} %add.317), channel_id=13, replica_groups=mesh['dp'=8,'tensor'=4] {'dp'}, use_global_device_ids=true, to_apply=%region_37.38.clone | all-reduce | flops 3072 | bytes 24576
  797.2 5.7 fusion.81
  812.4 15.5 %reduce-scatter.20.cloned.1.call-done = f32[384,192]{0,1:T(8,128)} async-done(((f32[384,1536]{0,1:T(8,128)}), f32[384,192]{0,1:T(8,128)}) %reduce-scatter.20.cloned.1.call-update) | async-done | bytes 294928 | tf_op jit(solution)/shard_map/reduce_scatter | solution.py:301
  827.9 72.1 %reduce-scatter.18.cloned.1.call-done = f32[192,384]{1,0:T(8,128)} async-done(((f32[1536,384]{1,0:T(8,128)}), f32[192,384]{1,0:T(8,128)}) %reduce-scatter.18.cloned.1.call-update) | async-done | bytes 294928 | tf_op jit(solution)/shard_map/reduce_scatter | solution.py:295
  900.1 72.1 %reduce-scatter.16.cloned.1.call-done = f32[192,384]{1,0:T(8,128)} async-done(((f32[1536,384]{1,0:T(8,128)}), f32[192,384]{1,0:T(8,128)}) %reduce-scatter.16.cloned.1.call-update) | async-done | bytes 294928 | tf_op jit(solution)/shard_map/reduce_scatter | solution.py:294
  972.2 72.1 %reduce-scatter.14.cloned.1.call-done = f32[192,384]{1,0:T(8,128)} async-done(((f32[1536,384]{1,0:T(8,128)}), f32[192,384]{1,0:T(8,128)}) %reduce-scatter.14.cloned.1.call-update) | async-done | bytes 294928 | tf_op jit(solution)/shard_map/reduce_scatter | solution.py:293
  1044.3 121.0 %reduce-scatter.24.cloned.1.call-done = f32[192,1024]{1,0:T(8,128)} async-done(((f32[1536,1024]{1,0:T(8,128)}), f32[192,1024]{1,0:T(8,128)}) %reduce-scatter.24.cloned.1.call-update) | async-done | bytes 786448 | tf_op jit(solution)/shard_map/reduce_scatter | solution.py:297
  1165.4 121.3 %reduce-scatter.22.cloned.1.call-done = f32[192,1024]{1,0:T(8,128)} async-done(((f32[1536,1024]{1,0:T(8,128)}), f32[192,1024]{1,0:T(8,128)}) %reduce-scatter.22.cloned.1.call-update) | async-done | bytes 786448 | tf_op jit(solution)/shard_map/reduce_scatter | solution.py:296
  1286.6 121.1 %reduce-scatter.26.cloned.1.call-done = f32[1024,192]{0,1:T(8,128)} async-done(((f32[1024,1536]{0,1:T(8,128)}), f32[1024,192]{0,1:T(8,128)}) %reduce-scatter.26.cloned.1.call-update) | async-done | bytes 786448 | tf_op jit(solution)/shard_map/reduce_scatter | solution.py:302
  (403 shorter events, 193.6 us)
Async XLA Ops:
  7.2 194.3 %copy-start = (bf16[1024,1536]{1,0:T(8,128)(2,1)S(1)}, bf16[1024,1536]{1,0:T(8,128)(2,1)}, u32[]{:S(2)}) copy-start(bf16[1024,1536]{1,0:T(8,128)(2,1)} %param.28) | copy-start | bytes 9437188
  7.2 178.0 %all-reduce.14.cloned.1.call-start = ((), (), s32[]{:S(2)}) async-start(), calls=%async_computation.20 | async-start | bytes 12582912 | tf_op jit(solution)/shard_map/psum | solution.py:132
  15.3 9.1 copy-start.97
  15.3 10.0 copy-start.108
  25.4 19.6 %copy-start.37 = (bf16[512,384]{0,1:T(8,128)(2,1)}, bf16[512,384]{0,1:T(8,128)(2,1)S(1)}, u32[]{:S(2)}) copy-start(bf16[512,384]{0,1:T(8,128)(2,1)S(1)} %fusion.157) | copy-start | bytes 1179652
  45.0 10.6 copy-start.114
  48.4 8.5 copy-start.21
  62.5 278.4 %all-reduce.12.cloned.1.call-start = ((), (), s32[]{:S(2)}) async-start(), calls=%async_computation.19 | async-start | bytes 12582912 | tf_op jit(solution)/shard_map/psum | solution.py:158
  205.1 8.5 copy-start.127
  220.8 252.4 %reduce-scatter.30.cloned.1.call-start = ((), (), s32[]{:S(2)}) async-start(), calls=%async_computation.17 | async-start | bytes 73728
  340.9 7.4 copy-start.26
  340.9 8.3 copy-start.27
  405.8 124.7 %reduce-scatter.28.cloned.1.call-start = ((), (), s32[]{:S(2)}) async-start(), calls=%async_computation.16 | async-start | bytes 147456
  413.7 340.8 %all-reduce.10.cloned.1.call-start = ((), (), s32[]{:S(2)}) async-start(), calls=%async_computation.18 | async-start | bytes 25165824 | tf_op jit(solution)/shard_map/psum | solution.py:142
  424.2 403.7 %reduce-scatter.20.cloned.1.call-start = ((), (), s32[]{:S(2)}) async-start(), calls=%async_computation.12 | async-start | bytes 2654208 | tf_op jit(solution)/shard_map/reduce_scatter | solution.py:301
  430.8 469.3 %reduce-scatter.18.cloned.1.call-start = ((), (), s32[]{:S(2)}) async-start(), calls=%async_computation.11 | async-start | bytes 2654208 | tf_op jit(solution)/shard_map/reduce_scatter | solution.py:295
  435.7 536.5 %reduce-scatter.16.cloned.1.call-start = ((), (), s32[]{:S(2)}) async-start(), calls=%async_computation.10 | async-start | bytes 2654208 | tf_op jit(solution)/shard_map/reduce_scatter | solution.py:294
  440.9 603.5 %reduce-scatter.14.cloned.1.call-start = ((), (), s32[]{:S(2)}) async-start(), calls=%async_computation.9 | async-start | bytes 2654208 | tf_op jit(solution)/shard_map/reduce_scatter | solution.py:293
  445.8 719.6 %reduce-scatter.24.cloned.1.call-start = ((), (), s32[]{:S(2)}) async-start(), calls=%async_computation.14 | async-start | bytes 7077888 | tf_op jit(solution)/shard_map/reduce_scatter | solution.py:297
  454.2 832.4 %reduce-scatter.22.cloned.1.call-start = ((), (), s32[]{:S(2)}) async-start(), calls=%async_computation.13 | async-start | bytes 7077888 | tf_op jit(solution)/shard_map/reduce_scatter | solution.py:296
  462.7 945.0 %reduce-scatter.26.cloned.1.call-start = ((), (), s32[]{:S(2)}) async-start(), calls=%async_computation.15 | async-start | bytes 7077888 | tf_op jit(solution)/shard_map/reduce_scatter | solution.py:302
  754.5 42.7 %copy-start.110 = (f32[512]{0:T(512)S(1)}, f32[512]{0:T(512)}, u32[]{:S(2)}) copy-start(f32[512]{0:T(512)} %get-tuple-element.121) | copy-start | bytes 6148
  754.5 42.7 %copy-start.111 = (f32[512]{0:T(512)S(1)}, f32[512]{0:T(512)}, u32[]{:S(2)}) copy-start(f32[512]{0:T(512)} %get-tuple-element.146) | copy-start | bytes 6148
  809.8 598.0 %copy-start.1 = (bf16[1024,1536]{1,0:T(8,128)(2,1)S(1)}, bf16[1024,1536]{1,0:T(8,128)(2,1)}, u32[]{:S(2)}) copy-start(bf16[1024,1536]{1,0:T(8,128)(2,1)} %param.28) | copy-start | bytes 9437188
  (119 other events, 359.0 us)
Sparse Core Ops, SparseCore 0:
  62.7 122.4 all-reduce.13
  220.9 119.9 all-reduce.11
  406.0 61.4 reduce-scatter.29
  470.6 59.9 reduce-scatter.27
  533.7 220.7 all-reduce.9
  758.4 69.4 reduce-scatter.19
  832.0 68.0 reduce-scatter.17
  904.1 68.0 reduce-scatter.15
  976.3 68.0 reduce-scatter.13
  1048.3 116.9 reduce-scatter.23
  1169.5 117.0 reduce-scatter.21
  1290.6 117.0 reduce-scatter.25
where the time goes:
time: 1420 us
  waiting for transfers between devices  1100 us (77%)
  matrix products  161 us (11%)
  other arithmetic  67.2 us (5%)
  blocking collectives  37.5 us (3%)
  local copies, waits for them, and re-layouts  28.6 us (2%)
  between operations  16.8 us (1%)
    psum x1, waiting for transfers between devices, micro_batch(): lax.psum(jnp.dot(hidden, down_weight, preferred_element_type=jnp.float32)...  223 us
    psum x1, waiting for transfers between devices, micro_batch(): lax.psum(jnp.dot(heads_out, out_weight, preferred_element_type=jnp.float3...  122 us
    reduce_scatter x1, waiting for transfers between devices, on_device(): lax.psum_scatter(row_grads[4], 'dp', scatter_dimension=0, tiled=True)  121 us
    reduce_scatter x1, waiting for transfers between devices, on_device(): lax.psum_scatter(col_grads[1], 'dp', scatter_dimension=1, tiled=True)  121 us
    reduce_scatter x1, waiting for transfers between devices, on_device(): lax.psum_scatter(row_grads[5], 'dp', scatter_dimension=0, tiled=True)  121 us
    psum x1, waiting for transfers between devices, micro_batch(): grad_normed_two = lax.psum(ffn_partial, 'tensor')  106 us
    reduce_scatter x1, waiting for transfers between devices, on_device(): lax.psum_scatter(row_grads[1], 'dp', scatter_dimension=0, tiled=True)  72.1 us
    reduce_scatter x1, waiting for transfers between devices, on_device(): lax.psum_scatter(row_grads[3], 'dp', scatter_dimension=0, tiled=True)  72.1 us
  transfers between devices with their start and end apart: 12, of which 11 were waited for; matrix products, arithmetic and copies ran while one was open for 7% of the time, Pallas kernels for 0%

commit v1 on v0

v1 whole, which is shorter than its diff:
```python
import math

import jax
import jax.numpy as jnp
from jax import lax
from jax.sharding import PartitionSpec as P

norm_epsilon = 1e-05
lambda_base = 0.8 - 0.6 * math.exp(-0.3 * 11.0)
rotary_base = 10000.0
floor_score = -60.0


def doc_tables(lengths, row_count):
    doc_ends = jnp.cumsum(lengths, dtype=jnp.int32)
    places = jnp.arange(row_count, dtype=jnp.int32)
    passed = (places[:, None] >= doc_ends[None, :]).astype(jnp.int32)
    segment = jnp.sum(passed, axis=1, dtype=jnp.int32)
    starts = jnp.sum(passed * lengths[None, :], axis=1, dtype=jnp.int32)
    allowed = (segment[:, None] == segment[None, :]) & (places[None, :] <= places[:, None])
    return (places - starts, allowed)


def rotary_tables(position, map_width):
    half_width = map_width // 2
    frequency = rotary_base ** (-2.0 * jnp.arange(half_width, dtype=jnp.float32) / map_width)
    angles = position.astype(jnp.float32)[:, None] * frequency[None, :]
    return (jnp.cos(angles), jnp.sin(angles))


def rotate(values, cosine_table, sine_table):
    half_width = values.shape[-1] // 2
    first_half = values[..., :half_width]
    second_half = values[..., half_width:]
    cos_wide = cosine_table[:, None, None, :]
    sin_wide = sine_table[:, None, None, :]
    return jnp.concatenate(
        [
            first_half * cos_wide - second_half * sin_wide,
            second_half * cos_wide + first_half * sin_wide,
        ],
        axis=-1,
    )


def rotate_back(values, cosine_table, sine_table):
    half_width = values.shape[-1] // 2
    first_half = values[..., :half_width]
    second_half = values[..., half_width:]
    cos_wide = cosine_table[:, None, None, :]
    sin_wide = sine_table[:, None, None, :]
    return jnp.concatenate(
        [
            first_half * cos_wide + second_half * sin_wide,
            second_half * cos_wide - first_half * sin_wide,
        ],
        axis=-1,
    )


def f32_dot(left, right):
    return jnp.dot(left, right, preferred_element_type=jnp.float32)


def dot_t(left, right):
    return lax.dot_general(
        left, right, (((1,), (1,)), ((), ())), preferred_element_type=jnp.float32
    )


def dot_rows(left, right):
    return lax.dot_general(
        left, right, (((0,), (0,)), ((), ())), preferred_element_type=jnp.float32
    )


def flip(values, axis_name, bit):
    size = lax.axis_size(axis_name)
    return lax.ppermute(values, axis_name, [(i, i ^ bit) for i in range(size)])


def half_rows(values, which):
    count = values.shape[0] // 2
    return lax.dynamic_slice_in_dim(values, which * count, count, 0)


def mine_first(values, core):
    return jnp.concatenate([half_rows(values, core), half_rows(values, 1 - core)], axis=0)


def in_order(values, core):
    half = values.shape[0] // 2
    swapped = jnp.concatenate([values[half:], values[:half]], 0)
    return jnp.where(core == 0, values, swapped)


def tensor_sum(keep, send):
    half = keep + flip(send, "tensor", 1)
    return half + flip(half, "tensor", 2)


def with_other(mine):
    return jnp.concatenate([mine, flip(mine, "tensor", 1)], axis=0)


def line_scatter(parts, dp_count):
    line = dp_count // 2
    place = lax.axis_index("dp") // 2
    up_in = None
    down_in = None
    own = parts
    for step in range(line - 1):
        up_at = jnp.clip(line - 1 - step + place, 0, line - 1)
        down_at = jnp.clip(step - line + 1 + place, 0, line - 1)
        up_out = lax.dynamic_index_in_dim(own, up_at, 0, keepdims=False)
        down_out = lax.dynamic_index_in_dim(own, down_at, 0, keepdims=False)
        if up_in is not None:
            up_out = up_out + up_in
            down_out = down_out + down_in
        up_in = lax.ppermute(
            up_out, "dp", [(2 * z + x, 2 * z + 2 + x) for z in range(step + 1) for x in range(2)]
        )
        down_in = lax.ppermute(
            down_out,
            "dp",
            [
                (2 * z + x, 2 * z - 2 + x)
                for z in range(line - 1, line - 2 - step, -1)
                for x in range(2)
            ],
        )
    return lax.dynamic_index_in_dim(own, place, 0, keepdims=False) + up_in + down_in


def pair_columns(values, dp_count):
    rows, width = values.shape
    line = dp_count // 2
    side = lax.axis_index("dp") % 2
    cut = values.reshape(rows, line, 2, width // dp_count)
    pick = lambda which: lax.dynamic_index_in_dim(cut, which, 2, keepdims=False).reshape(
        rows, width // 2
    )
    return pick(1 - side), pick(side)


def weight_scatter(pair, right, dp_count):
    send_left, keep_left = pair
    received = flip(dot_rows(send_left, right), "dp", 1)
    summed = dot_rows(keep_left, right) + received
    line = dp_count // 2
    return line_scatter(summed.reshape(line, -1, summed.shape[-1]), dp_count)


def rms_back(incoming, values, inverse_root):
    return inverse_root * incoming - values * inverse_root**3 * jnp.mean(
        incoming * values, axis=-1, keepdims=True
    )


def root_of(values):
    return lax.rsqrt(jnp.mean(values * values, axis=-1, keepdims=True) + norm_epsilon)


def attention_forward(row_in, lengths, weight_set, core):
    (norm1_gain, query_weight, key_weight, value_weight, lambda_param, sub_gain, out_weight) = (
        weight_set
    )
    row_count = row_in.shape[0]
    head_count = lambda_param.shape[0]
    map_width = lambda_param.shape[1] // 4
    value_width = sub_gain.shape[1]
    score_scale = map_width ** (-0.5)
    position, allowed = doc_tables(lengths, row_count)
    cosine_table, sine_table = rotary_tables(position, map_width)
    inputs = row_in.astype(jnp.float32)
    normed_one = (inputs * root_of(inputs) * norm1_gain).astype(jnp.bfloat16)
    query_raw = f32_dot(normed_one, query_weight).reshape(row_count, head_count, 2, map_width)
    query_rows = rotate(query_raw, cosine_table, sine_table).astype(jnp.bfloat16)
    key_raw = f32_dot(normed_one, key_weight).reshape(row_count, head_count, 2, map_width)
    key_rows = rotate(key_raw, cosine_table, sine_table).astype(jnp.bfloat16)
    value_rows = (
        f32_dot(normed_one, value_weight)
        .astype(jnp.bfloat16)
        .reshape(row_count, head_count, value_width)
    )
    lambda_parts = lambda_param.reshape(head_count, 4, map_width)
    first_exp = jnp.exp(jnp.sum(lambda_parts[:, 0] * lambda_parts[:, 1], axis=-1))
    second_exp = jnp.exp(jnp.sum(lambda_parts[:, 2] * lambda_parts[:, 3], axis=-1))
    lambda_head = first_exp - second_exp + lambda_base
    scores = (
        jnp.einsum("thmd,shmd->hmts", query_rows, key_rows, preferred_element_type=jnp.float32)
        * score_scale
    )
    row_max = jnp.max(jnp.where(allowed, scores, floor_score), axis=-1, keepdims=True)
    expanded = jnp.where(allowed, jnp.exp(jnp.where(allowed, scores - row_max, 0.0)), 0.0)
    row_total = jnp.sum(expanded, axis=-1, keepdims=True)
    log_total = row_max + jnp.log(row_total)
    softmax_maps = expanded / row_total
    combined = (softmax_maps[:, 0] - lambda_head[:, None, None] * softmax_maps[:, 1]).astype(
        jnp.bfloat16
    )
    mixed = jnp.einsum("hts,shd->thd", combined, value_rows, preferred_element_type=jnp.float32)
    root_sub = root_of(mixed)
    sub_scale = sub_gain * (1.0 - lambda_base)
    heads_out = (
        (mixed * root_sub * sub_scale)
        .astype(jnp.bfloat16)
        .reshape(row_count, head_count * value_width)
    )
    send = f32_dot(half_rows(heads_out, 1 - core), out_weight)
    keep = f32_dot(half_rows(heads_out, core), out_weight)
    kept = (
        allowed, cosine_table, sine_table, normed_one, query_rows, key_rows, value_rows,
        lambda_parts, first_exp, second_exp, lambda_head, log_total, mixed, root_sub, sub_scale,
        heads_out,
    )
    return keep, send, kept


def attention_backward(grad_attended, kept, weight_set, core):
    (query_weight, key_weight, value_weight, out_weight) = weight_set
    (
        allowed, cosine_table, sine_table, normed_one, query_rows, key_rows, value_rows,
        lambda_parts, first_exp, second_exp, lambda_head, log_total, mixed, root_sub, sub_scale,
        heads_out,
    ) = kept
    row_count, head_count, value_width = value_rows.shape
    map_width = query_rows.shape[-1]
    score_scale = map_width ** (-0.5)
    grad_heads = dot_t(grad_attended, out_weight).reshape(row_count, head_count, value_width)
    grad_sub = jnp.sum(grad_heads * mixed * root_sub, axis=0) * (1.0 - lambda_base)
    grad_mixed = rms_back(grad_heads * sub_scale, mixed, root_sub).astype(jnp.bfloat16)
    scores = (
        jnp.einsum("thmd,shmd->hmts", query_rows, key_rows, preferred_element_type=jnp.float32)
        * score_scale
    )
    maps_again = jnp.where(allowed, jnp.exp(jnp.where(allowed, scores - log_total, 0.0)), 0.0)
    first_map = maps_again[:, 0]
    second_map = maps_again[:, 1]
    combined_again = (first_map - lambda_head[:, None, None] * second_map).astype(jnp.bfloat16)
    grad_combined = jnp.einsum(
        "thd,shd->hts", grad_mixed, value_rows, preferred_element_type=jnp.float32
    )
    grad_value = (
        jnp.einsum("hts,thd->shd", combined_again, grad_mixed, preferred_element_type=jnp.float32)
        .astype(jnp.bfloat16)
        .reshape(row_count, head_count * value_width)
    )
    grad_lambda_head = -jnp.sum(grad_combined * second_map, axis=(1, 2))
    grad_first = first_map * (
        grad_combined - jnp.sum(grad_combined * first_map, axis=-1, keepdims=True)
    )
    second_in = -lambda_head[:, None, None] * grad_combined
    grad_second = second_map * (second_in - jnp.sum(second_in * second_map, axis=-1, keepdims=True))
    grad_scores = jnp.stack([grad_first, grad_second], axis=1).astype(jnp.bfloat16)
    grad_query_roped = (
        jnp.einsum("hmts,shmd->thmd", grad_scores, key_rows, preferred_element_type=jnp.float32)
        * score_scale
    )
    grad_key_roped = (
        jnp.einsum("hmts,thmd->shmd", grad_scores, query_rows, preferred_element_type=jnp.float32)
        * score_scale
    )
    grad_query = (
        rotate_back(grad_query_roped, cosine_table, sine_table)
        .astype(jnp.bfloat16)
        .reshape(row_count, head_count * 2 * map_width)
    )
    grad_key = (
        rotate_back(grad_key_roped, cosine_table, sine_table)
        .astype(jnp.bfloat16)
        .reshape(row_count, head_count * 2 * map_width)
    )

    def partial(which):
        return (
            dot_t(half_rows(grad_query, which), query_weight)
            + dot_t(half_rows(grad_key, which), key_weight)
            + dot_t(half_rows(grad_value, which), value_weight)
        )

    send = partial(1 - core)
    keep = partial(core)
    first_scale = (grad_lambda_head * first_exp)[:, None]
    second_scale = (grad_lambda_head * second_exp)[:, None]
    lambda_grad = jnp.stack(
        [
            first_scale * lambda_parts[:, 1],
            first_scale * lambda_parts[:, 0],
            -second_scale * lambda_parts[:, 3],
            -second_scale * lambda_parts[:, 2],
        ],
        axis=1,
    ).reshape(head_count, 4 * map_width)
    return keep, send, grad_query, grad_key, grad_value, lambda_grad, grad_sub


def feed_forward(normed_two, cot_rows, gate_weight, up_weight, down_weight):
    half = normed_two.shape[0] // 2
    gate_pre = f32_dot(normed_two, gate_weight)
    upward = f32_dot(normed_two, up_weight)
    sigmoid_gate = jax.nn.sigmoid(gate_pre)
    hidden = (gate_pre * sigmoid_gate * upward).astype(jnp.bfloat16)
    grad_hidden = dot_t(cot_rows, down_weight)
    grad_gate_pre = (
        grad_hidden * upward * sigmoid_gate * (1.0 + gate_pre * (1.0 - sigmoid_gate))
    ).astype(jnp.bfloat16)
    grad_up_pre = (grad_hidden * gate_pre * sigmoid_gate).astype(jnp.bfloat16)

    def back(at):
        return dot_t(grad_gate_pre[at], gate_weight) + dot_t(grad_up_pre[at], up_weight)

    send_back = back(slice(half, None))
    keep_back = back(slice(0, half))
    send_fed = f32_dot(hidden[half:], down_weight)
    keep_fed = f32_dot(hidden[:half], down_weight)
    return (keep_back, send_back), (keep_fed, send_fed), hidden, grad_gate_pre, grad_up_pre


def on_device(
    layer_in,
    short_lengths,
    long_lengths,
    norm1_gain,
    query_weight,
    key_weight,
    value_weight,
    lambda_param,
    sub_gain,
    out_weight,
    norm2_gain,
    gate_weight,
    up_weight,
    down_weight,
    out_cotangent,
):
    dp_count = lax.axis_size("dp")
    core = lax.axis_index("tensor") % 2
    head_count, lambda_width = lambda_param.shape
    value_width = sub_gain.shape[1]
    doc_lengths = (short_lengths[0], long_lengths[0])
    attention_weights = (
        norm1_gain, query_weight, key_weight, value_weight, lambda_param, sub_gain, out_weight,
    )
    cots = [mine_first(out_cotangent[m], core) for m in range(2)]
    cot_pair = pair_columns(jnp.concatenate(cots, 0), dp_count)
    half = cots[0].shape[0] // 2
    rows_in = [mine_first(layer_in[m], core).astype(jnp.float32) for m in range(2)]
    inputs = [rows_in[m][:half] for m in range(2)]
    front = [attention_forward(layer_in[m], doc_lengths[m], attention_weights, core) for m in range(2)]
    kept = [front[m][2] for m in range(2)]
    attended, middle, root_two, normed_two, ffn = [], [], [], [], []
    for m in range(2):
        attended.append(tensor_sum(front[m][0], front[m][1]))
        middle.append(inputs[m] + attended[m])
        root_two.append(root_of(middle[m]))
        normed_two.append((with_other(middle[m] * root_two[m]) * norm2_gain).astype(jnp.bfloat16))
        ffn.append(feed_forward(normed_two[m], cots[m], gate_weight, up_weight, down_weight))
    both = lambda index: jnp.concatenate([ffn[0][index], ffn[1][index]], 0)
    normed_two_pair = pair_columns(jnp.concatenate(normed_two, 0), dp_count)
    grad_down = weight_scatter(cot_pair, both(2), dp_count)
    grad_gate = weight_scatter(normed_two_pair, both(3), dp_count)
    grad_up = weight_scatter(normed_two_pair, both(4), dp_count)
    grad_norm2 = 0.0
    grad_norm1 = 0.0
    through_two, grad_attended, back = [], [], []
    for m in range(2):
        grad_normed_two = tensor_sum(*ffn[m][0])
        grad_norm2 = grad_norm2 + jnp.sum(grad_normed_two * middle[m] * root_two[m], axis=0)
        through_two.append(rms_back(grad_normed_two * norm2_gain, middle[m], root_two[m]))
        grad_middle = cots[m].astype(jnp.float32) + with_other(through_two[m])
        grad_attended.append(in_order(grad_middle, core).astype(jnp.bfloat16))
        back.append(
            attention_backward(
                grad_attended[m], kept[m], (query_weight, key_weight, value_weight, out_weight), core
            )
        )
    heads_both = jnp.concatenate([kept[0][-1], kept[1][-1]], 0)
    grad_out = weight_scatter(
        pair_columns(jnp.concatenate(grad_attended, 0), dp_count), heads_both, dp_count
    )
    normed_one_pair = pair_columns(jnp.concatenate([kept[0][3], kept[1][3]], 0), dp_count)
    grad_query, grad_key, grad_value = [
        weight_scatter(normed_one_pair, jnp.concatenate([back[0][i], back[1][i]], 0), dp_count)
        for i in (2, 3, 4)
    ]
    out_blocks, grad_blocks = [], []
    for m in range(2):
        fed = tensor_sum(*ffn[m][1])
        out_rows = rows_in[m] + with_other(attended[m] + fed)
        out_blocks.append(in_order(out_rows, core).astype(jnp.bfloat16))
        grad_normed_one = tensor_sum(back[m][0], back[m][1])
        root_one = root_of(inputs[m])
        grad_norm1 = grad_norm1 + jnp.sum(grad_normed_one * inputs[m] * root_one, axis=0)
        through = through_two[m] + rms_back(grad_normed_one * norm1_gain, inputs[m], root_one)
        grad_rows = cots[m].astype(jnp.float32) + with_other(through)
        grad_blocks.append(in_order(grad_rows, core).astype(jnp.bfloat16))
    norms = jnp.stack([grad_norm1, grad_norm2])
    norms = norms + flip(norms, "tensor", 1)
    small = [
        norms,
        back[0][5] + back[1][5],
        back[0][6] + back[1][6],
    ]
    width = norms.shape[-1]
    packed = jnp.concatenate(
        [
            part.reshape(part.shape[0], dp_count, -1).transpose(1, 0, 2).reshape(dp_count, -1)
            for part in small
        ],
        axis=1,
    )
    pairs = packed.reshape(dp_count // 2, 2, 1, -1)
    side = lax.axis_index("dp") % 2
    send = lax.dynamic_index_in_dim(pairs, 1 - side, 1, keepdims=False)
    keep = lax.dynamic_index_in_dim(pairs, side, 1, keepdims=False)
    small_sum = line_scatter(keep + flip(send, "dp", 1), dp_count)[0]
    sizes = [2 * width // dp_count, head_count * lambda_width // dp_count]
    norm_sum, lambda_sum, sub_sum = jnp.split(small_sum, [sizes[0], sizes[0] + sizes[1]])
    norm_sum = norm_sum.reshape(2, -1)
    return (
        jnp.stack(out_blocks),
        jnp.stack(grad_blocks),
        norm_sum[0],
        grad_query,
        grad_key,
        grad_value,
        lambda_sum.reshape(head_count, -1),
        sub_sum.reshape(head_count, -1),
        grad_out.T,
        norm_sum[1],
        grad_gate,
        grad_up,
        grad_down.T,
    )


def solution(mesh):
    return jax.shard_map(
        on_device,
        mesh=mesh,
        in_specs=(
            P(None, "dp", None),
            P("dp", None),
            P("dp", None),
            P(),
            P(None, "tensor"),
            P(None, "tensor"),
            P(None, "tensor"),
            P("tensor", None),
            P("tensor", None),
            P("tensor", None),
            P(),
            P(None, "tensor"),
            P(None, "tensor"),
            P("tensor", None),
            P(None, "dp", None),
        ),
        out_specs=(
            P(None, "dp", None),
            P(None, "dp", None),
            P("dp"),
            P("dp", "tensor"),
            P("dp", "tensor"),
            P("dp", "tensor"),
            P("tensor", "dp"),
            P("tensor", "dp"),
            P("tensor", "dp"),
            P("dp"),
            P("dp", "tensor"),
            P("dp", "tensor"),
            P("tensor", "dp"),
        ),
        check_vma=False,
    )
```

time: 1420 us -> 963 us (0.68)
  waiting for transfers between devices: 1100 us -> 377 us
  starting transfers between devices: 1.31 us -> 149 us
  other arithmetic: 67.2 us -> 144 us
  local copies, waits for them, and re-layouts: 28.6 us -> 102 us
  blocking collectives: 37.5 us -> 0 us
  matrix products: 161 us -> 181 us
    reduce_scatter x7 -> x0, waiting for transfers between devices: 595 us -> none  [the longest x1 121 us: on_device(): lax.psum_scatter(row_grads[4], 'dp', scatter_dimension=0, tiled=True)]
    psum x3 -> x0, waiting for transfers between devices: 451 us -> none  [the longest x1 223 us: micro_batch(): lax.psum(jnp.dot(hidden, down_weight, preferred_element_type=jnp.float32)...]
    ppermute x0 -> x81, waiting for transfers between devices: none -> 377 us  [the longest x33 293 us: flip(): return lax.ppermute(values, axis_name, [(i, i ^ bit) for i in range(size)])]
    ppermute x0 -> x81, starting transfers between devices: none -> 149 us  [the longest x24 100 us: line_scatter(): lax.ppermute(up_out, 'dp', [(2 * z + x, 2 * z + 2 + x) for z in range(ste...]
    unnamed x14 -> x0, waiting for transfers between devices: 56.2 us -> none
    add x9 -> x47, other arithmetic: 5.27 us -> 48 us  [the longest x16 13.8 us: line_scatter(): up_out = up_out + up_in]
    unnamed x1 -> x0, blocking collectives: 37.5 us -> none
    convert_element_type x7 -> x13, other arithmetic: 3.31 us -> 35.5 us  [the longest x2 8.04 us: on_device(): grad_attended.append(in_order(grad_middle, core).astype(jnp.bfloat16))]
  transfers between devices with their start and end apart: 12 -> 81, of which waited for: 11 -> 26; matrix products, arithmetic and copies ran while one was open for 7% -> 35% of each run, Pallas kernels for 0% -> 0%
where the time goes in v1:
time: 963 us; the launch traced here: 957 us
  waiting for transfers between devices  377 us (39%)
  matrix products  181 us (19%)
  starting transfers between devices  149 us (15%)
  other arithmetic  144 us (15%)
  local copies, waits for them, and re-layouts  102 us (11%)
    ppermute x33, waiting for transfers between devices, flip(): return lax.ppermute(values, axis_name, [(i, i ^ bit) for i in range(size)])  293 us
    ppermute x24, starting transfers between devices, line_scatter(): lax.ppermute(up_out, 'dp', [(2 * z + x, 2 * z + 2 + x) for z in range(ste...  100 us
    dot_general x18, matrix products, f32_dot(): return jnp.dot(left, right, preferred_element_type=jnp.float32)  53.9 us
    ppermute x24, waiting for transfers between devices, line_scatter(): lax.ppermute(up_out, 'dp', [(2 * z + x, 2 * z + 2 + x) for z in range(ste...  47.9 us
    dot_general x24, matrix products, dot_t(): lax.dot_general(left, right, (((1,), (1,)), ((), ())), preferred_element_...  43.5 us
    ppermute x24, waiting for transfers between devices, line_scatter(): lax.ppermute(down_out, 'dp', [(2 * z + x, 2 * z - 2 + x) for z in range(l...  36 us
    dot_general x14, matrix products, dot_rows(): lax.dot_general(left, right, (((0,), (0,)), ((), ())), preferred_element_...  31.9 us
    unnamed x412, local copies, waits for them, and re-layouts  29 us
  transfers between devices with their start and end apart: 81, of which 26 were waited for; matrix products, arithmetic and copies ran while one was open for 35% of the time, Pallas kernels for 0%

profile of v1, /device:TPU:0, one launch (start us, length us, event | category | flops | bytes accessed | tf_op | source)
XLA Modules:
  0.0 956.7 jit_solution(6975080536874256833)
XLA Ops:
  105.7 5.6 fusion.188
  119.7 6.5 exponential_select_fusion.1
  135.4 17.8 %collective-permute-done.7 = f32[256,1536]{1,0:T(8,128)} collective-permute-done((f32[256,1536]{1,0:T(8,128)}, f32[256,1536]{1,0:T(8,128)}, u32[]{:S(2)}, u32[]{:S(2)}) %collective-permute-start.7) | collective-permute-done | bytes 1572896 | tf_op jit(solution)/shard_map/ppermute | solution.py:79
  161.3 25.0 %collective-permute-done.1 = f32[256,1536]{1,0:T(8,128)} collective-permute-done((f32[256,1536]{1,0:T(8,128)}, f32[256,1536]{1,0:T(8,128)}, u32[]{:S(2)}, u32[]{:S(2)}) %collective-permute-start.1) | collective-permute-done | bytes 1572896 | tf_op jit(solution)/shard_map/ppermute | solution.py:79
  268.7 16.5 %collective-permute-done.13 = f32[256,1536]{1,0:T(8,128)S(1)} collective-permute-done((f32[256,1536]{1,0:T(8,128)S(1)}, f32[256,1536]{1,0:T(8,128)S(1)}, u32[]{:S(2)}, u32[]{:S(2)}) %collective-permute-start.13) | collective-permute-done | bytes 1572896 | tf_op jit(solution)/shard_map/ppermute | solution.py:79
  286.7 32.2 %collective-permute-done.19 = f32[256,1536]{1,0:T(8,128)S(1)} collective-permute-done((f32[256,1536]{1,0:T(8,128)S(1)}, f32[256,1536]{1,0:T(8,128)S(1)}, u32[]{:S(2)}, u32[]{:S(2)}) %collective-permute-start.19) | collective-permute-done | bytes 1572896 | tf_op jit(solution)/shard_map/ppermute | solution.py:79
  328.9 49.9 %collective-permute-done.67 = f32[768,1024]{1,0:T(8,128)} collective-permute-done((f32[768,1024]{1,0:T(8,128)}, f32[768,1024]{1,0:T(8,128)}, u32[]{:S(2)}, u32[]{:S(2)}) %collective-permute-start.67) | collective-permute-done | bytes 3145760 | tf_op jit(solution)/shard_map/ppermute | solution.py:79
  386.9 58.4 %collective-permute-done.74 = f32[768,1024]{1,0:T(8,128)} collective-permute-done((f32[768,1024]{1,0:T(8,128)}, f32[768,1024]{1,0:T(8,128)}, u32[]{:S(2)}, u32[]{:S(2)}) %collective-permute-start.74) | collective-permute-done | bytes 3145760 | tf_op jit(solution)/shard_map/ppermute | solution.py:79
  471.1 13.1 %collective-permute-done.68 = f32[192,1024]{1,0:T(8,128)S(1)} collective-permute-done((f32[192,1024]{1,0:T(8,128)}, f32[192,1024]{1,0:T(8,128)S(1)}, u32[]{:S(2)}, u32[]{:S(2)}) %collective-permute-start.68) | collective-permute-done | bytes 786464 | tf_op jit(solution)/shard_map/ppermute | solution.py:120
  486.3 12.8 %collective-permute-done.75 = f32[192,1024]{1,0:T(8,128)} collective-permute-done((f32[192,1024]{1,0:T(8,128)}, f32[192,1024]{1,0:T(8,128)}, u32[]{:S(2)}, u32[]{:S(2)}) %collective-permute-start.75) | collective-permute-done | bytes 786464 | tf_op jit(solution)/shard_map/ppermute | solution.py:120
  648.3 7.4 collective-permute-done.76
  662.3 9.9 %collective-permute-done.32 = f32[768,384]{1,0:T(8,128)S(1)} collective-permute-done((f32[768,384]{1,0:T(8,128)S(1)}, f32[768,384]{1,0:T(8,128)S(1)}, u32[]{:S(2)}, u32[]{:S(2)}) %collective-permute-start.32) | collective-permute-done | bytes 1179680 | tf_op jit(solution)/shard_map/ppermute | solution.py:79
  674.8 22.7 %collective-permute-done.39 = f32[768,384]{1,0:T(8,128)S(1)} collective-permute-done((f32[768,384]{1,0:T(8,128)S(1)}, f32[768,384]{1,0:T(8,128)S(1)}, u32[]{:S(2)}, u32[]{:S(2)}) %collective-permute-start.39) | collective-permute-done | bytes 1179680 | tf_op jit(solution)/shard_map/ppermute | solution.py:79
  697.5 5.5 collective-permute-start.63
  704.1 18.7 %collective-permute-done.46 = f32[768,384]{1,0:T(8,128)S(1)} collective-permute-done((f32[768,384]{1,0:T(8,128)S(1)}, f32[768,384]{1,0:T(8,128)S(1)}, u32[]{:S(2)}, u32[]{:S(2)}) %collective-permute-start.46) | collective-permute-done | bytes 1179680 | tf_op jit(solution)/shard_map/ppermute | solution.py:79
  725.2 21.8 %collective-permute-done.53 = f32[768,384]{1,0:T(8,128)S(1)} collective-permute-done((f32[768,384]{1,0:T(8,128)S(1)}, f32[768,384]{1,0:T(8,128)S(1)}, u32[]{:S(2)}, u32[]{:S(2)}) %collective-permute-start.53) | collective-permute-done | bytes 1179680 | tf_op jit(solution)/shard_map/ppermute | solution.py:79
  771.9 5.7 collective-permute-start.77
  779.6 11.6 %collective-permute-done.66 = f32[192,1024]{1,0:T(8,128)S(1)} collective-permute-done((f32[192,1024]{1,0:T(8,128)S(1)}, f32[192,1024]{1,0:T(8,128)S(1)}, u32[]{:S(2)}, u32[]{:S(2)}) %collective-permute-start.66) | collective-permute-done | bytes 786464 | tf_op jit(solution)/shard_map/ppermute | solution.py:123
  793.7 14.4 %collective-permute-done.73 = f32[192,1024]{1,0:T(8,128)S(1)} collective-permute-done((f32[192,1024]{1,0:T(8,128)S(1)}, f32[192,1024]{1,0:T(8,128)S(1)}, u32[]{:S(2)}, u32[]{:S(2)}) %collective-permute-start.73) | collective-permute-done | bytes 786464 | tf_op jit(solution)/shard_map/ppermute | solution.py:123
  813.8 7.5 collective-permute-done.80
  850.2 20.5 %collective-permute-start.42 = (f32[192,384]{1,0:T(8,128)S(1)}, f32[192,384]{1,0:T(8,128)S(1)}, u32[]{:S(2)}, u32[]{:S(2)}) collective-permute-start(f32[192,384]{1,0:T(8,128)S(1)} %get-tuple-element.109), channel_id=1, source_target_pairs={{0,8},{4,12},{8,16},{12,20},{16,24},{20,28},{1,9},{5,13},{9,17},{1... | collective-permute-start | bytes 884744 | tf_op jit(solution)/shard_map/ppermute | solution.py:120
  878.9 17.8 %collective-permute-done.22 = f32[256,1536]{1,0:T(8,128)S(1)} collective-permute-done((f32[256,1536]{1,0:T(8,128)S(1)}, f32[256,1536]{1,0:T(8,128)S(1)}, u32[]{:S(2)}, u32[]{:S(2)}) %collective-permute-start.22) | collective-permute-done | bytes 1572896 | tf_op jit(solution)/shard_map/ppermute | solution.py:79
  914.8 6.8 subtract_add_fusion.1
  926.2 6.9 collective-permute-start.28
  (799 shorter events, 537.6 us)
Async XLA Ops:
  60.5 65.7 %collective-permute-start = (f32[256,1536]{1,0:T(8,128)}, f32[256,1536]{1,0:T(8,128)}, u32[]{:S(2)}, u32[]{:S(2)}) collective-permute-start(f32[256,1536]{1,0:T(8,128)} %fusion.216), channel_id=1, source_target_pairs={{0,1},{1,0},{2,3},{3,2},{4,5},{5,4},{6,7},{7,6},{8,9},{9,8},{10,11... | collective-permute-start | bytes 4718600 | tf_op jit(solution)/shard_map/ppermute | solution.py:79
  129.5 56.7 %collective-permute-start.1 = (f32[256,1536]{1,0:T(8,128)}, f32[256,1536]{1,0:T(8,128)}, u32[]{:S(2)}, u32[]{:S(2)}) collective-permute-start(f32[256,1536]{1,0:T(8,128)} %convolution_add_fusion.15), channel_id=1, source_target_pairs={{0,2},{1,3},{2,0},{3,1},{4,6},{5,7},{6,4},{7,5},{8,10},{9,11},{10,... | collective-permute-start | bytes 4718600 | tf_op jit(solution)/shard_map/ppermute | solution.py:79
  240.3 83.0 %collective-permute-start.60 = (f32[768,1024]{1,0:T(8,128)S(1)}, f32[768,1024]{1,0:T(8,128)S(1)}, u32[]{:S(2)}, u32[]{:S(2)}) collective-permute-start(f32[768,1024]{1,0:T(8,128)S(1)} %fusion.104), channel_id=1, source_target_pairs={{0,4},{4,0},{8,12},{12,8},{16,20},{20,16},{24,28},{28,24},{1,5},{5... | collective-permute-start | bytes 9437192 | tf_op jit(solution)/shard_map/ppermute | solution.py:79
  252.0 66.9 %collective-permute-start.19 = (f32[256,1536]{1,0:T(8,128)S(1)}, f32[256,1536]{1,0:T(8,128)S(1)}, u32[]{:S(2)}, u32[]{:S(2)}) collective-permute-start(f32[256,1536]{1,0:T(8,128)S(1)} %fusion.59), channel_id=1, source_target_pairs={{0,2},{1,3},{2,0},{3,1},{4,6},{5,7},{6,4},{7,5},{8,10},{9,11},{10,... | collective-permute-start | bytes 4718600 | tf_op jit(solution)/shard_map/ppermute | solution.py:79
  259.5 119.4 %collective-permute-start.67 = (f32[768,1024]{1,0:T(8,128)}, f32[768,1024]{1,0:T(8,128)}, u32[]{:S(2)}, u32[]{:S(2)}) collective-permute-start(f32[768,1024]{1,0:T(8,128)} %fusion.103), channel_id=1, source_target_pairs={{0,4},{4,0},{8,12},{12,8},{16,20},{20,16},{24,28},{28,24},{1,5},{5... | collective-permute-start | bytes 9437192 | tf_op jit(solution)/shard_map/ppermute | solution.py:79
  263.4 181.9 %collective-permute-start.74 = (f32[768,1024]{1,0:T(8,128)}, f32[768,1024]{1,0:T(8,128)}, u32[]{:S(2)}, u32[]{:S(2)}) collective-permute-start(f32[768,1024]{1,0:T(8,128)} %fusion.102), channel_id=1, source_target_pairs={{0,4},{4,0},{8,12},{12,8},{16,20},{20,16},{24,28},{28,24},{1,5},{5... | collective-permute-start | bytes 9437192 | tf_op jit(solution)/shard_map/ppermute | solution.py:79
  285.2 168.6 %collective-permute-start.10 = (f32[256,1536]{1,0:T(8,128)}, f32[256,1536]{1,0:T(8,128)}, u32[]{:S(2)}, u32[]{:S(2)}) collective-permute-start(f32[256,1536]{1,0:T(8,128)} %convolution_add_fusion.4), channel_id=1, source_target_pairs={{0,2},{1,3},{2,0},{3,1},{4,6},{5,7},{6,4},{7,5},{8,10},{9,11},{10,... | collective-permute-start | bytes 4718600 | tf_op jit(solution)/shard_map/ppermute | solution.py:79
  318.9 141.0 %collective-permute-start.4 = (f32[256,1536]{1,0:T(8,128)}, f32[256,1536]{1,0:T(8,128)}, u32[]{:S(2)}, u32[]{:S(2)}) collective-permute-start(f32[256,1536]{1,0:T(8,128)} %convolution_add_fusion.5), channel_id=1, source_target_pairs={{0,2},{1,3},{2,0},{3,1},{4,6},{5,7},{6,4},{7,5},{8,10},{9,11},{10,... | collective-permute-start | bytes 4718600 | tf_op jit(solution)/shard_map/ppermute | solution.py:79
  323.3 179.7 %collective-permute-start.14 = (f32[256,1536]{1,0:T(8,128)S(1)}, f32[256,1536]{1,0:T(8,128)}, u32[]{:S(2)}, u32[]{:S(2)}) collective-permute-start(f32[256,1536]{1,0:T(8,128)S(1)} %get-tuple-element.155), channel_id=1, source_target_pairs={{0,1},{1,0},{2,3},{3,2},{4,5},{5,4},{6,7},{7,6},{8,9},{9,8},{10,11... | collective-permute-start | bytes 4718600 | tf_op jit(solution)/shard_map/ppermute | solution.py:79
  378.8 127.8 %collective-permute-start.20 = (f32[256,1536]{1,0:T(8,128)}, f32[256,1536]{1,0:T(8,128)}, u32[]{:S(2)}, u32[]{:S(2)}) collective-permute-start(f32[256,1536]{1,0:T(8,128)} %get-tuple-element.156), channel_id=1, source_target_pairs={{0,1},{1,0},{2,3},{3,2},{4,5},{5,4},{6,7},{7,6},{8,9},{9,8},{10,11... | collective-permute-start | bytes 4718600 | tf_op jit(solution)/shard_map/ppermute | solution.py:79
  468.6 93.3 %collective-permute-start.11 = (f32[256,1536]{1,0:T(8,128)}, f32[256,1536]{1,0:T(8,128)}, u32[]{:S(2)}, u32[]{:S(2)}) collective-permute-start(f32[256,1536]{1,0:T(8,128)} %add_add_fusion), channel_id=1, source_target_pairs={{0,1},{1,0},{2,3},{3,2},{4,5},{5,4},{6,7},{7,6},{8,9},{9,8},{10,11... | collective-permute-start | bytes 4718600 | tf_op jit(solution)/shard_map/ppermute | solution.py:79
  484.1 107.1 %collective-permute-start.5 = (f32[256,1536]{1,0:T(8,128)}, f32[256,1536]{1,0:T(8,128)}, u32[]{:S(2)}, u32[]{:S(2)}) collective-permute-start(f32[256,1536]{1,0:T(8,128)} %add_add_fusion.1), channel_id=1, source_target_pairs={{0,1},{1,0},{2,3},{3,2},{4,5},{5,4},{6,7},{7,6},{8,9},{9,8},{10,11... | collective-permute-start | bytes 4718600 | tf_op jit(solution)/shard_map/ppermute | solution.py:79
  499.1 139.8 %collective-permute-start.64 = (f32[192,1024]{1,0:T(8,128)}, f32[192,1024]{1,0:T(8,128)}, u32[]{:S(2)}, u32[]{:S(2)}) collective-permute-start(f32[192,1024]{1,0:T(8,128)} %get-tuple-element.66), channel_id=1, source_target_pairs={{24,16},{28,20},{25,17},{29,21},{26,18},{30,22},{27,19},{31,23}} | collective-permute-start | bytes 2359304 | tf_op jit(solution)/shard_map/ppermute | solution.py:123
  503.1 140.2 %collective-permute-start.71 = (f32[192,1024]{1,0:T(8,128)}, f32[192,1024]{1,0:T(8,128)}, u32[]{:S(2)}, u32[]{:S(2)}) collective-permute-start(f32[192,1024]{1,0:T(8,128)} %get-tuple-element.62), channel_id=1, source_target_pairs={{24,16},{28,20},{25,17},{29,21},{26,18},{30,22},{27,19},{31,23}} | collective-permute-start | bytes 2359304 | tf_op jit(solution)/shard_map/ppermute | solution.py:123
  506.7 140.8 %collective-permute-start.78 = (f32[192,1024]{1,0:T(8,128)}, f32[192,1024]{1,0:T(8,128)}, u32[]{:S(2)}, u32[]{:S(2)}) collective-permute-start(f32[192,1024]{1,0:T(8,128)} %get-tuple-element.56), channel_id=1, source_target_pairs={{24,16},{28,20},{25,17},{29,21},{26,18},{30,22},{27,19},{31,23}} | collective-permute-start | bytes 2359304 | tf_op jit(solution)/shard_map/ppermute | solution.py:123
  561.9 79.0 %collective-permute-start.62 = (f32[192,1024]{1,0:T(8,128)}, f32[192,1024]{1,0:T(8,128)}, u32[]{:S(2)}, u32[]{:S(2)}) collective-permute-start(f32[192,1024]{1,0:T(8,128)} %bitcast_add_fusion.12), channel_id=1, source_target_pairs={{0,8},{4,12},{8,16},{12,20},{1,9},{5,13},{9,17},{13,21},{2,10},{6,... | collective-permute-start | bytes 2359304 | tf_op jit(solution)/shard_map/ppermute | solution.py:120
  591.2 53.7 %collective-permute-start.69 = (f32[192,1024]{1,0:T(8,128)}, f32[192,1024]{1,0:T(8,128)}, u32[]{:S(2)}, u32[]{:S(2)}) collective-permute-start(f32[192,1024]{1,0:T(8,128)} %bitcast_add_fusion.7), channel_id=1, source_target_pairs={{0,8},{4,12},{8,16},{12,20},{1,9},{5,13},{9,17},{13,21},{2,10},{6,... | collective-permute-start | bytes 2359304 | tf_op jit(solution)/shard_map/ppermute | solution.py:120
  641.0 128.8 %collective-permute-start.15 = (f32[256,1536]{1,0:T(8,128)S(1)}, f32[256,1536]{1,0:T(8,128)S(1)}, u32[]{:S(2)}, u32[]{:S(2)}) collective-permute-start(f32[256,1536]{1,0:T(8,128)S(1)} %copy-done.113), channel_id=1, source_target_pairs={{0,1},{1,0},{2,3},{3,2},{4,5},{5,4},{6,7},{7,6},{8,9},{9,8},{10,11... | collective-permute-start | bytes 4718600 | tf_op jit(solution)/shard_map/ppermute | solution.py:79
  660.8 62.0 %collective-permute-start.46 = (f32[768,384]{1,0:T(8,128)S(1)}, f32[768,384]{1,0:T(8,128)S(1)}, u32[]{:S(2)}, u32[]{:S(2)}) collective-permute-start(f32[768,384]{1,0:T(8,128)S(1)} %fusion.184), channel_id=1, source_target_pairs={{0,4},{4,0},{8,12},{12,8},{16,20},{20,16},{24,28},{28,24},{1,5},{5... | collective-permute-start | bytes 3538952 | tf_op jit(solution)/shard_map/ppermute | solution.py:79
  662.2 115.4 %collective-permute-start.21 = (f32[256,1536]{1,0:T(8,128)S(1)}, f32[256,1536]{1,0:T(8,128)S(1)}, u32[]{:S(2)}, u32[]{:S(2)}) collective-permute-start(f32[256,1536]{1,0:T(8,128)S(1)} %copy-done.112), channel_id=1, source_target_pairs={{0,1},{1,0},{2,3},{3,2},{4,5},{5,4},{6,7},{7,6},{8,9},{9,8},{10,11... | collective-permute-start | bytes 4718600 | tf_op jit(solution)/shard_map/ppermute | solution.py:79
  672.2 74.8 %collective-permute-start.53 = (f32[768,384]{1,0:T(8,128)S(1)}, f32[768,384]{1,0:T(8,128)S(1)}, u32[]{:S(2)}, u32[]{:S(2)}) collective-permute-start(f32[768,384]{1,0:T(8,128)S(1)} %fusion.183), channel_id=1, source_target_pairs={{0,4},{4,0},{8,12},{12,8},{16,20},{20,16},{24,28},{28,24},{1,5},{5... | collective-permute-start | bytes 3538952 | tf_op jit(solution)/shard_map/ppermute | solution.py:79
  697.5 74.4 %collective-permute-start.63 = (f32[192,1024]{1,0:T(8,128)S(1)}, f32[192,1024]{1,0:T(8,128)S(1)}, u32[]{:S(2)}, u32[]{:S(2)}) collective-permute-start(f32[192,1024]{1,0:T(8,128)S(1)} %get-tuple-element.63), channel_id=1, source_target_pairs={{0,8},{4,12},{8,16},{12,20},{16,24},{20,28},{1,9},{5,13},{9,17},{1... | collective-permute-start | bytes 2359304 | tf_op jit(solution)/shard_map/ppermute | solution.py:120
  834.0 62.7 %collective-permute-start.22 = (f32[256,1536]{1,0:T(8,128)S(1)}, f32[256,1536]{1,0:T(8,128)S(1)}, u32[]{:S(2)}, u32[]{:S(2)}) collective-permute-start(f32[256,1536]{1,0:T(8,128)S(1)} %fusion.42), channel_id=1, source_target_pairs={{0,2},{1,3},{2,0},{3,1},{4,6},{5,7},{6,4},{7,5},{8,10},{9,11},{10,... | collective-permute-start | bytes 4718600 | tf_op jit(solution)/shard_map/ppermute | solution.py:79
  874.9 58.3 %collective-permute-start.56 = (f32[192,384]{1,0:T(8,128)}, f32[192,384]{1,0:T(8,128)}, u32[]{:S(2)}, u32[]{:S(2)}) collective-permute-start(f32[192,384]{1,0:T(8,128)} %get-tuple-element.101), channel_id=1, source_target_pairs={{0,8},{4,12},{8,16},{12,20},{16,24},{20,28},{1,9},{5,13},{9,17},{1... | collective-permute-start | bytes 884744 | tf_op jit(solution)/shard_map/ppermute | solution.py:120
  (262 other events, 4016.4 us)

commit v2 on v1

--- a/solution.py
+++ b/solution.py
@@ -1,14 +1,21 @@
+import functools
 import math
 
 import jax
 import jax.numpy as jnp
 from jax import lax
+from jax.experimental import pallas as pl
+from jax.experimental.pallas import tpu as pltpu
 from jax.sharding import PartitionSpec as P
 
 norm_epsilon = 1e-05
 lambda_base = 0.8 - 0.6 * math.exp(-0.3 * 11.0)
 rotary_base = 10000.0
 floor_score = -60.0
+chunk_columns = 256
+send_slots = 3
+held_slots = 4
+MESH = pl.DeviceIdType.MESH
 
 
 def doc_tables(lengths, row_count):
@@ -132,23 +139,198 @@
     return lax.dynamic_index_in_dim(own, place, 0, keepdims=False) + up_in + down_in
 
 
-def pair_columns(values, dp_count):
-    rows, width = values.shape
+def scatter_kernel(plan, line, left_count, right_count, *refs):
+    lefts, refs = refs[:left_count], refs[left_count:]
+    rights, refs = refs[:right_count], refs[right_count:]
+    outs, scratch = refs[:right_count], refs[right_count:]
+    send, held, total, landed, pair_out, pair_in, line_out, line_in, credit, out_sem = scratch
+    me = lax.axis_index("dp")
+    place, side = me // 2, me % 2
+    other = me + 1 - 2 * side
+    steps = line - 1
+    count = len(plan)
+    ring = total.shape[0]
+
+    barrier = pltpu.get_barrier_semaphore()
+    pl.semaphore_signal(barrier, inc=1, device_id={"dp": other}, device_id_type=MESH)
+
+    @pl.when(place > 0)
+    def _():
+        pl.semaphore_signal(barrier, inc=1, device_id={"dp": me - 2}, device_id_type=MESH)
+
+    @pl.when(place < line - 1)
+    def _():
+        pl.semaphore_signal(barrier, inc=1, device_id={"dp": me + 2}, device_id_type=MESH)
+
+    has_below = jnp.where(place > 0, 1, 0)
+    has_above = jnp.where(place < line - 1, 1, 0)
+    pl.semaphore_wait(barrier, 1 + has_below + has_above)
+
+    def compute(c):
+        left, right, first, width = plan[c]
+
+        def block(at, carry):
+            columns = rights[right][:, first : first + width]
+            send[c % send_slots, at, :, :width] = f32_dot(lefts[left][at, 1 - side], columns)
+            total[c % ring, at, :, :width] = f32_dot(lefts[left][at, side], columns)
+            return carry
+
+        lax.fori_loop(0, line, block, 0)
+
+    def pair_copy(c):
+        width = plan[c][3]
+        return pltpu.make_async_remote_copy(
+            src_ref=send.at[c % send_slots, :, :, :width],
+            dst_ref=held.at[c % held_slots, :, :, :width],
+            send_sem=pair_out.at[c % send_slots],
+            recv_sem=pair_in.at[c % held_slots],
+            device_id={"dp": other},
+            device_id_type=MESH,
+        )
+
+    def pair_finish(c):
+        width = plan[c][3]
+        pair_copy(c).wait_recv()
+
+        def block(at, carry):
+            total[c % ring, at, :, :width] += held[c % held_slots, at, :, :width]
+            return carry
+
+        lax.fori_loop(0, line, block, 0)
+        pair_copy(c).wait_send()
+
+    def line_copy(c, step, way):
+        width = plan[c][3]
+        block = line - 1 - step + place if way == 0 else place + step - line + 1
+        return pltpu.make_async_remote_copy(
+            src_ref=total.at[c % ring, block, :, :width],
+            dst_ref=landed.at[way, step, c % 2, :, :width],
+            send_sem=line_out.at[way, step, c % 2],
+            recv_sem=line_in.at[way, step, c % 2],
+            device_id={"dp": me + 2 - 4 * way},
+            device_id_type=MESH,
+        )
+
+    def line_sends(step, way):
+        if way == 0:
+            return (place <= step) & (place < line - 1)
+        return (place >= line - 1 - step) & (place > 0)
+
+    def line_start(c, step):
+        for way in range(2):
+
+            @pl.when(line_sends(step, way))
+            def _():
+                if c >= 2:
+                    pl.semaphore_wait(credit.at[way, step], 1)
+                line_copy(c, step, way).start()
+
+    def line_finish(c, step):
+        width = plan[c][3]
+        for way in range(2):
+            if way == 0:
+                gets = (place > 0) & (place - 1 <= step)
+                block = line - 2 - step + place
+            else:
+                gets = (place < line - 1) & (place + 1 >= line - 1 - step)
+                block = place + step - line + 2
+
+            @pl.when(gets)
+            def _():
+                pltpu.make_async_remote_copy(
+                    src_ref=total.at[c % ring, block, :, :width],
+                    dst_ref=landed.at[way, step, c % 2, :, :width],
+                    send_sem=line_out.at[way, step, c % 2],
+                    recv_sem=line_in.at[way, step, c % 2],
+                    device_id={"dp": me - 2 + 4 * way},
+                    device_id_type=MESH,
+                ).wait_recv()
+                total[c % ring, block, :, :width] += landed[way, step, c % 2, :, :width]
+                if c + 2 < count:
+                    pl.semaphore_signal(
+                        credit.at[way, step],
+                        inc=1,
+                        device_id={"dp": me - 2 + 4 * way},
+                        device_id_type=MESH,
+                    )
+
+            @pl.when(line_sends(step, way))
+            def _():
+                line_copy(c, step, way).wait_send()
+
+    def out_copy(c):
+        left, right, first, width = plan[c]
+        return pltpu.make_async_copy(
+            total.at[c % ring, place, :, :width],
+            outs[right].at[:, first : first + width],
+            out_sem.at[c % ring],
+        )
+
+    compute(0)
+    pair_copy(0).start()
+    if count > 1:
+        compute(1)
+    for slot in range(count + steps + 1):
+        for step in range(steps):
+            c = slot - 2 - step
+            if 0 <= c < count:
+                line_finish(c, step)
+        if 0 <= slot - 1 < count:
+            pair_finish(slot - 1)
+        for step in range(steps):
+            c = slot - 1 - step
+            if 0 <= c < count:
+                line_start(c, step)
+        if slot + 1 < count:
+            pair_copy(slot + 1).start()
+        done = slot - 1 - steps
+        if 0 <= done < count:
+            out_copy(done).start()
+        if slot + 2 < count:
+            if slot + 2 >= ring:
+                out_copy(slot + 2 - ring).wait()
+            compute(slot + 2)
+    for c in range(max(0, count - ring), count):
+        out_copy(c).wait()
+
+
+def weight_scatter(lefts, rights, pairs, dp_count, collective_id):
     line = dp_count // 2
-    side = lax.axis_index("dp") % 2
-    cut = values.reshape(rows, line, 2, width // dp_count)
-    pick = lambda which: lax.dynamic_index_in_dim(cut, which, 2, keepdims=False).reshape(
-        rows, width // 2
-    )
-    return pick(1 - side), pick(side)
-
-
-def weight_scatter(pair, right, dp_count):
-    send_left, keep_left = pair
-    received = flip(dot_rows(send_left, right), "dp", 1)
-    summed = dot_rows(keep_left, right) + received
-    line = dp_count // 2
-    return line_scatter(summed.reshape(line, -1, summed.shape[-1]), dp_count)
+    tokens, depth = lefts[0].shape
+    rows = depth // dp_count
+    lefts = [left.T.reshape(line, 2, rows, tokens) for left in lefts]
+    plan = []
+    for left, right in pairs:
+        width = rights[right].shape[1]
+        for first in range(0, width, chunk_columns):
+            plan.append((left, right, first, min(chunk_columns, width - first)))
+    ring = line + 4
+    wide = (line, rows, chunk_columns)
+    flops = 2 * tokens * depth * sum(item[3] for item in plan)
+    return pl.pallas_call(
+        functools.partial(scatter_kernel, tuple(plan), line, len(lefts), len(rights)),
+        out_shape=[
+            jax.ShapeDtypeStruct((rows, right.shape[1]), jnp.float32) for right in rights
+        ],
+        in_specs=[pl.BlockSpec(memory_space=pltpu.VMEM)] * (len(lefts) + len(rights)),
+        out_specs=[pl.BlockSpec(memory_space=pl.ANY)] * len(rights),
+        scratch_shapes=[
+            pltpu.VMEM((send_slots,) + wide, jnp.float32),
+            pltpu.VMEM((held_slots,) + wide, jnp.float32),
+            pltpu.VMEM((ring,) + wide, jnp.float32),
+            pltpu.VMEM((2, line - 1, 2, rows, chunk_columns), jnp.float32),
+            pltpu.SemaphoreType.DMA((send_slots,)),
+            pltpu.SemaphoreType.DMA((held_slots,)),
+            pltpu.SemaphoreType.DMA((2, line - 1, 2)),
+            pltpu.SemaphoreType.DMA((2, line - 1, 2)),
+            pltpu.SemaphoreType.REGULAR((2, line - 1)),
+            pltpu.SemaphoreType.DMA((ring,)),
+        ],
+        compiler_params=pltpu.CompilerParams(
+            collective_id=collective_id, has_side_effects=True, vmem_limit_bytes=48 * 1024 * 1024
+        ),
+        cost_estimate=pl.CostEstimate(flops=flops, bytes_accessed=flops // 16, transcendentals=0),
+    )(*lefts, *rights)
 
 
 def rms_back(incoming, values, inverse_root):
@@ -343,7 +525,6 @@
         norm1_gain, query_weight, key_weight, value_weight, lambda_param, sub_gain, out_weight,
     )
     cots = [mine_first(out_cotangent[m], core) for m in range(2)]
-    cot_pair = pair_columns(jnp.concatenate(cots, 0), dp_count)
     half = cots[0].shape[0] // 2
     rows_in = [mine_first(layer_in[m], core).astype(jnp.float32) for m in range(2)]
     inputs = [rows_in[m][:half] for m in range(2)]
@@ -357,10 +538,13 @@
         normed_two.append((with_other(middle[m] * root_two[m]) * norm2_gain).astype(jnp.bfloat16))
         ffn.append(feed_forward(normed_two[m], cots[m], gate_weight, up_weight, down_weight))
     both = lambda index: jnp.concatenate([ffn[0][index], ffn[1][index]], 0)
-    normed_two_pair = pair_columns(jnp.concatenate(normed_two, 0), dp_count)
-    grad_down = weight_scatter(cot_pair, both(2), dp_count)
-    grad_gate = weight_scatter(normed_two_pair, both(3), dp_count)
-    grad_up = weight_scatter(normed_two_pair, both(4), dp_count)
+    grad_down, grad_gate, grad_up = weight_scatter(
+        [jnp.concatenate(cots, 0), jnp.concatenate(normed_two, 0)],
+        [both(2), both(3), both(4)],
+        [(0, 0), (1, 1), (1, 2)],
+        dp_count,
+        0,
+    )
     grad_norm2 = 0.0
     grad_norm1 = 0.0
     through_two, grad_attended, back = [], [], []
@@ -376,14 +560,17 @@
             )
         )
     heads_both = jnp.concatenate([kept[0][-1], kept[1][-1]], 0)
-    grad_out = weight_scatter(
-        pair_columns(jnp.concatenate(grad_attended, 0), dp_count), heads_both, dp_count
-    )
-    normed_one_pair = pair_columns(jnp.concatenate([kept[0][3], kept[1][3]], 0), dp_count)
-    grad_query, grad_key, grad_value = [
-        weight_scatter(normed_one_pair, jnp.concatenate([back[0][i], back[1][i]], 0), dp_count)
-        for i in (2, 3, 4)
-    ]
+    grad_rows = jnp.concatenate(
+        [jnp.concatenate([back[m][i] for i in (2, 3, 4)], 1) for m in range(2)], 0
+    )
+    grad_out, grad_qkv = weight_scatter(
+        [jnp.concatenate(grad_attended, 0), jnp.concatenate([kept[0][3], kept[1][3]], 0)],
+        [heads_both, grad_rows],
+        [(0, 0), (1, 1)],
+        dp_count,
+        1,
+    )
+    grad_query, grad_key, grad_value = jnp.split(grad_qkv, 3, axis=1)
     out_blocks, grad_blocks = [], []
     for m in range(2):
         fed = tensor_sum(*ffn[m][1])

time: 963 us -> 820 us (0.85)
  Pallas kernels: 0 us -> 379 us
  waiting for transfers between devices: 377 us -> 96.3 us
  starting transfers between devices: 149 us -> 27.7 us
  matrix products: 181 us -> 113 us
  local copies, waits for them, and re-layouts: 102 us -> 67.7 us
  other arithmetic: 144 us -> 127 us
    pallas_call x0 -> x2, Pallas kernels: none -> 379 us  [weight_scatter(): pl.pallas_call(functools.partial(scatter_kernel, tuple(plan), line, len(l...]
    ppermute x33 -> x26, waiting for transfers between devices: 293 us -> 91.9 us  [flip(): return lax.ppermute(values, axis_name, [(i, i ^ bit) for i in range(size)])]
    ppermute x24 -> x3, starting transfers between devices: 100 us -> 10.3 us  [line_scatter(): lax.ppermute(up_out, 'dp', [(2 * z + x, 2 * z + 2 + x) for z in range(ste...]
    ppermute x24 -> x3, waiting for transfers between devices: 47.9 us -> 0.62 us  [line_scatter(): lax.ppermute(up_out, 'dp', [(2 * z + x, 2 * z + 2 + x) for z in range(ste...]
    ppermute x24 -> x3, waiting for transfers between devices: 36 us -> 3.74 us  [line_scatter(): lax.ppermute(down_out, 'dp', [(2 * z + x, 2 * z - 2 + x) for z in range(l...]
    dot_general x14 -> x0, matrix products: 31.9 us -> none  [dot_rows(): lax.dot_general(left, right, (((0,), (0,)), ((), ())), preferred_element_...]
    ppermute x24 -> x3, starting transfers between devices: 25.4 us -> 2.62 us  [line_scatter(): lax.ppermute(down_out, 'dp', [(2 * z + x, 2 * z - 2 + x) for z in range(l...]
    transpose x0 -> x4, local copies, waits for them, and re-layouts: none -> 17.8 us  [weight_scatter(): lefts = [left.T.reshape(line, 2, rows, tokens) for left in lefts]]
  transfers between devices with their start and end apart: 81 -> 32, of which waited for: 26 -> 9; matrix products, arithmetic and copies ran while one was open for 35% -> 25% of each run, Pallas kernels for 0% -> 47%
where the time goes in v2:
time: 820 us; the launch traced here: 815 us
  Pallas kernels  379 us (46%)
  other arithmetic  127 us (15%)
  matrix products  113 us (14%)
  waiting for transfers between devices  96.3 us (12%)
  local copies, waits for them, and re-layouts  67.7 us (8%)
  starting transfers between devices  27.7 us (3%)
    pallas_call x2, Pallas kernels, weight_scatter(): pl.pallas_call(functools.partial(scatter_kernel, tuple(plan), line, len(l...  379 us
    ppermute x26, waiting for transfers between devices, flip(): return lax.ppermute(values, axis_name, [(i, i ^ bit) for i in range(size)])  91.9 us
    dot_general x18, matrix products, f32_dot(): return jnp.dot(left, right, preferred_element_type=jnp.float32)  40.7 us
    unnamed x362, local copies, waits for them, and re-layouts  27.7 us
    dot_general x24, matrix products, dot_t(): lax.dot_general(left, right, (((1,), (1,)), ((), ())), preferred_element_...  27.1 us
    transpose x4, local copies, waits for them, and re-layouts, weight_scatter(): lefts = [left.T.reshape(line, 2, rows, tokens) for left in lefts]  17.8 us
  transfers between devices with their start and end apart: 32, of which 9 were waited for; matrix products, arithmetic and copies ran while one was open for 25% of the time, Pallas kernels for 47%

profile of v2, /device:TPU:0, one launch (start us, length us, event | category | flops | bytes accessed | tf_op | source)
XLA Modules:
  0.0 814.9 jit_solution(6385998159360591294)
XLA Ops:
  5.8 4.5 fusion.14
  30.6 3.9 fusion.4
  41.4 4.4 multiply_reduce_fusion.23
  51.1 4.3 exponential_select_fusion
  94.9 4.7 copy.170
  99.5 5.0 copy.179
  106.4 10.6 %collective-permute-done.1 = f32[256,1536]{1,0:T(8,128)} collective-permute-done((f32[256,1536]{1,0:T(8,128)}, f32[256,1536]{1,0:T(8,128)}, u32[]{:S(2)}, u32[]{:S(2)}) %collective-permute-start.1) | collective-permute-done | bytes 1572896 | tf_op jit(solution)/shard_map/ppermute | solution.py:86
  121.7 28.5 %collective-permute-done.7 = f32[256,1536]{1,0:T(8,128)} collective-permute-done((f32[256,1536]{1,0:T(8,128)}, f32[256,1536]{1,0:T(8,128)}, u32[]{:S(2)}, u32[]{:S(2)}) %collective-permute-start.7) | collective-permute-done | bytes 1572896 | tf_op jit(solution)/shard_map/ppermute | solution.py:86
  210.6 15.5 %collective-permute-done.13 = f32[256,1536]{1,0:T(8,128)} collective-permute-done((f32[256,1536]{1,0:T(8,128)}, f32[256,1536]{1,0:T(8,128)}, u32[]{:S(2)}, u32[]{:S(2)}) %collective-permute-start.13) | collective-permute-done | bytes 1572896 | tf_op jit(solution)/shard_map/ppermute | solution.py:86
  226.1 33.7 %collective-permute-done.19 = f32[256,1536]{1,0:T(8,128)} collective-permute-done((f32[256,1536]{1,0:T(8,128)}, f32[256,1536]{1,0:T(8,128)}, u32[]{:S(2)}, u32[]{:S(2)}) %collective-permute-start.19) | collective-permute-done | bytes 1572896 | tf_op jit(solution)/shard_map/ppermute | solution.py:86
  259.8 3.9 multiply_reduce_fusion.7
  267.4 241.5 %shard_map.247 = (f32[192,1024]{1,0:T(8,128)S(1)}, f32[192,1024]{1,0:T(8,128)S(1)}, f32[192,1024]{1,0:T(8,128)S(1)}) custom-call(bf16[4,2,192,1024]{3,2,1,0:T(8,128)(2,1)} %bitcast.420, bf16[4,2,192,1024]{3,2,1,0:T(8,128)(2,1)} %bitcast.421, bf16[1024,1024]{1,0:T(8,128)(2,1)S(1)} %pad_maximum_fusion.4.refs_2_, bf16[1024,1024]{1,0:T(8,128)(2,1)} %pad_maximum_fusion.5.refs_3_, ...), custom_call_target="tpu_custom_call" | custom-call | flops 9663676416 | bytes 603979776 | tf_op jit(solution)/shard_map/pallas_call | solution.py:310
  524.2 4.5 fusion.3
  528.7 5.4 fusion.78
  534.0 5.3 multiply_reduce_fusion.1
  544.4 5.5 fusion.81
  549.9 4.5 fusion.1
  554.4 5.0 multiply_reduce_fusion
  598.4 5.0 copy.169
  603.6 4.2 fusion.30
  607.8 11.9 %maximum_maximum_fusion.refs_3_ = bf16[1024,1152]{1,0:T(8,128)(2,1)S(1)} fusion(bf16[512,384]{1,0:T(8,128)(2,1)S(1)} %copy-done.97, bf16[512,384]{1,0:T(8,128)(2,1)S(1)} %copy-done.98, bf16[512,384]{1,0:T(8,128)(2,1)S(1)} %copy-done.99, bf16[512,384]{1,0:T(8,128)(2,1)S(1)} %copy-done.100, bf16[512,384]{1,0:T(8,128)(2,1)S(1)} %copy.174, ...), kind=kLoop, calls=%fused_computation.127 | loop fusion | flops 14155776 | bytes 4718592 | tf_op jit(solution)/shard_map/concatenate | solution.py:563
  619.8 137.6 %shard_map.246 = (f32[192,384]{1,0:T(8,128)S(1)}, f32[192,1152]{1,0:T(8,128)S(1)}) custom-call(bf16[4,2,192,1024]{3,2,1,0:T(8,128)(2,1)} %bitcast.422, bf16[4,2,192,1024]{3,2,1,0:T(8,128)(2,1)} %bitcast.419, bf16[1024,384]{1,0:T(8,128)(2,1)S(1)} %copy-done.8, bf16[1024,1152]{1,0:T(8,128)(2,1)S(1)} %maximum_maximum_fusion.refs_3_), custom_call_target="tpu_custom_call" | custom-call | flops 4831838208 | bytes 301989888 | tf_op jit(solution)/shard_map/pallas_call | solution.py:310
  771.4 4.4 collective-permute-start.27
  775.9 7.4 subtract_add_fusion.1
  (604 shorter events, 250.5 us)
Async XLA Ops:
  61.1 26.7 %collective-permute-start.6 = (f32[256,1536]{1,0:T(8,128)}, f32[256,1536]{1,0:T(8,128)}, u32[]{:S(2)}, u32[]{:S(2)}) collective-permute-start(f32[256,1536]{1,0:T(8,128)} %fusion.173), channel_id=1, source_target_pairs={{0,1},{1,0},{2,3},{3,2},{4,5},{5,4},{6,7},{7,6},{8,9},{9,8},{10,11... | collective-permute-start | bytes 4718600 | tf_op jit(solution)/shard_map/ppermute | solution.py:86
  63.3 11.7 %collective-permute-start = (f32[256,1536]{1,0:T(8,128)}, f32[256,1536]{1,0:T(8,128)}, u32[]{:S(2)}, u32[]{:S(2)}) collective-permute-start(f32[256,1536]{1,0:T(8,128)} %fusion.176), channel_id=1, source_target_pairs={{0,1},{1,0},{2,3},{3,2},{4,5},{5,4},{6,7},{7,6},{8,9},{9,8},{10,11... | collective-permute-start | bytes 4718600 | tf_op jit(solution)/shard_map/ppermute | solution.py:86
  78.6 38.5 %collective-permute-start.1 = (f32[256,1536]{1,0:T(8,128)}, f32[256,1536]{1,0:T(8,128)}, u32[]{:S(2)}, u32[]{:S(2)}) collective-permute-start(f32[256,1536]{1,0:T(8,128)} %convolution_add_fusion.15), channel_id=1, source_target_pairs={{0,2},{1,3},{2,0},{3,1},{4,6},{5,7},{6,4},{7,5},{8,10},{9,11},{10,... | collective-permute-start | bytes 4718600 | tf_op jit(solution)/shard_map/ppermute | solution.py:86
  91.0 59.2 %collective-permute-start.7 = (f32[256,1536]{1,0:T(8,128)}, f32[256,1536]{1,0:T(8,128)}, u32[]{:S(2)}, u32[]{:S(2)}) collective-permute-start(f32[256,1536]{1,0:T(8,128)} %convolution_add_fusion.14), channel_id=1, source_target_pairs={{0,2},{1,3},{2,0},{3,1},{4,6},{5,7},{6,4},{7,5},{8,10},{9,11},{10,... | collective-permute-start | bytes 4718600 | tf_op jit(solution)/shard_map/ppermute | solution.py:86
  121.7 41.0 %collective-permute-start.2 = (f32[256,1536]{1,0:T(8,128)S(1)}, f32[256,1536]{1,0:T(8,128)S(1)}, u32[]{:S(2)}, u32[]{:S(2)}) collective-permute-start(f32[256,1536]{1,0:T(8,128)S(1)} %broadcast_multiply_fusion.2), channel_id=1, source_target_pairs={{0,1},{1,0},{2,3},{3,2},{4,5},{5,4},{6,7},{7,6},{8,9},{9,8},{10,11... | collective-permute-start | bytes 4718600 | tf_op jit(solution)/shard_map/ppermute | solution.py:86
  173.1 13.2 %collective-permute-start.12 = (f32[256,1536]{1,0:T(8,128)S(1)}, f32[256,1536]{1,0:T(8,128)S(1)}, u32[]{:S(2)}, u32[]{:S(2)}) collective-permute-start(f32[256,1536]{1,0:T(8,128)S(1)} %convolution_add_fusion.2), channel_id=1, source_target_pairs={{0,1},{1,0},{2,3},{3,2},{4,5},{5,4},{6,7},{7,6},{8,9},{9,8},{10,11... | collective-permute-start | bytes 4718600 | tf_op jit(solution)/shard_map/ppermute | solution.py:86
  178.8 11.5 %collective-permute-start.18 = (f32[256,1536]{1,0:T(8,128)S(1)}, f32[256,1536]{1,0:T(8,128)S(1)}, u32[]{:S(2)}, u32[]{:S(2)}) collective-permute-start(f32[256,1536]{1,0:T(8,128)S(1)} %convolution_add_fusion), channel_id=1, source_target_pairs={{0,1},{1,0},{2,3},{3,2},{4,5},{5,4},{6,7},{7,6},{8,9},{9,8},{10,11... | collective-permute-start | bytes 4718600 | tf_op jit(solution)/shard_map/ppermute | solution.py:86
  181.5 20.5 %collective-permute-start.9 = (f32[256,1536]{1,0:T(8,128)}, f32[256,1536]{1,0:T(8,128)}, u32[]{:S(2)}, u32[]{:S(2)}) collective-permute-start(f32[256,1536]{1,0:T(8,128)} %fusion.146), channel_id=1, source_target_pairs={{0,1},{1,0},{2,3},{3,2},{4,5},{5,4},{6,7},{7,6},{8,9},{9,8},{10,11... | collective-permute-start | bytes 4718600 | tf_op jit(solution)/shard_map/ppermute | solution.py:86
  183.7 24.0 %collective-permute-start.3 = (f32[256,1536]{1,0:T(8,128)}, f32[256,1536]{1,0:T(8,128)}, u32[]{:S(2)}, u32[]{:S(2)}) collective-permute-start(f32[256,1536]{1,0:T(8,128)} %fusion.149), channel_id=1, source_target_pairs={{0,1},{1,0},{2,3},{3,2},{4,5},{5,4},{6,7},{7,6},{8,9},{9,8},{10,11... | collective-permute-start | bytes 4718600 | tf_op jit(solution)/shard_map/ppermute | solution.py:86
  188.5 37.6 %collective-permute-start.13 = (f32[256,1536]{1,0:T(8,128)}, f32[256,1536]{1,0:T(8,128)}, u32[]{:S(2)}, u32[]{:S(2)}) collective-permute-start(f32[256,1536]{1,0:T(8,128)} %fusion.60), channel_id=1, source_target_pairs={{0,2},{1,3},{2,0},{3,1},{4,6},{5,7},{6,4},{7,5},{8,10},{9,11},{10,... | collective-permute-start | bytes 4718600 | tf_op jit(solution)/shard_map/ppermute | solution.py:86
  192.5 67.4 %collective-permute-start.19 = (f32[256,1536]{1,0:T(8,128)}, f32[256,1536]{1,0:T(8,128)}, u32[]{:S(2)}, u32[]{:S(2)}) collective-permute-start(f32[256,1536]{1,0:T(8,128)} %fusion.61), channel_id=1, source_target_pairs={{0,2},{1,3},{2,0},{3,1},{4,6},{5,7},{6,4},{7,5},{8,10},{9,11},{10,... | collective-permute-start | bytes 4718600 | tf_op jit(solution)/shard_map/ppermute | solution.py:86
  205.9 303.1 %collective-permute-start.10 = (f32[256,1536]{1,0:T(8,128)S(1)}, f32[256,1536]{1,0:T(8,128)S(1)}, u32[]{:S(2)}, u32[]{:S(2)}) collective-permute-start(f32[256,1536]{1,0:T(8,128)S(1)} %convolution_add_fusion.4), channel_id=1, source_target_pairs={{0,2},{1,3},{2,0},{3,1},{4,6},{5,7},{6,4},{7,5},{8,10},{9,11},{10,... | collective-permute-start | bytes 4718600 | tf_op jit(solution)/shard_map/ppermute | solution.py:86
  210.1 300.8 %collective-permute-start.4 = (f32[256,1536]{1,0:T(8,128)S(1)}, f32[256,1536]{1,0:T(8,128)S(1)}, u32[]{:S(2)}, u32[]{:S(2)}) collective-permute-start(f32[256,1536]{1,0:T(8,128)S(1)} %convolution_add_fusion.5), channel_id=1, source_target_pairs={{0,2},{1,3},{2,0},{3,1},{4,6},{5,7},{6,4},{7,5},{8,10},{9,11},{10,... | collective-permute-start | bytes 4718600 | tf_op jit(solution)/shard_map/ppermute | solution.py:86
  267.3 246.4 %collective-permute-start.14 = (f32[256,1536]{1,0:T(8,128)S(1)}, f32[256,1536]{1,0:T(8,128)}, u32[]{:S(2)}, u32[]{:S(2)}) collective-permute-start(f32[256,1536]{1,0:T(8,128)S(1)} %get-tuple-element.128), channel_id=1, source_target_pairs={{0,1},{1,0},{2,3},{3,2},{4,5},{5,4},{6,7},{7,6},{8,9},{9,8},{10,11... | collective-permute-start | bytes 4718600 | tf_op jit(solution)/shard_map/ppermute | solution.py:86
  510.9 60.4 %collective-permute-start.11 = (f32[256,1536]{1,0:T(8,128)}, f32[256,1536]{1,0:T(8,128)}, u32[]{:S(2)}, u32[]{:S(2)}) collective-permute-start(f32[256,1536]{1,0:T(8,128)} %add_add_fusion), channel_id=1, source_target_pairs={{0,1},{1,0},{2,3},{3,2},{4,5},{5,4},{6,7},{7,6},{8,9},{9,8},{10,11... | collective-permute-start | bytes 4718600 | tf_op jit(solution)/shard_map/ppermute | solution.py:86
  513.2 67.4 %collective-permute-start.5 = (f32[256,1536]{1,0:T(8,128)}, f32[256,1536]{1,0:T(8,128)}, u32[]{:S(2)}, u32[]{:S(2)}) collective-permute-start(f32[256,1536]{1,0:T(8,128)} %add_add_fusion.1), channel_id=1, source_target_pairs={{0,1},{1,0},{2,3},{3,2},{4,5},{5,4},{6,7},{7,6},{8,9},{9,8},{10,11... | collective-permute-start | bytes 4718600 | tf_op jit(solution)/shard_map/ppermute | solution.py:86
  567.0 19.1 %collective-permute-start.15 = (f32[256,1536]{1,0:T(8,128)S(1)}, f32[256,1536]{1,0:T(8,128)S(1)}, u32[]{:S(2)}, u32[]{:S(2)}) collective-permute-start(f32[256,1536]{1,0:T(8,128)S(1)} %convolution_add_fusion.10), channel_id=1, source_target_pairs={{0,1},{1,0},{2,3},{3,2},{4,5},{5,4},{6,7},{7,6},{8,9},{9,8},{10,11... | collective-permute-start | bytes 4718600 | tf_op jit(solution)/shard_map/ppermute | solution.py:86
  570.4 19.1 %collective-permute-start.21 = (f32[256,1536]{1,0:T(8,128)S(1)}, f32[256,1536]{1,0:T(8,128)S(1)}, u32[]{:S(2)}, u32[]{:S(2)}) collective-permute-start(f32[256,1536]{1,0:T(8,128)S(1)} %convolution_add_fusion.6), channel_id=1, source_target_pairs={{0,1},{1,0},{2,3},{3,2},{4,5},{5,4},{6,7},{7,6},{8,9},{9,8},{10,11... | collective-permute-start | bytes 4718600 | tf_op jit(solution)/shard_map/ppermute | solution.py:86
  587.9 169.5 %collective-permute-start.16 = (f32[256,1536]{1,0:T(8,128)}, f32[256,1536]{1,0:T(8,128)}, u32[]{:S(2)}, u32[]{:S(2)}) collective-permute-start(f32[256,1536]{1,0:T(8,128)} %fusion.45), channel_id=1, source_target_pairs={{0,2},{1,3},{2,0},{3,1},{4,6},{5,7},{6,4},{7,5},{8,10},{9,11},{10,... | collective-permute-start | bytes 4718600 | tf_op jit(solution)/shard_map/ppermute | solution.py:86
  591.3 166.1 %collective-permute-start.22 = (f32[256,1536]{1,0:T(8,128)}, f32[256,1536]{1,0:T(8,128)}, u32[]{:S(2)}, u32[]{:S(2)}) collective-permute-start(f32[256,1536]{1,0:T(8,128)} %fusion.44), channel_id=1, source_target_pairs={{0,2},{1,3},{2,0},{3,1},{4,6},{5,7},{6,4},{7,5},{8,10},{9,11},{10,... | collective-permute-start | bytes 4718600 | tf_op jit(solution)/shard_map/ppermute | solution.py:86
  770.1 13.2 %collective-permute-start.29 = (f32[1,528]{1,0:T(1,128)S(1)}, f32[1,528]{1,0:T(1,128)S(1)}, u32[]{:S(2)}, u32[]{:S(2)}) collective-permute-start(f32[1,528]{1,0:T(1,128)S(1)} %get-tuple-element.121), channel_id=1, source_target_pairs={{24,16},{28,20},{25,17},{29,21},{26,18},{30,22},{27,19},{31,23}} | collective-permute-start | bytes 6344 | tf_op jit(solution)/shard_map/ppermute | solution.py:130
  771.4 11.9 %collective-permute-start.27 = (f32[1,528]{1,0:T(1,128)S(1)}, f32[1,528]{1,0:T(1,128)S(1)}, u32[]{:S(2)}, u32[]{:S(2)}) collective-permute-start(f32[1,528]{1,0:T(1,128)S(1)} %fusion.201), channel_id=1, source_target_pairs={{0,8},{4,12},{8,16},{12,20},{1,9},{5,13},{9,17},{13,21},{2,10},{6,... | collective-permute-start | bytes 6344 | tf_op jit(solution)/shard_map/ppermute | solution.py:127
  783.3 13.8 %collective-permute-start.23 = (f32[256,1536]{1,0:T(8,128)}, f32[256,1536]{1,0:T(8,128)}, u32[]{:S(2)}, u32[]{:S(2)}) collective-permute-start(f32[256,1536]{1,0:T(8,128)} %get-tuple-element.123), channel_id=1, source_target_pairs={{0,1},{1,0},{2,3},{3,2},{4,5},{5,4},{6,7},{7,6},{8,9},{9,8},{10,11... | collective-permute-start | bytes 4718600 | tf_op jit(solution)/shard_map/ppermute | solution.py:86
  786.0 13.8 %collective-permute-start.17 = (f32[256,1536]{1,0:T(8,128)}, f32[256,1536]{1,0:T(8,128)}, u32[]{:S(2)}, u32[]{:S(2)}) collective-permute-start(f32[256,1536]{1,0:T(8,128)} %get-tuple-element.122), channel_id=1, source_target_pairs={{0,1},{1,0},{2,3},{3,2},{4,5},{5,4},{6,7},{7,6},{8,9},{9,8},{10,11... | collective-permute-start | bytes 4718600 | tf_op jit(solution)/shard_map/ppermute | solution.py:86
  (186 other events, 2691.1 us)

commit v3 on v2

--- a/solution.py
+++ b/solution.py
@@ -11,7 +11,9 @@
 norm_epsilon = 1e-05
 lambda_base = 0.8 - 0.6 * math.exp(-0.3 * 11.0)
 rotary_base = 10000.0
-floor_score = -60.0
+closed_score = -1e30
+block_rows = 128
+longest_document = 256
 chunk_columns = 256
 send_slots = 3
 held_slots = 4
@@ -24,45 +26,56 @@
     passed = (places[:, None] >= doc_ends[None, :]).astype(jnp.int32)
     segment = jnp.sum(passed, axis=1, dtype=jnp.int32)
     starts = jnp.sum(passed * lengths[None, :], axis=1, dtype=jnp.int32)
-    allowed = (segment[:, None] == segment[None, :]) & (places[None, :] <= places[:, None])
-    return (places - starts, allowed)
+    return (places - starts, segment)
 
 
 def rotary_tables(position, map_width):
     half_width = map_width // 2
     frequency = rotary_base ** (-2.0 * jnp.arange(half_width, dtype=jnp.float32) / map_width)
     angles = position.astype(jnp.float32)[:, None] * frequency[None, :]
-    return (jnp.cos(angles), jnp.sin(angles))
-
-
-def rotate(values, cosine_table, sine_table):
-    half_width = values.shape[-1] // 2
-    first_half = values[..., :half_width]
-    second_half = values[..., half_width:]
-    cos_wide = cosine_table[:, None, None, :]
-    sin_wide = sine_table[:, None, None, :]
-    return jnp.concatenate(
-        [
-            first_half * cos_wide - second_half * sin_wide,
-            second_half * cos_wide + first_half * sin_wide,
-        ],
-        axis=-1,
-    )
-
-
-def rotate_back(values, cosine_table, sine_table):
-    half_width = values.shape[-1] // 2
-    first_half = values[..., :half_width]
-    second_half = values[..., half_width:]
-    cos_wide = cosine_table[:, None, None, :]
-    sin_wide = sine_table[:, None, None, :]
-    return jnp.concatenate(
-        [
-            first_half * cos_wide + second_half * sin_wide,
-            second_half * cos_wide - first_half * sin_wide,
-        ],
-        axis=-1,
-    )
+    cosine, sine = jnp.cos(angles), jnp.sin(angles)
+    return (
+        jnp.concatenate([cosine] * 4, axis=1),
+        jnp.concatenate([-sine, sine, -sine, sine], axis=1),
+    )
+
+
+def turn(values, cosine, sine):
+    width = values.shape[-1]
+    quarter = width // 4
+    lane = lax.broadcasted_iota(jnp.int32, values.shape, 1)
+    partner = jnp.where(
+        lane % (2 * quarter) < quarter,
+        pltpu.roll(values, width - quarter, 1),
+        pltpu.roll(values, quarter, 1),
+    )
+    return values * cosine + partner * sine
+
+
+def map_of(values, which):
+    lane = lax.broadcasted_iota(jnp.int32, values.shape, 1)
+    mine = (lane >= values.shape[-1] // 2) == (which == 1)
+    return jnp.where(mine, values, jnp.zeros_like(values))
+
+
+def key_range(block):
+    first = max(0, block * block_rows - longest_document + 1) // block_rows * block_rows
+    return first, (block + 1) * block_rows
+
+
+def open_pairs(block, segment_column, segment_row):
+    first, last = key_range(block)
+    rows = pl.ds(block * block_rows, block_rows)
+    shape = (block_rows, last - first)
+    row_at = lax.broadcasted_iota(jnp.int32, shape, 0) + block * block_rows
+    key_at = lax.broadcasted_iota(jnp.int32, shape, 1) + first
+    return (segment_column[rows, :] == segment_row[:, first:last]) & (key_at <= row_at)
+
+
+def softmax_map(query, key, opened, scale):
+    scores = jnp.where(opened, dot_t(query, key) * scale, closed_score)
+    expanded = jnp.exp(scores - jnp.max(scores, axis=-1, keepdims=True))
+    return expanded * (1.0 / jnp.sum(expanded, axis=-1, keepdims=True))
 
 
 def f32_dot(left, right):
@@ -343,138 +356,159 @@
     return lax.rsqrt(jnp.mean(values * values, axis=-1, keepdims=True) + norm_epsilon)
 
 
-def attention_forward(row_in, lengths, weight_set, core):
-    (norm1_gain, query_weight, key_weight, value_weight, lambda_param, sub_gain, out_weight) = (
-        weight_set
-    )
-    row_count = row_in.shape[0]
-    head_count = lambda_param.shape[0]
-    map_width = lambda_param.shape[1] // 4
-    value_width = sub_gain.shape[1]
-    score_scale = map_width ** (-0.5)
-    position, allowed = doc_tables(lengths, row_count)
-    cosine_table, sine_table = rotary_tables(position, map_width)
-    inputs = row_in.astype(jnp.float32)
-    normed_one = (inputs * root_of(inputs) * norm1_gain).astype(jnp.bfloat16)
-    query_raw = f32_dot(normed_one, query_weight).reshape(row_count, head_count, 2, map_width)
-    query_rows = rotate(query_raw, cosine_table, sine_table).astype(jnp.bfloat16)
-    key_raw = f32_dot(normed_one, key_weight).reshape(row_count, head_count, 2, map_width)
-    key_rows = rotate(key_raw, cosine_table, sine_table).astype(jnp.bfloat16)
-    value_rows = (
-        f32_dot(normed_one, value_weight)
-        .astype(jnp.bfloat16)
-        .reshape(row_count, head_count, value_width)
-    )
-    lambda_parts = lambda_param.reshape(head_count, 4, map_width)
-    first_exp = jnp.exp(jnp.sum(lambda_parts[:, 0] * lambda_parts[:, 1], axis=-1))
-    second_exp = jnp.exp(jnp.sum(lambda_parts[:, 2] * lambda_parts[:, 3], axis=-1))
-    lambda_head = first_exp - second_exp + lambda_base
-    scores = (
-        jnp.einsum("thmd,shmd->hmts", query_rows, key_rows, preferred_element_type=jnp.float32)
-        * score_scale
-    )
-    row_max = jnp.max(jnp.where(allowed, scores, floor_score), axis=-1, keepdims=True)
-    expanded = jnp.where(allowed, jnp.exp(jnp.where(allowed, scores - row_max, 0.0)), 0.0)
-    row_total = jnp.sum(expanded, axis=-1, keepdims=True)
-    log_total = row_max + jnp.log(row_total)
-    softmax_maps = expanded / row_total
-    combined = (softmax_maps[:, 0] - lambda_head[:, None, None] * softmax_maps[:, 1]).astype(
-        jnp.bfloat16
-    )
-    mixed = jnp.einsum("hts,shd->thd", combined, value_rows, preferred_element_type=jnp.float32)
-    root_sub = root_of(mixed)
-    sub_scale = sub_gain * (1.0 - lambda_base)
-    heads_out = (
-        (mixed * root_sub * sub_scale)
-        .astype(jnp.bfloat16)
-        .reshape(row_count, head_count * value_width)
-    )
-    send = f32_dot(half_rows(heads_out, 1 - core), out_weight)
-    keep = f32_dot(half_rows(heads_out, core), out_weight)
-    kept = (
-        allowed, cosine_table, sine_table, normed_one, query_rows, key_rows, value_rows,
-        lambda_parts, first_exp, second_exp, lambda_head, log_total, mixed, root_sub, sub_scale,
-        heads_out,
-    )
-    return keep, send, kept
-
-
-def attention_backward(grad_attended, kept, weight_set, core):
-    (query_weight, key_weight, value_weight, out_weight) = weight_set
-    (
-        allowed, cosine_table, sine_table, normed_one, query_rows, key_rows, value_rows,
-        lambda_parts, first_exp, second_exp, lambda_head, log_total, mixed, root_sub, sub_scale,
-        heads_out,
-    ) = kept
-    row_count, head_count, value_width = value_rows.shape
-    map_width = query_rows.shape[-1]
-    score_scale = map_width ** (-0.5)
-    grad_heads = dot_t(grad_attended, out_weight).reshape(row_count, head_count, value_width)
-    grad_sub = jnp.sum(grad_heads * mixed * root_sub, axis=0) * (1.0 - lambda_base)
-    grad_mixed = rms_back(grad_heads * sub_scale, mixed, root_sub).astype(jnp.bfloat16)
-    scores = (
-        jnp.einsum("thmd,shmd->hmts", query_rows, key_rows, preferred_element_type=jnp.float32)
-        * score_scale
-    )
-    maps_again = jnp.where(allowed, jnp.exp(jnp.where(allowed, scores - log_total, 0.0)), 0.0)
-    first_map = maps_again[:, 0]
-    second_map = maps_again[:, 1]
-    combined_again = (first_map - lambda_head[:, None, None] * second_map).astype(jnp.bfloat16)
-    grad_combined = jnp.einsum(
-        "thd,shd->hts", grad_mixed, value_rows, preferred_element_type=jnp.float32
-    )
-    grad_value = (
-        jnp.einsum("hts,thd->shd", combined_again, grad_mixed, preferred_element_type=jnp.float32)
-        .astype(jnp.bfloat16)
-        .reshape(row_count, head_count * value_width)
-    )
-    grad_lambda_head = -jnp.sum(grad_combined * second_map, axis=(1, 2))
-    grad_first = first_map * (
-        grad_combined - jnp.sum(grad_combined * first_map, axis=-1, keepdims=True)
-    )
-    second_in = -lambda_head[:, None, None] * grad_combined
-    grad_second = second_map * (second_in - jnp.sum(second_in * second_map, axis=-1, keepdims=True))
-    grad_scores = jnp.stack([grad_first, grad_second], axis=1).astype(jnp.bfloat16)
-    grad_query_roped = (
-        jnp.einsum("hmts,shmd->thmd", grad_scores, key_rows, preferred_element_type=jnp.float32)
-        * score_scale
-    )
-    grad_key_roped = (
-        jnp.einsum("hmts,thmd->shmd", grad_scores, query_rows, preferred_element_type=jnp.float32)
-        * score_scale
-    )
-    grad_query = (
-        rotate_back(grad_query_roped, cosine_table, sine_table)
-        .astype(jnp.bfloat16)
-        .reshape(row_count, head_count * 2 * map_width)
-    )
-    grad_key = (
-        rotate_back(grad_key_roped, cosine_table, sine_table)
-        .astype(jnp.bfloat16)
-        .reshape(row_count, head_count * 2 * map_width)
-    )
+def forward_kernel(
+    lam, rows, gain, query_weight, key_weight, value_weight, cosine, sine, segment_column,
+    segment_row, sub_scale, normed_one, query, key, value, mixed, heads_out,
+):
+    head_count, width = sub_scale.shape
+    scale = (width // 2) ** (-0.5)
+    values = rows[...].astype(jnp.float32)
+    normed_one[...] = (values * root_of(values) * gain[...]).astype(jnp.bfloat16)
+    raw_query = f32_dot(normed_one[...], query_weight[...])
+    raw_key = f32_dot(normed_one[...], key_weight[...])
+    value[...] = f32_dot(normed_one[...], value_weight[...]).astype(jnp.bfloat16)
+    for head in range(head_count):
+        at = slice(head * width, (head + 1) * width)
+        query[:, at] = turn(raw_query[:, at], cosine[...], sine[...]).astype(jnp.bfloat16)
+        key[:, at] = turn(raw_key[:, at], cosine[...], sine[...]).astype(jnp.bfloat16)
+    for block in range(rows.shape[0] // block_rows):
+        first, last = key_range(block)
+        here = slice(block * block_rows, last)
+        opened = open_pairs(block, segment_column, segment_row)
+        for head in range(head_count):
+            at = slice(head * width, (head + 1) * width)
+            keys = key[first:last, at]
+            maps = [softmax_map(map_of(query[here, at], c), keys, opened, scale) for c in range(2)]
+            combined = (maps[0] - lam[head] * maps[1]).astype(jnp.bfloat16)
+            out = f32_dot(combined, value[first:last, at])
+            mixed[here, at] = out
+            heads_out[here, at] = (out * root_of(out) * sub_scale[head : head + 1, :]).astype(
+                jnp.bfloat16
+            )
+
+
+def backward_kernel(
+    lam, grad_attended, out_weight, query, key, value, mixed, cosine, sine, segment_column,
+    segment_row, sub_scale, grad_rows, grad_sub, grad_lam, grad_heads, grad_mixed, grad_key,
+    grad_value,
+):
+    head_count, width = sub_scale.shape
+    row_count = query.shape[0]
+    inner = head_count * width
+    scale = (width // 2) ** (-0.5)
+    grad_heads[...] = dot_t(grad_attended[...], out_weight[...])
+    for head in range(head_count):
+        at = slice(head * width, (head + 1) * width)
+        heads = mixed[:, at]
+        root = root_of(heads)
+        grads = grad_heads[:, at]
+        grad_sub[head : head + 1, :] = jnp.sum(grads * heads * root, axis=0, keepdims=True) * (
+            1.0 - lambda_base
+        )
+        grad_mixed[:, at] = rms_back(grads * sub_scale[head : head + 1, :], heads, root).astype(
+            jnp.bfloat16
+        )
+    grad_key[...] = jnp.zeros_like(grad_key)
+    grad_value[...] = jnp.zeros_like(grad_value)
+    lam_sums = [0.0] * head_count
+    for block in range(row_count // block_rows):
+        first, last = key_range(block)
+        here = slice(block * block_rows, last)
+        opened = open_pairs(block, segment_column, segment_row)
+        for head in range(head_count):
+            at = slice(head * width, (head + 1) * width)
+            keys = key[first:last, at]
+            queries = [map_of(query[here, at], c) for c in range(2)]
+            maps = [softmax_map(queries[c], keys, opened, scale) for c in range(2)]
+            mixes = grad_mixed[here, at]
+            combined = (maps[0] - lam[head] * maps[1]).astype(jnp.bfloat16)
+            grad_value[first:last, at] += dot_rows(combined, mixes)
+            grads = dot_t(mixes, value[first:last, at])
+            first_sum = jnp.sum(grads * maps[0], axis=-1, keepdims=True)
+            second_sum = jnp.sum(grads * maps[1], axis=-1, keepdims=True)
+            lam_sums[head] = lam_sums[head] + jnp.sum(second_sum, axis=0, keepdims=True)
+            score_grads = [
+                (maps[0] * (grads - first_sum)).astype(jnp.bfloat16),
+                (maps[1] * (-lam[head] * (grads - second_sum))).astype(jnp.bfloat16),
+            ]
+            grad_query = f32_dot(score_grads[0], map_of(keys, 0)) + f32_dot(
+                score_grads[1], map_of(keys, 1)
+            )
+            grad_rows[here, at] = turn(
+                grad_query * scale, cosine[here, :], -sine[here, :]
+            ).astype(jnp.bfloat16)
+            grad_key[first:last, at] += dot_rows(score_grads[0], queries[0]) + dot_rows(
+                score_grads[1], queries[1]
+            )
+    for head in range(head_count):
+        at = slice(head * width, (head + 1) * width)
+        grad_rows[:, inner + head * width : inner + (head + 1) * width] = turn(
+            grad_key[:, at] * scale, cosine[...], -sine[...]
+        ).astype(jnp.bfloat16)
+        grad_lam[head : head + 1, :] = jnp.broadcast_to(-lam_sums[head], (1, width))
+    grad_rows[:, 2 * inner :] = grad_value[...].astype(jnp.bfloat16)
+
+
+def in_vmem(count):
+    return [pl.BlockSpec(memory_space=pltpu.VMEM)] * count
+
+
+def attention_forward(row_in, tables, lam, sub_scale, norm1_gain, projections):
+    row_count, depth = row_in.shape
+    inner = projections[0].shape[1]
+    narrow = jax.ShapeDtypeStruct((row_count, inner), jnp.bfloat16)
+    return pl.pallas_call(
+        forward_kernel,
+        out_shape=[
+            jax.ShapeDtypeStruct((row_count, depth), jnp.bfloat16),
+            narrow,
+            narrow,
+            narrow,
+            jax.ShapeDtypeStruct((row_count, inner), jnp.float32),
+            narrow,
+        ],
+        in_specs=[pl.BlockSpec(memory_space=pltpu.SMEM)] + in_vmem(10),
+        out_specs=in_vmem(6),
+        compiler_params=pltpu.CompilerParams(vmem_limit_bytes=32 * 1024 * 1024),
+        cost_estimate=pl.CostEstimate(
+            flops=12 * row_count * depth * inner, bytes_accessed=8 << 20, transcendentals=0
+        ),
+    )(lam, row_in, norm1_gain[None, :], *projections, *tables, sub_scale)
+
+
+def attention_backward(grad_attended, out_weight, kept, tables, lam, sub_scale):
+    row_count, depth = grad_attended.shape
+    head_count, width = sub_scale.shape
+    inner = out_weight.shape[0]
+    small = jax.ShapeDtypeStruct((head_count, width), jnp.float32)
+    return pl.pallas_call(
+        backward_kernel,
+        out_shape=[jax.ShapeDtypeStruct((row_count, 3 * inner), jnp.bfloat16), small, small],
+        in_specs=[pl.BlockSpec(memory_space=pltpu.SMEM)] + in_vmem(11),
+        out_specs=in_vmem(3),
+        scratch_shapes=[
+            pltpu.VMEM((row_count, inner), jnp.float32),
+            pltpu.VMEM((row_count, inner), jnp.bfloat16),
+            pltpu.VMEM((row_count, inner), jnp.float32),
+            pltpu.VMEM((row_count, inner), jnp.float32),
+        ],
+        compiler_params=pltpu.CompilerParams(vmem_limit_bytes=32 * 1024 * 1024),
+        cost_estimate=pl.CostEstimate(
+            flops=12 * row_count * depth * inner, bytes_accessed=8 << 20, transcendentals=0
+        ),
+    )(lam, grad_attended, out_weight, *kept, *tables, sub_scale)
+
+
+def through_projections(grad_rows, projections, core):
+    inner = projections[0].shape[1]
 
     def partial(which):
-        return (
-            dot_t(half_rows(grad_query, which), query_weight)
-            + dot_t(half_rows(grad_key, which), key_weight)
-            + dot_t(half_rows(grad_value, which), value_weight)
-        )
-
-    send = partial(1 - core)
-    keep = partial(core)
-    first_scale = (grad_lambda_head * first_exp)[:, None]
-    second_scale = (grad_lambda_head * second_exp)[:, None]
-    lambda_grad = jnp.stack(
-        [
-            first_scale * lambda_parts[:, 1],
-            first_scale * lambda_parts[:, 0],
-            -second_scale * lambda_parts[:, 3],
-            -second_scale * lambda_parts[:, 2],
-        ],
-        axis=1,
-    ).reshape(head_count, 4 * map_width)
-    return keep, send, grad_query, grad_key, grad_value, lambda_grad, grad_sub
+        rows = half_rows(grad_rows, which)
+        return sum(
+            dot_t(rows[:, i * inner : (i + 1) * inner], projections[i]) for i in range(3)
+        )
+
+    return partial(core), partial(1 - core)
 
 
 def feed_forward(normed_two, cot_rows, gate_weight, up_weight, down_weight):
@@ -519,20 +553,34 @@
     dp_count = lax.axis_size("dp")
     core = lax.axis_index("tensor") % 2
     head_count, lambda_width = lambda_param.shape
-    value_width = sub_gain.shape[1]
     doc_lengths = (short_lengths[0], long_lengths[0])
-    attention_weights = (
-        norm1_gain, query_weight, key_weight, value_weight, lambda_param, sub_gain, out_weight,
-    )
+    map_width = lambda_width // 4
+    projections = (query_weight, key_weight, value_weight)
+    lambda_parts = lambda_param.reshape(head_count, 4, map_width)
+    first_exp = jnp.exp(jnp.sum(lambda_parts[:, 0] * lambda_parts[:, 1], axis=-1))
+    second_exp = jnp.exp(jnp.sum(lambda_parts[:, 2] * lambda_parts[:, 3], axis=-1))
+    lam = first_exp - second_exp + lambda_base
+    sub_scale = sub_gain * (1.0 - lambda_base)
+    tables = []
+    for m in range(2):
+        position, segment = doc_tables(doc_lengths[m], layer_in.shape[1])
+        tables.append(
+            rotary_tables(position, map_width) + (segment[:, None], segment[None, :])
+        )
     cots = [mine_first(out_cotangent[m], core) for m in range(2)]
     half = cots[0].shape[0] // 2
     rows_in = [mine_first(layer_in[m], core).astype(jnp.float32) for m in range(2)]
     inputs = [rows_in[m][:half] for m in range(2)]
-    front = [attention_forward(layer_in[m], doc_lengths[m], attention_weights, core) for m in range(2)]
-    kept = [front[m][2] for m in range(2)]
+    front = [
+        attention_forward(layer_in[m], tables[m], lam, sub_scale, norm1_gain, projections)
+        for m in range(2)
+    ]
+    heads = [front[m][5] for m in range(2)]
     attended, middle, root_two, normed_two, ffn = [], [], [], [], []
     for m in range(2):
-        attended.append(tensor_sum(front[m][0], front[m][1]))
+        keep = f32_dot(half_rows(heads[m], core), out_weight)
+        send = f32_dot(half_rows(heads[m], 1 - core), out_weight)
+        attended.append(tensor_sum(keep, send))
         middle.append(inputs[m] + attended[m])
         root_two.append(root_of(middle[m]))
         normed_two.append((with_other(middle[m] * root_two[m]) * norm2_gain).astype(jnp.bfloat16))
@@ -556,16 +604,12 @@
         grad_attended.append(in_order(grad_middle, core).astype(jnp.bfloat16))
         back.append(
             attention_backward(
-                grad_attended[m], kept[m], (query_weight, key_weight, value_weight, out_weight), core
+                grad_attended[m], out_weight, front[m][1:5], tables[m], lam, sub_scale
             )
         )
-    heads_both = jnp.concatenate([kept[0][-1], kept[1][-1]], 0)
-    grad_rows = jnp.concatenate(
-        [jnp.concatenate([back[m][i] for i in (2, 3, 4)], 1) for m in range(2)], 0
-    )
     grad_out, grad_qkv = weight_scatter(
-        [jnp.concatenate(grad_attended, 0), jnp.concatenate([kept[0][3], kept[1][3]], 0)],
-        [heads_both, grad_rows],
+        [jnp.concatenate(grad_attended, 0), jnp.concatenate([front[0][0], front[1][0]], 0)],
+        [jnp.concatenate(heads, 0), jnp.concatenate([back[0][0], back[1][0]], 0)],
         [(0, 0), (1, 1)],
         dp_count,
         1,
@@ -576,7 +620,7 @@
         fed = tensor_sum(*ffn[m][1])
         out_rows = rows_in[m] + with_other(attended[m] + fed)
         out_blocks.append(in_order(out_rows, core).astype(jnp.bfloat16))
-        grad_normed_one = tensor_sum(back[m][0], back[m][1])
+        grad_normed_one = tensor_sum(*through_projections(back[m][0], projections, core))
         root_one = root_of(inputs[m])
         grad_norm1 = grad_norm1 + jnp.sum(grad_normed_one * inputs[m] * root_one, axis=0)
         through = through_two[m] + rms_back(grad_normed_one * norm1_gain, inputs[m], root_one)
@@ -584,11 +628,19 @@
         grad_blocks.append(in_order(grad_rows, core).astype(jnp.bfloat16))
     norms = jnp.stack([grad_norm1, grad_norm2])
     norms = norms + flip(norms, "tensor", 1)
-    small = [
-        norms,
-        back[0][5] + back[1][5],
-        back[0][6] + back[1][6],
-    ]
+    grad_lam = (back[0][2] + back[1][2])[:, :1]
+    first_scale = grad_lam * first_exp[:, None]
+    second_scale = grad_lam * second_exp[:, None]
+    lambda_grad = jnp.concatenate(
+        [
+            first_scale * lambda_parts[:, 1],
+            first_scale * lambda_parts[:, 0],
+            -second_scale * lambda_parts[:, 3],
+            -second_scale * lambda_parts[:, 2],
+        ],
+        axis=1,
+    )
+    small = [norms, lambda_grad, back[0][1] + back[1][1]]
     width = norms.shape[-1]
     packed = jnp.concatenate(
         [

time: 820 us -> 786 us (0.959)
  matrix products: 113 us -> 59.1 us
  other arithmetic: 127 us -> 80.8 us
  Pallas kernels: 379 us -> 418 us
  waiting for transfers between devices: 96.3 us -> 109 us
  local copies, waits for them, and re-layouts: 67.7 us -> 78.1 us
    pallas_call x0 -> x4, Pallas kernels: none -> 38.5 us  [the longest x2 20.6 us: attention_backward(): pl.pallas_call(backward_kernel, out_shape=[jax.ShapeDtypeStruct((row_coun...]
    dot_general x12 -> x0, matrix products: 25.8 us -> none  [the longest x2 10.3 us: attention_backward(): jnp.einsum('thd,shd->hts', grad_mixed, value_rows, preferred_element_type...]
    sub x4 -> x0, matrix products: 19.8 us -> none  [the longest x2 10.8 us: attention_backward(): second_in - jnp.sum(second_in * second_map, axis=-1, keepdims=True)]
    ppermute x26, waiting for transfers between devices: 91.9 us -> 105 us  [flip(): return lax.ppermute(values, axis_name, [(i, i ^ bit) for i in range(size)])]
    dot_general x18 -> x12, matrix products: 40.7 us -> 29.9 us  [f32_dot(): return jnp.dot(left, right, preferred_element_type=jnp.float32)]
    squeeze x0 -> x5, local copies, waits for them, and re-layouts: none -> 10.3 us  [the longest x1 4.97 us: on_device(): layer_in[m]]
    concatenate x6 -> x4, other arithmetic: 13 us -> 4.02 us  [the longest x1 2.11 us: on_device(): jnp.concatenate(heads, 0)]
    unnamed x362 -> x330, local copies, waits for them, and re-layouts: 27.7 us -> 35.4 us
  transfers between devices with their start and end apart: 32 -> 32, of which waited for: 9 -> 8; matrix products, arithmetic and copies ran while one was open for 25% -> 19% of each run, Pallas kernels for 47% -> 53%
where the time goes in v3:
time: 786 us; the launch traced here: 776 us
  Pallas kernels  418 us (53%)
  waiting for transfers between devices  109 us (14%)
  other arithmetic  80.8 us (10%)
  local copies, waits for them, and re-layouts  78.1 us (10%)
  matrix products  59.1 us (8%)
  starting transfers between devices  28 us (4%)
    pallas_call x2, Pallas kernels, weight_scatter(): pl.pallas_call(functools.partial(scatter_kernel, tuple(plan), line, len(l...  379 us
    ppermute x26, waiting for transfers between devices, flip(): return lax.ppermute(values, axis_name, [(i, i ^ bit) for i in range(size)])  105 us
    unnamed x330, local copies, waits for them, and re-layouts  35.4 us
    dot_general x12, matrix products, f32_dot(): return jnp.dot(left, right, preferred_element_type=jnp.float32)  29.9 us
    dot_general x22, matrix products, dot_t(): lax.dot_general(left, right, (((1,), (1,)), ((), ())), preferred_element_...  29.2 us
    pallas_call x2, Pallas kernels, attention_backward(): pl.pallas_call(backward_kernel, out_shape=[jax.ShapeDtypeStruct((row_coun...  20.6 us
    transpose x4, local copies, waits for them, and re-layouts, weight_scatter(): lefts = [left.T.reshape(line, 2, rows, tokens) for left in lefts]  19.4 us
    pallas_call x2, Pallas kernels, attention_forward(): pl.pallas_call(forward_kernel, out_shape=[jax.ShapeDtypeStruct((row_count...  17.9 us
  transfers between devices with their start and end apart: 32, of which 8 were waited for; matrix products, arithmetic and copies ran while one was open for 19% of the time, Pallas kernels for 53%

profile of v3, /device:TPU:0, one launch (start us, length us, event | category | flops | bytes accessed | tf_op | source)
XLA Modules:
  0.0 775.8 jit_solution(14576790118407934440)
XLA Ops:
  0.7 5.0 slice_bitcast_fusion.9
  15.1 8.8 %shard_map.246 = (bf16[512,1536]{1,0:T(8,128)(2,1)S(1)}, bf16[512,384]{1,0:T(8,128)(2,1)S(1)}, bf16[512,384]{1,0:T(8,128)(2,1)S(1)}, bf16[512,384]{1,0:T(8,128)(...) custom-call(f32[3]{0:T(128)S(1)} %get-tuple-element.161.lam, bf16[512,1536]{1,0:T(8,128)(2,1)S(1)} %copy-done.22, ...), custom_call_target="tpu_custom_call" | custom-call | flops 3623878656 | bytes 8388608 | tf_op jit(solution)/shard_map/pallas_call | solution.py:460
  38.3 9.1 %shard_map.247 = (bf16[512,1536]{1,0:T(8,128)(2,1)S(1)}, bf16[512,384]{1,0:T(8,128)(2,1)S(1)}, bf16[512,384]{1,0:T(8,128)(2,1)S(1)}, bf16[512,384]{1,0:T(8,128)(...) custom-call(f32[3]{0:T(128)S(1)} %copy-done.50, bf16[512,1536]{1,0:T(8,128)(2,1)S(1)} %copy-done.21, ...), custom_call_target="tpu_custom_call" | custom-call | flops 3623878656 | bytes 8388608 | tf_op jit(solution)/shard_map/pallas_call | solution.py:460
  68.4 28.1 %collective-permute-done.1 = f32[256,1536]{1,0:T(8,128)S(1)} collective-permute-done((f32[256,1536]{1,0:T(8,128)S(1)}, f32[256,1536]{1,0:T(8,128)S(1)}, u32[]{:S(2)}, u32[]{:S(2)}) %collective-permute-start.1) | collective-permute-done | bytes 1572896 | tf_op jit(solution)/shard_map/ppermute | solution.py:99
  100.5 29.1 %collective-permute-done.7 = f32[256,1536]{1,0:T(8,128)S(1)} collective-permute-done((f32[256,1536]{1,0:T(8,128)S(1)}, f32[256,1536]{1,0:T(8,128)S(1)}, u32[]{:S(2)}, u32[]{:S(2)}) %collective-permute-start.7) | collective-permute-done | bytes 1572896 | tf_op jit(solution)/shard_map/ppermute | solution.py:99
  144.6 4.7 copy.95
  149.3 5.2 copy.96
  156.6 3.9 fusion.34
  163.6 3.8 fusion
  194.7 4.7 copy.97
  206.8 3.5 convolution_add_fusion.4
  212.1 3.6 convolution_add_fusion.5
  216.1 10.9 %collective-permute-done.13 = f32[256,1536]{1,0:T(8,128)} collective-permute-done((f32[256,1536]{1,0:T(8,128)S(1)}, f32[256,1536]{1,0:T(8,128)}, u32[]{:S(2)}, u32[]{:S(2)}) %collective-permute-start.13) | collective-permute-done | bytes 1572896 | tf_op jit(solution)/shard_map/ppermute | solution.py:99
  227.1 33.7 %collective-permute-done.19 = f32[256,1536]{1,0:T(8,128)} collective-permute-done((f32[256,1536]{1,0:T(8,128)S(1)}, f32[256,1536]{1,0:T(8,128)}, u32[]{:S(2)}, u32[]{:S(2)}) %collective-permute-start.19) | collective-permute-done | bytes 1572896 | tf_op jit(solution)/shard_map/ppermute | solution.py:99
  266.4 241.5 %shard_map.251 = (f32[192,1024]{1,0:T(8,128)S(1)}, f32[192,1024]{1,0:T(8,128)S(1)}, f32[192,1024]{1,0:T(8,128)S(1)}) custom-call(bf16[4,2,192,1024]{3,2,1,0:T(8,128)(2,1)} %bitcast.185, bf16[4,2,192,1024]{3,2,1,0:T(8,128)(2,1)} %bitcast.186, bf16[1024,1024]{1,0:T(8,128)(2,1)S(1)} %pad_maximum_fusion.3.refs_2_, bf16[1024,1024]{1,0:T(8,128)(2,1)} %pad_maximum_fusion.4.refs_3_, ...), custom_call_target="tpu_custom_call" | custom-call | flops 9663676416 | bytes 603979776 | tf_op jit(solution)/shard_map/pallas_call | solution.py:323
  518.0 10.2 %shard_map.248 = (bf16[512,1152]{1,0:T(8,128)(2,1)S(1)}, f32[3,128]{1,0:T(4,128)S(1)}, f32[3,128]{1,0:T(4,128)S(1)}) custom-call(f32[3]{0:T(128)S(1)} %copy-done.51, bf16[512,1536]{1,0:T(8,128)(2,1)S(1)} %fusion.6.grad_attended, bf16[384,1536]{1,0:T(8,128)(2,1)S(1)} %copy-done.5, bf16[512,384]{1,0:T(8,128)(2,1)S(1)} %copy-done.63, ...), custom_call_target="tpu_custom_call" | custom-call | flops 3623878656 | bytes 8388608 | tf_op jit(solution)/shard_map/pallas_call | solution.py:484
  535.6 10.4 %shard_map.249 = (bf16[512,1152]{1,0:T(8,128)(2,1)S(1)}, f32[3,128]{1,0:T(4,128)S(1)}, f32[3,128]{1,0:T(4,128)S(1)}) custom-call(f32[3]{0:T(128)S(1)} %copy-done.51, bf16[512,1536]{1,0:T(8,128)(2,1)S(1)} %fusion.9.grad_attended, bf16[384,1536]{1,0:T(8,128)(2,1)S(1)} %copy-done.5, bf16[512,384]{1,0:T(8,128)(2,1)S(1)} %copy-done.57, ...), custom_call_target="tpu_custom_call" | custom-call | flops 3623878656 | bytes 8388608 | tf_op jit(solution)/shard_map/pallas_call | solution.py:484
  558.7 4.9 copy.94
  566.0 4.0 fusion.5
  583.2 137.6 %shard_map.250 = (f32[192,384]{1,0:T(8,128)S(1)}, f32[192,1152]{1,0:T(8,128)S(1)}) custom-call(bf16[4,2,192,1024]{3,2,1,0:T(8,128)(2,1)} %bitcast.187, bf16[4,2,192,1024]{3,2,1,0:T(8,128)(2,1)} %bitcast.184, bf16[1024,384]{1,0:T(8,128)(2,1)S(1)} %copy-done.33, bf16[1024,1152]{1,0:T(8,128)(2,1)S(1)} %pad_maximum_fusion.2.refs_3_), custom_call_target="tpu_custom_call" | custom-call | flops 4831838208 | bytes 301989888 | tf_op jit(solution)/shard_map/pallas_call | solution.py:323
  729.2 3.4 collective-permute-start.26
  734.0 4.2 collective-permute-start.27
  738.2 6.8 subtract_add_fusion.1
  753.2 3.5 collective-permute-done.31
  (526 shorter events, 192.1 us)
Async XLA Ops:
  26.2 28.7 %collective-permute-start = (f32[256,1536]{1,0:T(8,128)}, f32[256,1536]{1,0:T(8,128)}, u32[]{:S(2)}, u32[]{:S(2)}) collective-permute-start(f32[256,1536]{1,0:T(8,128)} %fusion.55), channel_id=1, source_target_pairs={{0,1},{1,0},{2,3},{3,2},{4,5},{5,4},{6,7},{7,6},{8,9},{9,8},{10,11... | collective-permute-start | bytes 4718600 | tf_op jit(solution)/shard_map/ppermute | solution.py:99
  58.3 38.2 %collective-permute-start.1 = (f32[256,1536]{1,0:T(8,128)S(1)}, f32[256,1536]{1,0:T(8,128)S(1)}, u32[]{:S(2)}, u32[]{:S(2)}) collective-permute-start(f32[256,1536]{1,0:T(8,128)S(1)} %convolution_add_fusion.15), channel_id=1, source_target_pairs={{0,2},{1,3},{2,0},{3,1},{4,6},{5,7},{6,4},{7,5},{8,10},{9,11},{10,... | collective-permute-start | bytes 4718600 | tf_op jit(solution)/shard_map/ppermute | solution.py:99
  66.4 63.2 %collective-permute-start.7 = (f32[256,1536]{1,0:T(8,128)S(1)}, f32[256,1536]{1,0:T(8,128)S(1)}, u32[]{:S(2)}, u32[]{:S(2)}) collective-permute-start(f32[256,1536]{1,0:T(8,128)S(1)} %convolution_add_fusion.14), channel_id=1, source_target_pairs={{0,2},{1,3},{2,0},{3,1},{4,6},{5,7},{6,4},{7,5},{8,10},{9,11},{10,... | collective-permute-start | bytes 4718600 | tf_op jit(solution)/shard_map/ppermute | solution.py:99
  100.5 63.1 %collective-permute-start.2 = (f32[256,1536]{1,0:T(8,128)}, f32[256,1536]{1,0:T(8,128)}, u32[]{:S(2)}, u32[]{:S(2)}) collective-permute-start(f32[256,1536]{1,0:T(8,128)} %broadcast_multiply_fusion.1), channel_id=1, source_target_pairs={{0,1},{1,0},{2,3},{3,2},{4,5},{5,4},{6,7},{7,6},{8,9},{9,8},{10,11... | collective-permute-start | bytes 4718600 | tf_op jit(solution)/shard_map/ppermute | solution.py:99
  133.8 29.8 %collective-permute-start.8 = (f32[256,1536]{1,0:T(8,128)}, f32[256,1536]{1,0:T(8,128)}, u32[]{:S(2)}, u32[]{:S(2)}) collective-permute-start(f32[256,1536]{1,0:T(8,128)} %broadcast_multiply_fusion), channel_id=1, source_target_pairs={{0,1},{1,0},{2,3},{3,2},{4,5},{5,4},{6,7},{7,6},{8,9},{9,8},{10,11... | collective-permute-start | bytes 4718600 | tf_op jit(solution)/shard_map/ppermute | solution.py:99
  175.9 12.7 %collective-permute-start.12 = (f32[256,1536]{1,0:T(8,128)S(1)}, f32[256,1536]{1,0:T(8,128)S(1)}, u32[]{:S(2)}, u32[]{:S(2)}) collective-permute-start(f32[256,1536]{1,0:T(8,128)S(1)} %convolution_add_fusion.2), channel_id=1, source_target_pairs={{0,1},{1,0},{2,3},{3,2},{4,5},{5,4},{6,7},{7,6},{8,9},{9,8},{10,11... | collective-permute-start | bytes 4718600 | tf_op jit(solution)/shard_map/ppermute | solution.py:99
  183.7 21.6 %collective-permute-start.9 = (f32[256,1536]{1,0:T(8,128)}, f32[256,1536]{1,0:T(8,128)}, u32[]{:S(2)}, u32[]{:S(2)}) collective-permute-start(f32[256,1536]{1,0:T(8,128)} %fusion.28), channel_id=1, source_target_pairs={{0,1},{1,0},{2,3},{3,2},{4,5},{5,4},{6,7},{7,6},{8,9},{9,8},{10,11... | collective-permute-start | bytes 4718600 | tf_op jit(solution)/shard_map/ppermute | solution.py:99
  186.0 26.1 %collective-permute-start.3 = (f32[256,1536]{1,0:T(8,128)}, f32[256,1536]{1,0:T(8,128)}, u32[]{:S(2)}, u32[]{:S(2)}) collective-permute-start(f32[256,1536]{1,0:T(8,128)} %fusion.31), channel_id=1, source_target_pairs={{0,1},{1,0},{2,3},{3,2},{4,5},{5,4},{6,7},{7,6},{8,9},{9,8},{10,11... | collective-permute-start | bytes 4718600 | tf_op jit(solution)/shard_map/ppermute | solution.py:99
  189.7 37.4 %collective-permute-start.13 = (f32[256,1536]{1,0:T(8,128)S(1)}, f32[256,1536]{1,0:T(8,128)}, u32[]{:S(2)}, u32[]{:S(2)}) collective-permute-start(f32[256,1536]{1,0:T(8,128)S(1)} %fusion.14), channel_id=1, source_target_pairs={{0,2},{1,3},{2,0},{3,1},{4,6},{5,7},{6,4},{7,5},{8,10},{9,11},{10,... | collective-permute-start | bytes 4718600 | tf_op jit(solution)/shard_map/ppermute | solution.py:99
  192.5 68.3 %collective-permute-start.19 = (f32[256,1536]{1,0:T(8,128)S(1)}, f32[256,1536]{1,0:T(8,128)}, u32[]{:S(2)}, u32[]{:S(2)}) collective-permute-start(f32[256,1536]{1,0:T(8,128)S(1)} %fusion.15), channel_id=1, source_target_pairs={{0,2},{1,3},{2,0},{3,1},{4,6},{5,7},{6,4},{7,5},{8,10},{9,11},{10,... | collective-permute-start | bytes 4718600 | tf_op jit(solution)/shard_map/ppermute | solution.py:99
  210.4 297.6 %collective-permute-start.10 = (f32[256,1536]{1,0:T(8,128)}, f32[256,1536]{1,0:T(8,128)}, u32[]{:S(2)}, u32[]{:S(2)}) collective-permute-start(f32[256,1536]{1,0:T(8,128)} %convolution_add_fusion.4), channel_id=1, source_target_pairs={{0,2},{1,3},{2,0},{3,1},{4,6},{5,7},{6,4},{7,5},{8,10},{9,11},{10,... | collective-permute-start | bytes 4718600 | tf_op jit(solution)/shard_map/ppermute | solution.py:99
  215.7 295.5 %collective-permute-start.4 = (f32[256,1536]{1,0:T(8,128)}, f32[256,1536]{1,0:T(8,128)}, u32[]{:S(2)}, u32[]{:S(2)}) collective-permute-start(f32[256,1536]{1,0:T(8,128)} %convolution_add_fusion.5), channel_id=1, source_target_pairs={{0,2},{1,3},{2,0},{3,1},{4,6},{5,7},{6,4},{7,5},{8,10},{9,11},{10,... | collective-permute-start | bytes 4718600 | tf_op jit(solution)/shard_map/ppermute | solution.py:99
  266.3 249.0 %collective-permute-start.14 = (f32[256,1536]{1,0:T(8,128)S(1)}, f32[256,1536]{1,0:T(8,128)S(1)}, u32[]{:S(2)}, u32[]{:S(2)}) collective-permute-start(f32[256,1536]{1,0:T(8,128)S(1)} %get-tuple-element.124), channel_id=1, source_target_pairs={{0,1},{1,0},{2,3},{3,2},{4,5},{5,4},{6,7},{7,6},{8,9},{9,8},{10,11... | collective-permute-start | bytes 4718600 | tf_op jit(solution)/shard_map/ppermute | solution.py:99
  511.1 39.0 %collective-permute-start.11 = (f32[256,1536]{1,0:T(8,128)S(1)}, f32[256,1536]{1,0:T(8,128)S(1)}, u32[]{:S(2)}, u32[]{:S(2)}) collective-permute-start(f32[256,1536]{1,0:T(8,128)S(1)} %add_add_fusion), channel_id=1, source_target_pairs={{0,1},{1,0},{2,3},{3,2},{4,5},{5,4},{6,7},{7,6},{8,9},{9,8},{10,11... | collective-permute-start | bytes 4718600 | tf_op jit(solution)/shard_map/ppermute | solution.py:99
  514.0 42.2 %collective-permute-start.5 = (f32[256,1536]{1,0:T(8,128)S(1)}, f32[256,1536]{1,0:T(8,128)S(1)}, u32[]{:S(2)}, u32[]{:S(2)}) collective-permute-start(f32[256,1536]{1,0:T(8,128)S(1)} %add_add_fusion.1), channel_id=1, source_target_pairs={{0,1},{1,0},{2,3},{3,2},{4,5},{5,4},{6,7},{7,6},{8,9},{9,8},{10,11... | collective-permute-start | bytes 4718600 | tf_op jit(solution)/shard_map/ppermute | solution.py:99
  514.2 18.9 %collective-permute-start.20 = (f32[256,1536]{1,0:T(8,128)S(1)}, f32[256,1536]{1,0:T(8,128)S(1)}, u32[]{:S(2)}, u32[]{:S(2)}) collective-permute-start(f32[256,1536]{1,0:T(8,128)S(1)} %get-tuple-element.125), channel_id=1, source_target_pairs={{0,1},{1,0},{2,3},{3,2},{4,5},{5,4},{6,7},{7,6},{8,9},{9,8},{10,11... | collective-permute-start | bytes 4718600 | tf_op jit(solution)/shard_map/ppermute | solution.py:99
  533.0 38.9 %collective-permute-start.15 = (f32[256,1536]{1,0:T(8,128)}, f32[256,1536]{1,0:T(8,128)}, u32[]{:S(2)}, u32[]{:S(2)}) collective-permute-start(f32[256,1536]{1,0:T(8,128)} %convolution_add_fusion.10), channel_id=1, source_target_pairs={{0,1},{1,0},{2,3},{3,2},{4,5},{5,4},{6,7},{7,6},{8,9},{9,8},{10,11... | collective-permute-start | bytes 4718600 | tf_op jit(solution)/shard_map/ppermute | solution.py:99
  549.1 26.5 %collective-permute-start.21 = (f32[256,1536]{1,0:T(8,128)}, f32[256,1536]{1,0:T(8,128)}, u32[]{:S(2)}, u32[]{:S(2)}) collective-permute-start(f32[256,1536]{1,0:T(8,128)} %convolution_add_fusion.6), channel_id=1, source_target_pairs={{0,1},{1,0},{2,3},{3,2},{4,5},{5,4},{6,7},{7,6},{8,9},{9,8},{10,11... | collective-permute-start | bytes 4718600 | tf_op jit(solution)/shard_map/ppermute | solution.py:99
  574.0 146.8 %collective-permute-start.16 = (f32[256,1536]{1,0:T(8,128)S(1)}, f32[256,1536]{1,0:T(8,128)}, u32[]{:S(2)}, u32[]{:S(2)}) collective-permute-start(f32[256,1536]{1,0:T(8,128)S(1)} %fusion.13), channel_id=1, source_target_pairs={{0,2},{1,3},{2,0},{3,1},{4,6},{5,7},{6,4},{7,5},{8,10},{9,11},{10,... | collective-permute-start | bytes 4718600 | tf_op jit(solution)/shard_map/ppermute | solution.py:99
  577.8 143.0 %collective-permute-start.22 = (f32[256,1536]{1,0:T(8,128)S(1)}, f32[256,1536]{1,0:T(8,128)}, u32[]{:S(2)}, u32[]{:S(2)}) collective-permute-start(f32[256,1536]{1,0:T(8,128)S(1)} %fusion.12), channel_id=1, source_target_pairs={{0,2},{1,3},{2,0},{3,1},{4,6},{5,7},{6,4},{7,5},{8,10},{9,11},{10,... | collective-permute-start | bytes 4718600 | tf_op jit(solution)/shard_map/ppermute | solution.py:99
  732.7 12.3 %collective-permute-start.29 = (f32[1,528]{1,0:T(1,128)S(1)}, f32[1,528]{1,0:T(1,128)S(1)}, u32[]{:S(2)}, u32[]{:S(2)}) collective-permute-start(f32[1,528]{1,0:T(1,128)S(1)} %get-tuple-element.119), channel_id=1, source_target_pairs={{24,16},{28,20},{25,17},{29,21},{26,18},{30,22},{27,19},{31,23}} | collective-permute-start | bytes 6344 | tf_op jit(solution)/shard_map/ppermute | solution.py:143
  734.0 11.0 %collective-permute-start.27 = (f32[1,528]{1,0:T(1,128)S(1)}, f32[1,528]{1,0:T(1,128)S(1)}, u32[]{:S(2)}, u32[]{:S(2)}) collective-permute-start(f32[1,528]{1,0:T(1,128)S(1)} %fusion.74), channel_id=1, source_target_pairs={{0,8},{4,12},{8,16},{12,20},{1,9},{5,13},{9,17},{13,21},{2,10},{6,... | collective-permute-start | bytes 6344 | tf_op jit(solution)/shard_map/ppermute | solution.py:140
  745.0 13.8 %collective-permute-start.23 = (f32[256,1536]{1,0:T(8,128)}, f32[256,1536]{1,0:T(8,128)}, u32[]{:S(2)}, u32[]{:S(2)}) collective-permute-start(f32[256,1536]{1,0:T(8,128)} %get-tuple-element.121), channel_id=1, source_target_pairs={{0,1},{1,0},{2,3},{3,2},{4,5},{5,4},{6,7},{7,6},{8,9},{9,8},{10,11... | collective-permute-start | bytes 4718600 | tf_op jit(solution)/shard_map/ppermute | solution.py:99
  747.7 13.6 %collective-permute-start.17 = (f32[256,1536]{1,0:T(8,128)}, f32[256,1536]{1,0:T(8,128)}, u32[]{:S(2)}, u32[]{:S(2)}) collective-permute-start(f32[256,1536]{1,0:T(8,128)} %get-tuple-element.120), channel_id=1, source_target_pairs={{0,1},{1,0},{2,3},{3,2},{4,5},{5,4},{6,7},{7,6},{8,9},{9,8},{10,11... | collective-permute-start | bytes 4718600 | tf_op jit(solution)/shard_map/ppermute | solution.py:99
  (171 other events, 2896.7 us)

commit v4 on v3

v4 whole, which is shorter than its diff:
```python
import functools
import math

import jax
import jax.numpy as jnp
from jax import lax
from jax.experimental import pallas as pl
from jax.experimental.pallas import tpu as pltpu
from jax.sharding import PartitionSpec as P

norm_epsilon = 1e-05
lambda_base = 0.8 - 0.6 * math.exp(-0.3 * 11.0)
rotary_base = 10000.0
closed_score = -1e30
block_rows = 128
longest_document = 256
row_group = 16
send_slots = 3
held_slots = 4
MESH = pl.DeviceIdType.MESH


def doc_tables(lengths, row_count):
    doc_ends = jnp.cumsum(lengths, dtype=jnp.int32)
    places = jnp.arange(row_count, dtype=jnp.int32)
    passed = (places[:, None] >= doc_ends[None, :]).astype(jnp.int32)
    segment = jnp.sum(passed, axis=1, dtype=jnp.int32)
    starts = jnp.sum(passed * lengths[None, :], axis=1, dtype=jnp.int32)
    return (places - starts, segment)


def rotary_tables(position, map_width):
    half_width = map_width // 2
    frequency = rotary_base ** (-2.0 * jnp.arange(half_width, dtype=jnp.float32) / map_width)
    angles = position.astype(jnp.float32)[:, None] * frequency[None, :]
    cosine, sine = jnp.cos(angles), jnp.sin(angles)
    return (
        jnp.concatenate([cosine] * 4, axis=1),
        jnp.concatenate([-sine, sine, -sine, sine], axis=1),
    )


def turn(values, cosine, sine):
    width = values.shape[-1]
    quarter = width // 4
    lane = lax.broadcasted_iota(jnp.int32, values.shape, 1)
    partner = jnp.where(
        lane % (2 * quarter) < quarter,
        pltpu.roll(values, width - quarter, 1),
        pltpu.roll(values, quarter, 1),
    )
    return values * cosine + partner * sine


def map_of(values, which):
    lane = lax.broadcasted_iota(jnp.int32, values.shape, 1)
    mine = (lane >= values.shape[-1] // 2) == (which == 1)
    return jnp.where(mine, values, jnp.zeros_like(values))


def key_range(block):
    first = max(0, block * block_rows - longest_document + 1) // block_rows * block_rows
    return first, (block + 1) * block_rows


def open_pairs(block, segment_column, segment_row):
    first, last = key_range(block)
    rows = pl.ds(block * block_rows, block_rows)
    shape = (block_rows, last - first)
    row_at = lax.broadcasted_iota(jnp.int32, shape, 0) + block * block_rows
    key_at = lax.broadcasted_iota(jnp.int32, shape, 1) + first
    return (segment_column[rows, :] == segment_row[:, first:last]) & (key_at <= row_at)


def softmax_map(query, key, opened, scale):
    scores = jnp.where(opened, dot_t(query, key) * scale, closed_score)
    expanded = jnp.exp(scores - jnp.max(scores, axis=-1, keepdims=True))
    return expanded * (1.0 / jnp.sum(expanded, axis=-1, keepdims=True))


def f32_dot(left, right):
    return jnp.dot(left, right, preferred_element_type=jnp.float32)


def dot_t(left, right):
    return lax.dot_general(
        left, right, (((1,), (1,)), ((), ())), preferred_element_type=jnp.float32
    )


def dot_rows(left, right):
    return lax.dot_general(
        left, right, (((0,), (0,)), ((), ())), preferred_element_type=jnp.float32
    )


def flip(values, axis_name, bit):
    size = lax.axis_size(axis_name)
    return lax.ppermute(values, axis_name, [(i, i ^ bit) for i in range(size)])


def half_rows(values, which):
    count = values.shape[0] // 2
    return lax.dynamic_slice_in_dim(values, which * count, count, 0)


def mine_first(values, core):
    return jnp.concatenate([half_rows(values, core), half_rows(values, 1 - core)], axis=0)


def tensor_sum(keep, send):
    half = keep + flip(send, "tensor", 1)
    return half + flip(half, "tensor", 2)


def with_other(mine):
    return jnp.concatenate([mine, flip(mine, "tensor", 1)], axis=0)


def rms_back(incoming, values, inverse_root):
    return inverse_root * incoming - values * inverse_root**3 * jnp.mean(
        incoming * values, axis=-1, keepdims=True
    )


def root_of(values):
    return lax.rsqrt(jnp.mean(values * values, axis=-1, keepdims=True) + norm_epsilon)


def forward_kernel(
    lam, rows, gain, query_weight, key_weight, value_weight, cosine, sine, segment_column,
    segment_row, sub_scale, normed_one, query, key, value, mixed, heads_out,
):
    head_count, width = sub_scale.shape
    scale = (width // 2) ** (-0.5)
    values = rows[...].astype(jnp.float32)
    normed_one[...] = (values * root_of(values) * gain[...]).astype(jnp.bfloat16)
    raw_query = f32_dot(normed_one[...], query_weight[...])
    raw_key = f32_dot(normed_one[...], key_weight[...])
    value[...] = f32_dot(normed_one[...], value_weight[...]).astype(jnp.bfloat16)
    for head in range(head_count):
        at = slice(head * width, (head + 1) * width)
        query[:, at] = turn(raw_query[:, at], cosine[...], sine[...]).astype(jnp.bfloat16)
        key[:, at] = turn(raw_key[:, at], cosine[...], sine[...]).astype(jnp.bfloat16)
    for block in range(rows.shape[0] // block_rows):
        first, last = key_range(block)
        here = slice(block * block_rows, last)
        opened = open_pairs(block, segment_column, segment_row)
        for head in range(head_count):
            at = slice(head * width, (head + 1) * width)
            keys = key[first:last, at]
            maps = [softmax_map(map_of(query[here, at], c), keys, opened, scale) for c in range(2)]
            combined = (maps[0] - lam[head] * maps[1]).astype(jnp.bfloat16)
            out = f32_dot(combined, value[first:last, at])
            mixed[here, at] = out
            heads_out[here, at] = (out * root_of(out) * sub_scale[head : head + 1, :]).astype(
                jnp.bfloat16
            )


def backward_kernel(
    lam, grad_attended, out_weight, query, key, value, mixed, cosine, sine, segment_column,
    segment_row, sub_scale, grad_rows, grad_sub, grad_lam, grad_heads, grad_mixed, grad_key,
    grad_value,
):
    head_count, width = sub_scale.shape
    row_count = query.shape[0]
    inner = head_count * width
    scale = (width // 2) ** (-0.5)
    grad_heads[...] = dot_t(grad_attended[...], out_weight[...])
    for head in range(head_count):
        at = slice(head * width, (head + 1) * width)
        heads = mixed[:, at]
        root = root_of(heads)
        grads = grad_heads[:, at]
        grad_sub[head : head + 1, :] = jnp.sum(grads * heads * root, axis=0, keepdims=True) * (
            1.0 - lambda_base
        )
        grad_mixed[:, at] = rms_back(grads * sub_scale[head : head + 1, :], heads, root).astype(
            jnp.bfloat16
        )
    grad_key[...] = jnp.zeros_like(grad_key)
    grad_value[...] = jnp.zeros_like(grad_value)
    lam_sums = [0.0] * head_count
    for block in range(row_count // block_rows):
        first, last = key_range(block)
        here = slice(block * block_rows, last)
        opened = open_pairs(block, segment_column, segment_row)
        for head in range(head_count):
            at = slice(head * width, (head + 1) * width)
            keys = key[first:last, at]
            queries = [map_of(query[here, at], c) for c in range(2)]
            maps = [softmax_map(queries[c], keys, opened, scale) for c in range(2)]
            mixes = grad_mixed[here, at]
            combined = (maps[0] - lam[head] * maps[1]).astype(jnp.bfloat16)
            grad_value[first:last, at] += dot_rows(combined, mixes)
            grads = dot_t(mixes, value[first:last, at])
            first_sum = jnp.sum(grads * maps[0], axis=-1, keepdims=True)
            second_sum = jnp.sum(grads * maps[1], axis=-1, keepdims=True)
            lam_sums[head] = lam_sums[head] + jnp.sum(second_sum, axis=0, keepdims=True)
            score_grads = [
                (maps[0] * (grads - first_sum)).astype(jnp.bfloat16),
                (maps[1] * (-lam[head] * (grads - second_sum))).astype(jnp.bfloat16),
            ]
            grad_query = f32_dot(score_grads[0], map_of(keys, 0)) + f32_dot(
                score_grads[1], map_of(keys, 1)
            )
            grad_rows[here, at] = turn(
                grad_query * scale, cosine[here, :], -sine[here, :]
            ).astype(jnp.bfloat16)
            grad_key[first:last, at] += dot_rows(score_grads[0], queries[0]) + dot_rows(
                score_grads[1], queries[1]
            )
    for head in range(head_count):
        at = slice(head * width, (head + 1) * width)
        grad_rows[:, inner + head * width : inner + (head + 1) * width] = turn(
            grad_key[:, at] * scale, cosine[...], -sine[...]
        ).astype(jnp.bfloat16)
        grad_lam[head : head + 1, :] = jnp.broadcast_to(-lam_sums[head], (1, width))
    grad_rows[:, 2 * inner :] = grad_value[...].astype(jnp.bfloat16)


def in_vmem(count):
    return [pl.BlockSpec(memory_space=pltpu.VMEM)] * count


class Reducer:
    def __init__(self, plan, line, refs):
        self.plan, self.line = plan, line
        (
            self.send, self.held, self.total, self.landed, self.pair_out, self.pair_in,
            self.line_out, self.line_in, self.credit, self.out_sem,
        ) = refs
        self.me = lax.axis_index("dp")
        self.place, self.side = self.me // 2, self.me % 2
        self.other = self.me + 1 - 2 * self.side
        self.steps = line - 1
        self.ring = self.total.shape[0]
        self.rows = self.total.shape[2]

    def compute(self, c):
        item = self.plan[c]
        width = item.width
        left, right = item.left(), item.right()

        def block(at, carry):
            first = pl.multiple_of(2 * at * self.rows, self.rows)
            columns = right[...]
            away = left[pl.ds(first + (1 - self.side) * self.rows, self.rows), :]
            here = left[pl.ds(first + self.side * self.rows, self.rows), :]
            self.send[c % send_slots, at, :, :width] = f32_dot(away, columns)
            self.total[c % self.ring, at, :, :width] = f32_dot(here, columns)
            return carry

        lax.fori_loop(0, self.line, block, 0)
        item.computed()

    def pair_copy(self, c):
        width = self.plan[c].width
        return pltpu.make_async_remote_copy(
            src_ref=self.send.at[c % send_slots, :, :, :width],
            dst_ref=self.held.at[c % held_slots, :, :, :width],
            send_sem=self.pair_out.at[c % send_slots],
            recv_sem=self.pair_in.at[c % held_slots],
            device_id={"dp": self.other},
            device_id_type=MESH,
        )

    def pair_finish(self, c):
        width = self.plan[c].width
        self.pair_copy(c).wait_recv()

        def block(at, carry):
            self.total[c % self.ring, at, :, :width] += self.held[c % held_slots, at, :, :width]
            return carry

        lax.fori_loop(0, self.line, block, 0)
        self.pair_copy(c).wait_send()

    def line_copy(self, c, step, way, block, target):
        width = self.plan[c].width
        return pltpu.make_async_remote_copy(
            src_ref=self.total.at[c % self.ring, block, :, :width],
            dst_ref=self.landed.at[way, step, c % 2, :, :width],
            send_sem=self.line_out.at[way, step, c % 2],
            recv_sem=self.line_in.at[way, step, c % 2],
            device_id={"dp": target},
            device_id_type=MESH,
        )

    def line_sends(self, step, way):
        place, line = self.place, self.line
        if way == 0:
            block = line - 1 - step + place
            return (place <= step) & (place < line - 1), block, self.me + 2
        block = place + step - line + 1
        return (place >= line - 1 - step) & (place > 0), block, self.me - 2

    def line_gets(self, step, way):
        place, line = self.place, self.line
        if way == 0:
            return (place > 0) & (place - 1 <= step), line - 2 - step + place, self.me - 2
        gets = (place < line - 1) & (place + 1 >= line - 1 - step)
        return gets, place + step - line + 2, self.me + 2

    def line_start(self, c, step):
        for way in range(2):
            sends, block, target = self.line_sends(step, way)

            @pl.when(sends)
            def _():
                if c >= 2:
                    pl.semaphore_wait(self.credit.at[way, step], 1)
                self.line_copy(c, step, way, block, target).start()

    def line_finish(self, c, step):
        width = self.plan[c].width
        for way in range(2):
            gets, block, source = self.line_gets(step, way)

            @pl.when(gets)
            def _():
                self.line_copy(c, step, way, block, source).wait_recv()
                self.total[c % self.ring, block, :, :width] += self.landed[
                    way, step, c % 2, :, :width
                ]
                if c + 2 < len(self.plan):
                    pl.semaphore_signal(
                        self.credit.at[way, step],
                        inc=1,
                        device_id={"dp": source},
                        device_id_type=MESH,
                    )

            sends, sent, target = self.line_sends(step, way)

            @pl.when(sends)
            def _():
                self.line_copy(c, step, way, sent, target).wait_send()

    def out_copy(self, c):
        item = self.plan[c]
        return pltpu.make_async_copy(
            self.total.at[c % self.ring, self.place, :, : item.width],
            item.out.at[:, item.first : item.first + item.width],
            self.out_sem.at[c % self.ring],
        )

    def run(self, tasks):
        count, steps = len(self.plan), self.steps
        self.compute(0)
        self.pair_copy(0).start()
        self.compute(1)
        for slot in range(count + steps + 1):
            for step in range(steps):
                c = slot - 2 - step
                if 0 <= c < count:
                    self.line_finish(c, step)
            if 0 <= slot - 1 < count:
                self.pair_finish(slot - 1)
            for step in range(steps):
                c = slot - 1 - step
                if 0 <= c < count:
                    self.line_start(c, step)
            if slot + 1 < count:
                self.pair_copy(slot + 1).start()
            done = slot - 1 - steps
            if 0 <= done < count:
                self.out_copy(done).start()
            if slot + 2 < count:
                if slot + 2 >= self.ring:
                    self.out_copy(slot + 2 - self.ring).wait()
                self.compute(slot + 2)
            for task in tasks.get(slot, ()):
                task()
        for c in range(max(0, count - self.ring), count):
            self.out_copy(c).wait()


class Chunk:
    def __init__(self, left, right, computed, out, first, width):
        self.left, self.right, self.computed = left, right, computed
        self.out, self.first, self.width = out, first, width


def for_rows(count, body):
    def step(i, carry):
        body(pl.ds(pl.multiple_of(i * row_group, row_group), row_group))
        return carry

    lax.fori_loop(0, count // row_group, step, 0)


class TensorSum:
    def __init__(self, uses, own, near, far, near_sems, far_sems, near_credit, far_credit):
        self.own, self.near, self.far = own, near, far
        self.near_sems, self.far_sems = near_sems, far_sems
        self.near_credit, self.far_credit = near_credit, far_credit
        index = lax.axis_index("tensor")
        self.core_peer = index + 1 - 2 * (index % 2)
        self.far_peer = index + 2 - 4 * (index // 2)
        self.near_left, self.far_left = 2 * uses, uses
        self.near_first, self.far_first = True, True

    def near_copy(self, source):
        return pltpu.make_async_remote_copy(
            src_ref=source, dst_ref=self.near, send_sem=self.near_sems.at[0],
            recv_sem=self.near_sems.at[1], device_id={"tensor": self.core_peer},
            device_id_type=MESH,
        )

    def far_copy(self):
        return pltpu.make_async_remote_copy(
            src_ref=self.own, dst_ref=self.far, send_sem=self.far_sems.at[0],
            recv_sem=self.far_sems.at[1], device_id={"tensor": self.far_peer},
            device_id_type=MESH,
        )

    def near_start(self, source):
        if not self.near_first:
            pl.semaphore_wait(self.near_credit, 1)
        self.near_first = False
        self.pending = source
        self.near_copy(source).start()

    def near_wait(self):
        self.near_copy(self.pending).wait()

    def near_free(self):
        self.near_left -= 1
        if self.near_left:
            pl.semaphore_signal(
                self.near_credit, inc=1, device_id={"tensor": self.core_peer}, device_id_type=MESH
            )

    def far_start(self):
        self.near_wait()

        def add(rows):
            self.own[rows, :] += self.near[rows, :]

        for_rows(self.own.shape[0], add)
        self.near_free()
        if not self.far_first:
            pl.semaphore_wait(self.far_credit, 1)
        self.far_first = False
        self.far_copy().start()

    def far_wait(self):
        self.far_copy().wait()

    def far_free(self):
        self.far_left -= 1
        if self.far_left:
            pl.semaphore_signal(
                self.far_credit, inc=1, device_id={"tensor": self.far_peer}, device_id_type=MESH
            )


def back_kernel(dp_count, *refs):
    refs = list(refs)
    take = lambda n: [refs.pop(0) for _ in range(n)]
    (lam,) = take(1)
    cot_left, two_left, one_left = [take(2) for _ in range(3)]
    hidden, gate_pre, up_pre, heads = [take(2) for _ in range(4)]
    keep_back, send_back, keep_fed, send_fed, middle = [take(2) for _ in range(5)]
    (layer_in, cotangent) = take(2)
    weights_in = take(4)
    kept_in = [take(4) for _ in range(2)]
    tables = [take(4) for _ in range(2)]
    (sub_scale, gain_one, gain_two) = take(3)
    (grad_down, grad_gate, grad_up, grad_out, grad_qkv, layer_out, grad_in, small_out) = take(8)
    reducer_refs = take(10)
    (left_a, left_b, rights, rows_qkv) = take(4)
    weights = take(4)
    kept = [take(4) for _ in range(2)]
    backward_scratch = take(4)
    (grad_sub, grad_lam) = take(2)
    sets = [take(3) for _ in range(2)]
    through = take(2)
    (spare, projected, attended, rows_in, rows_out) = take(5)
    (small, small_near, small_landed) = take(3)
    (near_sems, far_sems, near_credit, far_credit) = take(4)
    (load_sems, small_near_sems, small_send, small_recv) = take(4)
    assert not refs

    me = lax.axis_index("dp")
    tensor = lax.axis_index("tensor")
    core = tensor % 2
    core_peer = tensor + 1 - 2 * core
    far_peer = tensor + 2 - 4 * (tensor // 2)
    line = dp_count // 2
    half = middle[0].shape[0]
    row_count = 2 * half
    head_count, head_width = sub_scale.shape
    out_weight, projections = weights[0], weights[1:]
    inner = out_weight.shape[0]
    tokens = [slice(m * row_count, (m + 1) * row_count) for m in range(2)]

    barrier = pltpu.get_barrier_semaphore()
    for offset in range(1, dp_count):
        pl.semaphore_signal(
            barrier, inc=1, device_id={"dp": lax.rem(me + offset, dp_count)}, device_id_type=MESH
        )
    for peer in (core_peer, far_peer):
        pl.semaphore_signal(barrier, inc=1, device_id={"tensor": peer}, device_id_type=MESH)
    pl.semaphore_wait(barrier, dp_count + 1)

    used = [0]

    def load(source, target):
        copy = pltpu.make_async_copy(source, target, load_sems.at[used[0]])
        used[0] += 1
        copy.start()
        return copy

    def wait_all(copies):
        for copy in copies:
            copy.wait()

    reducer_width = reducer_refs[0].shape[-1]
    plan, sources, left_loads, right_loads = [], {}, {}, {}

    def load_left(sources_of, left):
        return [load(sources_of[m], left.at[:, tokens[m]]) for m in range(2)]

    def load_right(c):
        if c in sources:
            source, first, width = sources[c]
            right_loads[c] = [
                load(source[m].at[:, first : first + width], rights.at[c % 2, tokens[m], :width])
                for m in range(2)
            ]

    def get_left(c, left):
        wait_all(left_loads.pop(c, ()))
        return left

    def get_right(c, first, width):
        if c in sources:
            wait_all(right_loads[c])
            return rights.at[c % 2, :, :width]
        return rows_qkv.at[:, first : first + width]

    def computed(c):
        load_right(c + 2)
        if c == last_two:
            left_loads[first_one] = load_left(one_left, left_b)

    def add_group(left, source, columns, out):
        for first in range(0, columns, reducer_width):
            width = min(reducer_width, columns - first)
            c = len(plan)
            if source is not None:
                sources[c] = (source, first, width)
            plan.append(
                Chunk(
                    functools.partial(get_left, c, left),
                    functools.partial(get_right, c, first, width),
                    functools.partial(computed, c),
                    out,
                    first,
                    width,
                )
            )

    add_group(left_a, hidden, hidden[0].shape[1], grad_down)
    first_two = len(plan)
    add_group(left_b, gate_pre, gate_pre[0].shape[1], grad_gate)
    add_group(left_b, up_pre, up_pre[0].shape[1], grad_up)
    last_two = len(plan) - 1
    add_group(left_a, heads, inner, grad_out)
    first_one = len(plan)
    add_group(left_b, None, 3 * inner, grad_qkv)

    left_loads[0] = load_left(cot_left, left_a)
    load_right(0)
    load_right(1)
    sums = [
        TensorSum(
            3, *sets[m], near_sems.at[m], far_sems.at[m], near_credit.at[m], far_credit.at[m]
        )
        for m in range(2)
    ]
    own_loads = {}
    for m in range(2):
        own_loads[m] = load(keep_back[m], sets[m][0])
        sums[m].near_start(send_back[m])
    left_loads[first_two] = load_left(two_left, left_b)
    weight_loads = [load(*pair) for pair in zip(weights_in, weights)]
    kept_loads = [[load(*pair) for pair in zip(kept_in[m], kept[m])] for m in range(2)]
    spare_queue = [middle[0], middle[1], middle[0], middle[1]]
    rows_queue = [cotangent.at[0], cotangent.at[1]]
    rows_queue += [layer_in.at[0], cotangent.at[0], layer_in.at[1], cotangent.at[1]]
    queued = {}

    def next_spare():
        queued["spare"] = load(spare_queue.pop(0), spare) if spare_queue else None

    def next_rows():
        queued["rows"] = load(rows_queue.pop(0), rows_in) if rows_queue else None

    next_spare()
    next_rows()
    out_loads = []
    small[...] = jnp.zeros_like(small)

    def mine(rows):
        return pl.ds(pl.multiple_of(core * half + rows.start, row_group), row_group)

    def others(rows):
        return pl.ds(pl.multiple_of((1 - core) * half + rows.start, row_group), row_group)

    def exchange(m):
        if m in own_loads:
            own_loads.pop(m).wait()
        sums[m].far_start()

    def norm_two(m):
        own, near, far = sets[m]
        queued["spare"].wait()
        sums[m].far_wait()

        def body(rows):
            grads = own[rows, :] + far[rows, :]
            values = spare[rows, :]
            root = root_of(values)
            small[1:2, :] += jnp.sum(grads * values * root, axis=0, keepdims=True)
            through[m][rows, :] = rms_back(grads * gain_two[...], values, root)

        for_rows(half, body)
        sums[m].far_free()
        sums[m].near_start(through[m])
        next_spare()

    def attend(m):
        near = sets[m][1]
        queued["rows"].wait()
        sums[m].near_wait()

        def body(rows):
            attended[mine(rows), :] = (
                rows_in[mine(rows), :].astype(jnp.float32) + through[m][rows, :]
            ).astype(jnp.bfloat16)
            attended[others(rows), :] = (
                rows_in[others(rows), :].astype(jnp.float32) + near[rows, :]
            ).astype(jnp.bfloat16)

        for_rows(half, body)
        sums[m].near_free()
        next_rows()

        def flip_block(i, carry):
            at = pl.ds(pl.multiple_of(i * 128, 128), 128)
            left_a[at, tokens[m]] = attended[:, at].T
            return carry

        lax.fori_loop(0, attended.shape[1] // 128, flip_block, 0)
        if m == 0:
            wait_all(weight_loads)
        wait_all(kept_loads[m])
        backward_kernel(
            lam, attended, out_weight, *kept[m], *tables[m], sub_scale,
            rows_qkv.at[tokens[m], :], grad_sub, grad_lam, *backward_scratch,
        )
        for head in range(head_count):
            at = slice(head * head_width, (head + 1) * head_width)
            small[2:3, at] += grad_sub[head : head + 1, :]
            small[3:4, at] += grad_lam[head : head + 1, :]

    def project(m):
        def part(which, target):
            rows = pl.ds(pl.multiple_of(m * row_count + which * half, half), half)

            def block(i, carry):
                at = pl.ds(pl.multiple_of(i * 512, 512), 512)
                total = 0.0
                for p in range(3):
                    grads = rows_qkv[rows, p * inner : (p + 1) * inner]
                    total = total + dot_t(grads, projections[p][at, :])
                target[:, at] = total
                return carry

            lax.fori_loop(0, target.shape[1] // 512, block, 0)

        part(1 - core, projected)
        sums[m].near_start(projected)
        part(core, sets[m][0])

    def norm_one(m):
        own, near, far = sets[m]
        queued["rows"].wait()
        sums[m].far_wait()

        def body(rows):
            grads = own[rows, :] + far[rows, :]
            values = rows_in[mine(rows), :].astype(jnp.float32)
            root = root_of(values)
            small[0:1, :] += jnp.sum(grads * values * root, axis=0, keepdims=True)
            through[m][rows, :] += rms_back(grads * gain_one[...], values, root)

        for_rows(half, body)
        sums[m].far_free()
        sums[m].near_start(through[m])
        next_rows()
        own_loads[m] = load(keep_fed[m], own)

    def store_rows(target):
        out_loads.append(load(rows_out, target))

    def finish_in(m):
        near = sets[m][1]
        queued["rows"].wait()
        sums[m].near_wait()
        wait_all(out_loads)
        out_loads.clear()

        def body(rows):
            rows_out[mine(rows), :] = (
                rows_in[mine(rows), :].astype(jnp.float32) + through[m][rows, :]
            ).astype(jnp.bfloat16)
            rows_out[others(rows), :] = (
                rows_in[others(rows), :].astype(jnp.float32) + near[rows, :]
            ).astype(jnp.bfloat16)

        for_rows(half, body)
        sums[m].near_free()
        next_rows()
        store_rows(grad_in.at[m])
        sums[m].near_start(send_fed[m])

    def add_fed(m):
        own, near, far = sets[m]
        queued["spare"].wait()
        sums[m].far_wait()

        def body(rows):
            own[rows, :] = spare[rows, :] + (own[rows, :] + far[rows, :])

        for_rows(half, body)
        sums[m].far_free()
        sums[m].near_start(own)
        next_spare()

    def finish_out(m):
        own, near = sets[m][:2]
        sums[m].near_wait()
        wait_all(out_loads)
        out_loads.clear()

        def body(rows):
            rows_out[mine(rows), :] = own[rows, :].astype(jnp.bfloat16)
            rows_out[others(rows), :] = near[rows, :].astype(jnp.bfloat16)

        for_rows(half, body)
        sums[m].near_free()
        store_rows(layer_out.at[m])

    small_core = pltpu.make_async_remote_copy(
        src_ref=small, dst_ref=small_near, send_sem=small_near_sems.at[0],
        recv_sem=small_near_sems.at[1], device_id={"tensor": core_peer}, device_id_type=MESH,
    )

    def small_copy(offset):
        return pltpu.make_async_remote_copy(
            src_ref=small, dst_ref=small_landed.at[offset - 1], send_sem=small_send.at[offset - 1],
            recv_sem=small_recv.at[offset - 1],
            device_id={"dp": lax.rem(me + offset, dp_count)}, device_id_type=MESH,
        )

    def small_spread():
        small_core.wait()
        small[0:2, :] += small_near[0:2, :]
        for offset in range(1, dp_count):
            small_copy(offset).start()

    def small_finish():
        for offset in range(1, dp_count):
            small_copy(offset).wait()
        total = small[...]
        for offset in range(1, dp_count):
            total = total + small_landed[offset - 1]
        small_near[...] = total
        out_loads.append(load(small_near, small_out))

    order = {
        0: [lambda: exchange(0)],
        2: [lambda: norm_two(0), lambda: exchange(1)],
        3: [lambda: attend(0), lambda: project(0)],
        4: [lambda: norm_two(1), lambda: exchange(0)],
        5: [lambda: attend(1), lambda: project(1)],
        6: [lambda: norm_one(0), lambda: exchange(1)],
        7: [lambda: finish_in(0)],
        8: [lambda: norm_one(1), lambda: exchange(0), small_core.start],
        9: [lambda: finish_in(1), small_spread],
        10: [lambda: add_fed(0), lambda: exchange(1), small_finish],
        11: [lambda: finish_out(0)],
        12: [lambda: add_fed(1)],
        13: [lambda: finish_out(1)],
    }
    stretch = 256 // reducer_width
    tasks = {slot * stretch: items for slot, items in order.items()}
    Reducer(plan, line, reducer_refs).run(tasks)
    wait_all(out_loads)


def back_call(dp_count, lam, arrays, blocks, shapes):
    depth, row_count, inner, hidden_count, head_count, head_width = shapes
    line = dp_count // 2
    rows = depth // dp_count
    half = row_count // 2
    width = 256 if line <= 4 else 128
    ring = line + 4
    wide = (line, rows, width)
    bf16, f32 = jnp.bfloat16, jnp.float32
    dma, regular = pltpu.SemaphoreType.DMA, pltpu.SemaphoreType.REGULAR
    wide_half = pltpu.VMEM((half, depth), f32)
    wide_rows = pltpu.VMEM((row_count, depth), bf16)
    narrow = pltpu.VMEM((row_count, inner), bf16)
    narrow_f32 = pltpu.VMEM((row_count, inner), f32)
    small = pltpu.VMEM((8, depth), f32)
    grad = lambda columns: jax.ShapeDtypeStruct((rows, columns), f32)
    rows_shape = jax.ShapeDtypeStruct((2, row_count, depth), bf16)
    flops = 2 * 2 * row_count * depth * (3 * hidden_count + 8 * inner)
    return pl.pallas_call(
        functools.partial(back_kernel, dp_count),
        out_shape=[grad(hidden_count)] * 3
        + [grad(inner), grad(3 * inner), rows_shape, rows_shape]
        + [jax.ShapeDtypeStruct((8, depth), f32)],
        in_specs=[pl.BlockSpec(memory_space=pltpu.SMEM)]
        + [pl.BlockSpec(memory_space=pl.ANY)] * len(arrays)
        + in_vmem(len(blocks)),
        out_specs=[pl.BlockSpec(memory_space=pl.ANY)] * 8,
        scratch_shapes=[
            pltpu.VMEM((send_slots,) + wide, f32),
            pltpu.VMEM((held_slots,) + wide, f32),
            pltpu.VMEM((ring,) + wide, f32),
            pltpu.VMEM((2, line - 1, 2, rows, width), f32),
            dma((send_slots,)),
            dma((held_slots,)),
            dma((2, line - 1, 2)),
            dma((2, line - 1, 2)),
            regular((2, line - 1)),
            dma((ring,)),
            pltpu.VMEM((depth, 2 * row_count), bf16),
            pltpu.VMEM((depth, 2 * row_count), bf16),
            pltpu.VMEM((2, 2 * row_count, width), bf16),
            pltpu.VMEM((2 * row_count, 3 * inner), bf16),
            pltpu.VMEM((inner, depth), bf16),
        ]
        + [pltpu.VMEM((depth, inner), bf16)] * 3
        + [narrow, narrow, narrow, narrow_f32] * 2
        + [narrow_f32, narrow, narrow_f32, narrow_f32]
        + [pltpu.VMEM((head_count, head_width), f32)] * 2
        + [wide_half] * 10
        + [wide_rows] * 3
        + [
            small,
            small,
            pltpu.VMEM((dp_count - 1, 8, depth), f32),
            dma((2, 2)),
            dma((2, 2)),
            regular((2,)),
            regular((2,)),
            dma((128,)),
            dma((2,)),
            dma((dp_count - 1,)),
            dma((dp_count - 1,)),
        ],
        compiler_params=pltpu.CompilerParams(
            collective_id=0, has_side_effects=True, vmem_limit_bytes=60 * 1024 * 1024
        ),
        cost_estimate=pl.CostEstimate(flops=flops, bytes_accessed=64 << 20, transcendentals=0),
    )(lam, *arrays, *blocks)


def attention_forward(row_in, tables, lam, sub_scale, norm1_gain, projections):
    row_count, depth = row_in.shape
    inner = projections[0].shape[1]
    narrow = jax.ShapeDtypeStruct((row_count, inner), jnp.bfloat16)
    return pl.pallas_call(
        forward_kernel,
        out_shape=[
            jax.ShapeDtypeStruct((row_count, depth), jnp.bfloat16),
            narrow,
            narrow,
            narrow,
            jax.ShapeDtypeStruct((row_count, inner), jnp.float32),
            narrow,
        ],
        in_specs=[pl.BlockSpec(memory_space=pltpu.SMEM)] + in_vmem(10),
        out_specs=in_vmem(6),
        compiler_params=pltpu.CompilerParams(vmem_limit_bytes=32 * 1024 * 1024),
        cost_estimate=pl.CostEstimate(
            flops=12 * row_count * depth * inner, bytes_accessed=8 << 20, transcendentals=0
        ),
    )(lam, row_in, norm1_gain[None, :], *projections, *tables, sub_scale)


def feed_forward(normed_two, cot_rows, gate_weight, up_weight, down_weight):
    half = normed_two.shape[0] // 2
    gate_pre = f32_dot(normed_two, gate_weight)
    upward = f32_dot(normed_two, up_weight)
    sigmoid_gate = jax.nn.sigmoid(gate_pre)
    hidden = (gate_pre * sigmoid_gate * upward).astype(jnp.bfloat16)
    grad_hidden = dot_t(cot_rows, down_weight)
    grad_gate_pre = (
        grad_hidden * upward * sigmoid_gate * (1.0 + gate_pre * (1.0 - sigmoid_gate))
    ).astype(jnp.bfloat16)
    grad_up_pre = (grad_hidden * gate_pre * sigmoid_gate).astype(jnp.bfloat16)

    def back(at):
        return dot_t(grad_gate_pre[at], gate_weight) + dot_t(grad_up_pre[at], up_weight)

    send_back = back(slice(half, None))
    keep_back = back(slice(0, half))
    send_fed = f32_dot(hidden[half:], down_weight)
    keep_fed = f32_dot(hidden[:half], down_weight)
    return (keep_back, send_back), (keep_fed, send_fed), hidden, grad_gate_pre, grad_up_pre


def on_device(
    layer_in,
    short_lengths,
    long_lengths,
    norm1_gain,
    query_weight,
    key_weight,
    value_weight,
    lambda_param,
    sub_gain,
    out_weight,
    norm2_gain,
    gate_weight,
    up_weight,
    down_weight,
    out_cotangent,
):
    dp_count = lax.axis_size("dp")
    core = lax.axis_index("tensor") % 2
    head_count, lambda_width = lambda_param.shape
    doc_lengths = (short_lengths[0], long_lengths[0])
    map_width = lambda_width // 4
    projections = (query_weight, key_weight, value_weight)
    lambda_parts = lambda_param.reshape(head_count, 4, map_width)
    first_exp = jnp.exp(jnp.sum(lambda_parts[:, 0] * lambda_parts[:, 1], axis=-1))
    second_exp = jnp.exp(jnp.sum(lambda_parts[:, 2] * lambda_parts[:, 3], axis=-1))
    lam = first_exp - second_exp + lambda_base
    sub_scale = sub_gain * (1.0 - lambda_base)
    tables = []
    for m in range(2):
        position, segment = doc_tables(doc_lengths[m], layer_in.shape[1])
        tables.append(
            rotary_tables(position, map_width) + (segment[:, None], segment[None, :])
        )
    cots = [mine_first(out_cotangent[m], core) for m in range(2)]
    inputs = [half_rows(layer_in[m], core).astype(jnp.float32) for m in range(2)]
    front = [
        attention_forward(layer_in[m], tables[m], lam, sub_scale, norm1_gain, projections)
        for m in range(2)
    ]
    heads = [front[m][5] for m in range(2)]
    middle, normed_two, ffn = [], [], []
    for m in range(2):
        keep = f32_dot(half_rows(heads[m], core), out_weight)
        send = f32_dot(half_rows(heads[m], 1 - core), out_weight)
        middle.append(inputs[m] + tensor_sum(keep, send))
        scaled = middle[m] * root_of(middle[m])
        normed_two.append((with_other(scaled) * norm2_gain).astype(jnp.bfloat16))
        ffn.append(feed_forward(normed_two[m], cots[m], gate_weight, up_weight, down_weight))
    turned = lambda parts: [part.T for part in parts]
    arrays = turned(cots) + turned(normed_two) + turned([front[m][0] for m in range(2)])
    for index in (2, 3, 4):
        arrays += [ffn[m][index] for m in range(2)]
    arrays += heads
    for group, part in ((0, 0), (0, 1), (1, 0), (1, 1)):
        arrays += [ffn[m][group][part] for m in range(2)]
    arrays += middle + [layer_in, out_cotangent, out_weight, *projections]
    for m in range(2):
        arrays += front[m][1:5]
    blocks = [*tables[0], *tables[1], sub_scale, norm1_gain[None, :], norm2_gain[None, :]]
    depth, inner = query_weight.shape
    shapes = (
        depth, layer_in.shape[1], inner, gate_weight.shape[1], head_count, sub_gain.shape[1],
    )
    grad_down, grad_gate, grad_up, grad_out, grad_qkv, layer_out, grad_in, small = back_call(
        dp_count, lam, arrays, blocks, shapes
    )
    grad_query, grad_key, grad_value = jnp.split(grad_qkv, 3, axis=1)
    per_head = lambda row: row[:inner].reshape(head_count, -1)
    grad_lam = per_head(small[3])[:, :1]
    first_scale = grad_lam * first_exp[:, None]
    second_scale = grad_lam * second_exp[:, None]
    lambda_grad = jnp.concatenate(
        [
            first_scale * lambda_parts[:, 1],
            first_scale * lambda_parts[:, 0],
            -second_scale * lambda_parts[:, 3],
            -second_scale * lambda_parts[:, 2],
        ],
        axis=1,
    )
    index = lax.axis_index("dp")

    def block_of(values):
        size = values.shape[-1] // dp_count
        return lax.dynamic_slice_in_dim(values, index * size, size, values.ndim - 1)

    return (
        layer_out,
        grad_in,
        block_of(small[0]),
        grad_query,
        grad_key,
        grad_value,
        block_of(lambda_grad),
        block_of(per_head(small[2])),
        grad_out.T,
        block_of(small[1]),
        grad_gate,
        grad_up,
        grad_down.T,
    )


def solution(mesh):
    return jax.shard_map(
        on_device,
        mesh=mesh,
        in_specs=(
            P(None, "dp", None),
            P("dp", None),
            P("dp", None),
            P(),
            P(None, "tensor"),
            P(None, "tensor"),
            P(None, "tensor"),
            P("tensor", None),
            P("tensor", None),
            P("tensor", None),
            P(),
            P(None, "tensor"),
            P(None, "tensor"),
            P("tensor", None),
            P(None, "dp", None),
        ),
        out_specs=(
            P(None, "dp", None),
            P(None, "dp", None),
            P("dp"),
            P("dp", "tensor"),
            P("dp", "tensor"),
            P("dp", "tensor"),
            P("tensor", "dp"),
            P("tensor", "dp"),
            P("tensor", "dp"),
            P("dp"),
            P("dp", "tensor"),
            P("dp", "tensor"),
            P("tensor", "dp"),
        ),
        check_vma=False,
    )
```

time: 786 us -> 573 us (0.73)
  other arithmetic: 80.8 us -> 21.7 us
  Pallas kernels: 418 us -> 367 us
  waiting for transfers between devices: 109 us -> 63.1 us
  starting transfers between devices: 28 us -> 4.53 us
  matrix products: 59.1 us -> 42.5 us
  local copies, waits for them, and re-layouts: 78.1 us -> 61.6 us
    pallas_call x4 -> x1, Pallas kernels: 400 us -> 349 us  [back_call(): pl.pallas_call(functools.partial(back_kernel, dp_count), out_shape=[grad(...]
    ppermute x26 -> x6, waiting for transfers between devices: 105 us -> 63.1 us  [flip(): return lax.ppermute(values, axis_name, [(i, i ^ bit) for i in range(size)])]
    add x19 -> x1, other arithmetic: 20.9 us -> 0.01 us  [on_device(): lam = first_exp - second_exp + lambda_base]
    transpose x6 -> x2, local copies, waits for them, and re-layouts: 19.4 us -> 3.18 us  [on_device(): turned = lambda parts: [part.T for part in parts]]
    ppermute x6 -> x0, starting transfers between devices: 13 us -> none  [the longest x3 10.1 us: line_scatter(): lax.ppermute(up_out, 'dp', [(2 * z + x, 2 * z + 2 + x) for z in range(ste...]
    dot_general x22 -> x10, matrix products: 29.2 us -> 16.6 us  [dot_t(): lax.dot_general(left, right, (((1,), (1,)), ((), ())), preferred_element_...]
    convert_element_type x9 -> x1, other arithmetic: 16.2 us -> 3.77 us  [on_device(): normed_two.append((with_other(scaled) * norm2_gain).astype(jnp.bfloat16))]
    ppermute x26 -> x6, starting transfers between devices: 15 us -> 4.53 us  [flip(): return lax.ppermute(values, axis_name, [(i, i ^ bit) for i in range(size)])]
  transfers between devices with their start and end apart: 32 -> 6, of which waited for: 8 -> 2; matrix products, arithmetic and copies ran while one was open for 19% -> 7% of each run, Pallas kernels for 53% -> 2%
where the time goes in v4:
time: 573 us; the launch traced here: 563 us
  Pallas kernels  367 us (64%)
  waiting for transfers between devices  63.1 us (11%)
  local copies, waits for them, and re-layouts  61.6 us (11%)
  matrix products  42.5 us (7%)
  other arithmetic  21.7 us (4%)
    pallas_call x1, Pallas kernels, back_call(): pl.pallas_call(functools.partial(back_kernel, dp_count), out_shape=[grad(...  349 us
    ppermute x6, waiting for transfers between devices, flip(): return lax.ppermute(values, axis_name, [(i, i ^ bit) for i in range(size)])  63.1 us
    unnamed x167, local copies, waits for them, and re-layouts  28.3 us
    dot_general x12, matrix products, f32_dot(): return jnp.dot(left, right, preferred_element_type=jnp.float32)  25.8 us
    pallas_call x2, Pallas kernels, attention_forward(): pl.pallas_call(forward_kernel, out_shape=[jax.ShapeDtypeStruct((row_count...  17.9 us
    dot_general x10, matrix products, dot_t(): lax.dot_general(left, right, (((1,), (1,)), ((), ())), preferred_element_...  16.6 us
  transfers between devices with their start and end apart: 6, of which 2 were waited for; matrix products, arithmetic and copies ran while one was open for 7% of the time, Pallas kernels for 2%

profile of v4, /device:TPU:0, one launch (start us, length us, event | category | flops | bytes accessed | tf_op | source)
XLA Modules:
  0.0 562.6 jit_solution(5804178358577334737)
XLA Ops:
  4.9 4.9 fusion.53
  11.4 2.8 fusion.33
  18.7 8.8 %shard_map.246 = (bf16[512,1536]{1,0:T(8,128)(2,1)S(1)}, bf16[512,384]{1,0:T(8,128)(2,1)S(1)}, bf16[512,384]{1,0:T(8,128)(2,1)S(1)}, bf16[512,384]{1,0:T(8,128)(...) custom-call(f32[3]{0:T(128)S(1)} %subtract_add_fusion.lam.refs_0_, bf16[512,1536]{1,0:T(8,128)(2,1)S(1)} %copy-done.3, ...), custom_call_target="tpu_custom_call" | custom-call | flops 3623878656 | bytes 8388608 | tf_op jit(solution)/shard_map/pallas_call | solution.py:881
  35.0 2.4 pad_maximum_fusion.6
  44.5 9.1 %shard_map.247 = (bf16[512,1536]{1,0:T(8,128)(2,1)S(1)}, bf16[512,384]{1,0:T(8,128)(2,1)S(1)}, bf16[512,384]{1,0:T(8,128)(2,1)S(1)}, bf16[512,384]{1,0:T(8,128)(...) custom-call(f32[3]{0:T(128)S(1)} %copy-done.27, bf16[512,1536]{1,0:T(8,128)(2,1)S(1)} %copy-done.2, ...), custom_call_target="tpu_custom_call" | custom-call | flops 3623878656 | bytes 8388608 | tf_op jit(solution)/shard_map/pallas_call | solution.py:881
  57.4 2.5 convolution_add_fusion.5
  59.9 3.0 collective-permute-start.1
  66.0 32.1 %collective-permute-done.1 = f32[256,1536]{1,0:T(8,128)S(1)} collective-permute-done((f32[256,1536]{1,0:T(8,128)S(1)}, f32[256,1536]{1,0:T(8,128)S(1)}, u32[]{:S(2)}, u32[]{:S(2)}) %collective-permute-start.1) | collective-permute-done | bytes 1572896 | tf_op jit(solution)/shard_map/ppermute | solution.py:99
  100.2 31.0 %collective-permute-done.4 = f32[256,1536]{1,0:T(8,128)S(1)} collective-permute-done((f32[256,1536]{1,0:T(8,128)S(1)}, f32[256,1536]{1,0:T(8,128)S(1)}, u32[]{:S(2)}, u32[]{:S(2)}) %collective-permute-start.4) | collective-permute-done | bytes 1572896 | tf_op jit(solution)/shard_map/ppermute | solution.py:99
  134.9 2.3 copy.74
  137.2 2.3 copy.75
  139.5 2.3 copy.72
  141.8 2.3 copy.73
  144.1 2.6 copy.80
  146.6 2.7 copy.81
  149.9 2.8 fusion.3.refs_2_
  158.9 3.8 fusion.1
  164.5 2.8 multiply_convert_fusion
  171.3 2.9 multiply_convert_fusion.1
  178.5 2.2 fusion.6.refs_22_
  185.1 2.2 convolution_add_fusion.refs_18_
  191.6 2.2 convolution_add_fusion.3.refs_15_
  197.0 349.4 %shard_map.248 = (f32[192,1024]{1,0:T(8,128)}, f32[192,1024]{1,0:T(8,128)}, f32[192,1024]{1,0:T(8,128)}, f32[192,384]{1,0:T(8,128)}, f32[192,1152]{1,0:T(8,128)}...) custom-call(f32[3]{0:T(128)} %copy-done.26, bf16[1536,512]{1,0:T(8,128)(2,1)} %fusion.5.refs_1_, ...), custom_call_target="tpu_custom_call" | custom-call | flops 19327352832 | bytes 67108864 | tf_op jit(solution)/shard_map/pallas_call | solution.py:825
  553.1 3.9 copy.119
  (229 shorter events, 77.6 us)
Async XLA Ops:
  0.6 163.9 %copy-start = (bf16[1536,1024]{1,0:T(8,128)(2,1)S(1)}, bf16[1536,1024]{1,0:T(8,128)(2,1)}, u32[]{:S(2)}) copy-start(bf16[1536,1024]{1,0:T(8,128)(2,1)} %param.26) | copy-start | bytes 9437188
  3.2 34.2 %copy-start.15 = (s32[512]{0:T(512)}, s32[512]{0:T(512)S(1)}, u32[]{:S(2)}) copy-start(s32[512]{0:T(512)S(1)} %get-tuple-element.55) | copy-start | bytes 6148
  10.6 26.8 %copy-start.17 = (f32[1,1536]{1,0:T(1,128)}, f32[1,1536]{1,0:T(1,128)S(1)}, u32[]{:S(2)}) copy-start(f32[1,1536]{1,0:T(1,128)S(1)} %broadcast_in_dim.12.gain.refs_48_) | copy-start | bytes 18436
  11.4 16.1 %copy-start.26 = (f32[3]{0:T(128)}, f32[3]{0:T(128)S(1)}, u32[]{:S(2)}) copy-start(f32[3]{0:T(128)S(1)} %subtract_add_fusion.lam.refs_0_) | copy-start | bytes 40
  18.7 13.3 %copy-start.38 = (bf16[384,1536]{1,0:T(8,128)(2,1)S(1)}, bf16[384,1536]{1,0:T(8,128)(2,1)}, u32[]{:S(2)}) copy-start(bf16[384,1536]{1,0:T(8,128)(2,1)} %refs_27_.1) | copy-start | bytes 3538948
  32.0 25.4 %copy-start.6 = (bf16[512,384]{1,0:T(8,128)(2,1)}, bf16[512,384]{1,0:T(8,128)(2,1)S(1)}, u32[]{:S(2)}) copy-start(bf16[512,384]{1,0:T(8,128)(2,1)S(1)} %get-tuple-element.33.refs_13_) | copy-start | bytes 1179652
  33.7 23.7 %collective-permute-start = (f32[256,1536]{1,0:T(8,128)}, f32[256,1536]{1,0:T(8,128)}, u32[]{:S(2)}, u32[]{:S(2)}) collective-permute-start(f32[256,1536]{1,0:T(8,128)} %fusion.29), channel_id=1, source_target_pairs={{0,1},{1,0},{2,3},{3,2},{4,5},{5,4},{6,7},{7,6},{8,9},{9,8},{10,11... | collective-permute-start | bytes 4718600 | tf_op jit(solution)/shard_map/ppermute | solution.py:99
  37.4 16.1 %copy-start.11 = (f32[512,128]{1,0:T(8,128)}, f32[512,128]{1,0:T(8,128)S(1)}, u32[]{:S(2)}) copy-start(f32[512,128]{1,0:T(8,128)S(1)} %get-tuple-element.111.cosine.refs_43_) | copy-start | bytes 786436
  37.4 16.1 %copy-start.12 = (f32[512,128]{1,0:T(8,128)}, f32[512,128]{1,0:T(8,128)S(1)}, u32[]{:S(2)}) copy-start(f32[512,128]{1,0:T(8,128)S(1)} %get-tuple-element.112.sine.refs_44_) | copy-start | bytes 786436
  57.2 5.6 %collective-permute-start.3 = (f32[256,1536]{1,0:T(8,128)}, f32[256,1536]{1,0:T(8,128)}, u32[]{:S(2)}, u32[]{:S(2)}) collective-permute-start(f32[256,1536]{1,0:T(8,128)} %fusion.26), channel_id=1, source_target_pairs={{0,1},{1,0},{2,3},{3,2},{4,5},{5,4},{6,7},{7,6},{8,9},{9,8},{10,11... | collective-permute-start | bytes 4718600 | tf_op jit(solution)/shard_map/ppermute | solution.py:99
  59.9 38.2 %collective-permute-start.1 = (f32[256,1536]{1,0:T(8,128)S(1)}, f32[256,1536]{1,0:T(8,128)S(1)}, u32[]{:S(2)}, u32[]{:S(2)}) collective-permute-start(f32[256,1536]{1,0:T(8,128)S(1)} %convolution_add_fusion.5), channel_id=1, source_target_pairs={{0,2},{1,3},{2,0},{3,1},{4,6},{5,7},{6,4},{7,5},{8,10},{9,11},{10,... | collective-permute-start | bytes 4718600 | tf_op jit(solution)/shard_map/ppermute | solution.py:99
  64.9 33.2 %copy-start.48 = (bf16[1,512,1536]{2,1,0:T(8,128)(2,1)S(1)}, bf16[1,512,1536]{2,1,0:T(8,128)(2,1)}, u32[]{:S(2)}) copy-start(bf16[1,512,1536]{2,1,0:T(8,128)(2,1)} %get-tuple-element.72) | copy-start | bytes 4718596
  64.9 66.3 %collective-permute-start.4 = (f32[256,1536]{1,0:T(8,128)S(1)}, f32[256,1536]{1,0:T(8,128)S(1)}, u32[]{:S(2)}, u32[]{:S(2)}) collective-permute-start(f32[256,1536]{1,0:T(8,128)S(1)} %convolution_add_fusion.4), channel_id=1, source_target_pairs={{0,2},{1,3},{2,0},{3,1},{4,6},{5,7},{6,4},{7,5},{8,10},{9,11},{10,... | collective-permute-start | bytes 4718600 | tf_op jit(solution)/shard_map/ppermute | solution.py:99
  98.4 32.8 %copy-start.47 = (bf16[1,512,1536]{2,1,0:T(8,128)(2,1)S(1)}, bf16[1,512,1536]{2,1,0:T(8,128)(2,1)}, u32[]{:S(2)}) copy-start(bf16[1,512,1536]{2,1,0:T(8,128)(2,1)} %get-tuple-element.69) | copy-start | bytes 4718596
  100.2 58.7 %collective-permute-start.2 = (f32[256,1536]{1,0:T(8,128)}, f32[256,1536]{1,0:T(8,128)}, u32[]{:S(2)}, u32[]{:S(2)}) collective-permute-start(f32[256,1536]{1,0:T(8,128)} %broadcast_multiply_fusion.1), channel_id=1, source_target_pairs={{0,1},{1,0},{2,3},{3,2},{4,5},{5,4},{6,7},{7,6},{8,9},{9,8},{10,11... | collective-permute-start | bytes 4718600 | tf_op jit(solution)/shard_map/ppermute | solution.py:99
  133.2 25.7 %collective-permute-start.5 = (f32[256,1536]{1,0:T(8,128)}, f32[256,1536]{1,0:T(8,128)}, u32[]{:S(2)}, u32[]{:S(2)}) collective-permute-start(f32[256,1536]{1,0:T(8,128)} %broadcast_multiply_fusion), channel_id=1, source_target_pairs={{0,1},{1,0},{2,3},{3,2},{4,5},{5,4},{6,7},{7,6},{8,9},{9,8},{10,11... | collective-permute-start | bytes 4718600 | tf_op jit(solution)/shard_map/ppermute | solution.py:99
  167.3 20.0 %copy-start.59 = (bf16[512,1024]{1,0:T(8,128)(2,1)}, bf16[512,1024]{1,0:T(8,128)(2,1)S(1)}, u32[]{:S(2)}) copy-start(bf16[512,1024]{1,0:T(8,128)(2,1)S(1)} %get-tuple-element.63.refs_12_) | copy-start | bytes 3145732
  174.2 17.4 %copy-start.60 = (bf16[512,1024]{1,0:T(8,128)(2,1)}, bf16[512,1024]{1,0:T(8,128)(2,1)S(1)}, u32[]{:S(2)}) copy-start(bf16[512,1024]{1,0:T(8,128)(2,1)S(1)} %get-tuple-element.66.refs_11_) | copy-start | bytes 3145732
  197.0 351.3 %copy-start.76 = (f32[3]{0:T(128)S(1)}, f32[3]{0:T(128)}, u32[]{:S(2)}) copy-start(f32[3]{0:T(128)} %copy-done.75) | copy-start | bytes 40
  197.0 351.3 %copy-start.78 = (f32[3]{0:T(128)S(1)}, f32[3]{0:T(128)}, u32[]{:S(2)}) copy-start(f32[3]{0:T(128)} %copy-done.77) | copy-start | bytes 40
  197.0 351.3 %copy-start.71 = (f32[3,1,64]{2,1,0:T(1,128)S(1)}, f32[3,1,64]{2,1,0:T(1,128)}, u32[]{:S(2)}) copy-start(f32[3,1,64]{2,1,0:T(1,128)} %copy-done.70) | copy-start | bytes 2308
  197.0 351.3 %copy-start.73 = (f32[3,1,64]{2,1,0:T(1,128)S(1)}, f32[3,1,64]{2,1,0:T(1,128)}, u32[]{:S(2)}) copy-start(f32[3,1,64]{2,1,0:T(1,128)} %copy-done.72) | copy-start | bytes 2308
  197.0 351.4 %copy-start.67 = (f32[3,1,64]{2,1,0:T(1,128)S(1)}, f32[3,1,64]{2,1,0:T(1,128)}, u32[]{:S(2)}) copy-start(f32[3,1,64]{2,1,0:T(1,128)} %copy-done.66) | copy-start | bytes 2308
  197.0 351.4 %copy-start.69 = (f32[3,1,64]{2,1,0:T(1,128)S(1)}, f32[3,1,64]{2,1,0:T(1,128)}, u32[]{:S(2)}) copy-start(f32[3,1,64]{2,1,0:T(1,128)} %copy-done.68) | copy-start | bytes 2308
  (62 other events, 238.9 us)

commit v5 on v4

--- a/solution.py
+++ b/solution.py
@@ -92,29 +92,6 @@
     return lax.dot_general(
         left, right, (((0,), (0,)), ((), ())), preferred_element_type=jnp.float32
     )
-
-
-def flip(values, axis_name, bit):
-    size = lax.axis_size(axis_name)
-    return lax.ppermute(values, axis_name, [(i, i ^ bit) for i in range(size)])
-
-
-def half_rows(values, which):
-    count = values.shape[0] // 2
-    return lax.dynamic_slice_in_dim(values, which * count, count, 0)
-
-
-def mine_first(values, core):
-    return jnp.concatenate([half_rows(values, core), half_rows(values, 1 - core)], axis=0)
-
-
-def tensor_sum(keep, send):
-    half = keep + flip(send, "tensor", 1)
-    return half + flip(half, "tensor", 2)
-
-
-def with_other(mine):
-    return jnp.concatenate([mine, flip(mine, "tensor", 1)], axis=0)
 
 
 def rms_back(incoming, values, inverse_root):
@@ -433,7 +410,7 @@
                 self.near_credit, inc=1, device_id={"tensor": self.core_peer}, device_id_type=MESH
             )
 
-    def far_start(self):
+    def near_add(self):
         self.near_wait()
 
         def add(rows):
@@ -441,6 +418,8 @@
 
         for_rows(self.own.shape[0], add)
         self.near_free()
+
+    def far_go(self):
         if not self.far_first:
             pl.semaphore_wait(self.far_credit, 1)
         self.far_first = False
@@ -463,7 +442,7 @@
     (lam,) = take(1)
     cot_left, two_left, one_left = [take(2) for _ in range(3)]
     hidden, gate_pre, up_pre, heads = [take(2) for _ in range(4)]
-    keep_back, send_back, keep_fed, send_fed, middle = [take(2) for _ in range(5)]
+    part_back, part_fed, middle = [take(2) for _ in range(3)]
     (layer_in, cotangent) = take(2)
     weights_in = take(4)
     kept_in = [take(4) for _ in range(2)]
@@ -495,6 +474,8 @@
     head_count, head_width = sub_scale.shape
     out_weight, projections = weights[0], weights[1:]
     inner = out_weight.shape[0]
+    kept_half = pl.ds(pl.multiple_of(core * half, half), half)
+    sent_half = pl.ds(pl.multiple_of((1 - core) * half, half), half)
     tokens = [slice(m * row_count, (m + 1) * row_count) for m in range(2)]
 
     barrier = pltpu.get_barrier_semaphore()
@@ -584,8 +565,8 @@
     ]
     own_loads = {}
     for m in range(2):
-        own_loads[m] = load(keep_back[m], sets[m][0])
-        sums[m].near_start(send_back[m])
+        own_loads[m] = load(part_back[m].at[kept_half], sets[m][0])
+        sums[m].near_start(part_back[m].at[sent_half])
     left_loads[first_two] = load_left(two_left, left_b)
     weight_loads = [load(*pair) for pair in zip(weights_in, weights)]
     kept_loads = [[load(*pair) for pair in zip(kept_in[m], kept[m])] for m in range(2)]
@@ -614,7 +595,8 @@
     def exchange(m):
         if m in own_loads:
             own_loads.pop(m).wait()
-        sums[m].far_start()
+        sums[m].near_add()
+        sums[m].far_go()
 
     def norm_two(m):
         own, near, far = sets[m]
@@ -703,7 +685,7 @@
         sums[m].far_free()
         sums[m].near_start(through[m])
         next_rows()
-        own_loads[m] = load(keep_fed[m], own)
+        own_loads[m] = load(part_fed[m].at[kept_half], own)
 
     def store_rows(target):
         out_loads.append(load(rows_out, target))
@@ -727,7 +709,7 @@
         sums[m].near_free()
         next_rows()
         store_rows(grad_in.at[m])
-        sums[m].near_start(send_fed[m])
+        sums[m].near_start(part_fed[m].at[sent_half])
 
     def add_fed(m):
         own, near, far = sets[m]
@@ -874,49 +856,225 @@
     )(lam, *arrays, *blocks)
 
 
-def attention_forward(row_in, tables, lam, sub_scale, norm1_gain, projections):
-    row_count, depth = row_in.shape
-    inner = projections[0].shape[1]
-    narrow = jax.ShapeDtypeStruct((row_count, inner), jnp.bfloat16)
+def front_kernel(*refs):
+    refs = list(refs)
+    take = lambda n: [refs.pop(0) for _ in range(n)]
+    (lam,) = take(1)
+    layer_in, cotangent = take(2)
+    weights_in = take(7)
+    tables = [take(4) for _ in range(2)]
+    (sub_scale, gain_one, gain_two) = take(3)
+    outs = [take(14) for _ in range(2)]
+    rows_in, cot_rows = take(2), take(2)
+    (normed_one, normed_two, flipped) = take(3)
+    weights = take(7)
+    kept = [take(5) for _ in range(2)]
+    sets = [take(3) for _ in range(2)]
+    (projected,) = take(1)
+    hidden = [take(3) for _ in range(2)]
+    (back, fed) = take(2)
+    (near_sems, far_sems, near_credit, load_sems) = take(4)
+    assert not refs
+
+    tensor = lax.axis_index("tensor")
+    core = tensor % 2
+    out_weight, gate_weight, up_weight, down_weight = weights[3:]
+    row_count, depth = normed_one.shape
+    half = row_count // 2
+    hidden_count = gate_weight.shape[1]
+    used = [0]
+
+    def load(source, target):
+        copy = pltpu.make_async_copy(source, target, load_sems.at[used[0]])
+        used[0] += 1
+        copy.start()
+        return copy
+
+    def wait_all(copies):
+        for copy in copies:
+            copy.wait()
+        copies.clear()
+
+    rows_loads = [load(layer_in.at[0], rows_in[0])]
+    weight_loads = [load(*pair) for pair in zip(weights_in[:4], weights[:4])]
+    rows_loads.append(load(layer_in.at[1], rows_in[1]))
+    cot_loads = [load(cotangent.at[m], cot_rows[m]) for m in range(2)]
+    wide_loads = [load(*pair) for pair in zip(weights_in[4:], weights[4:])]
+
+    barrier = pltpu.get_barrier_semaphore()
+    for peer in (tensor + 1 - 2 * core, tensor + 2 - 4 * (tensor // 2)):
+        pl.semaphore_signal(barrier, inc=1, device_id={"tensor": peer}, device_id_type=MESH)
+    pl.semaphore_wait(barrier, 2)
+    sums = [
+        TensorSum(1, *sets[m], near_sems.at[m], far_sems.at[m], near_credit.at[m], None)
+        for m in range(2)
+    ]
+    out_loads, flip_loads, wide_outs = [], [], []
+
+    def mine(rows):
+        return pl.ds(pl.multiple_of(core * half + rows.start, row_group), row_group)
+
+    def others(rows):
+        return pl.ds(pl.multiple_of((1 - core) * half + rows.start, row_group), row_group)
+
+    def flip_to(source, target):
+        wait_all(flip_loads)
+
+        def block(i, carry):
+            at = pl.ds(pl.multiple_of(i * 128, 128), 128)
+            flipped[at, :] = source[:, at].T
+            return carry
+
+        lax.fori_loop(0, depth // 128, block, 0)
+        flip_loads.append(load(flipped, target))
+
+    def attend(m):
+        rows_loads[m].wait()
+        if m == 0:
+            wait_all(weight_loads)
+        forward_kernel(
+            lam, rows_in[m], gain_one, *weights[:3], *tables[m], sub_scale, normed_one, *kept[m]
+        )
+        heads = kept[m][4]
+
+        def part(which, target):
+            rows = pl.ds(pl.multiple_of(which * half, half), half)
+
+            def block(i, carry):
+                at = pl.ds(pl.multiple_of(i * 512, 512), 512)
+                target[:, at] = f32_dot(heads[rows, :], out_weight[:, at])
+                return carry
+
+            lax.fori_loop(0, depth // 512, block, 0)
+
+        part(1 - core, projected)
+        sums[m].near_start(projected)
+        part(core, sets[m][0])
+        out_loads.extend(load(*pair) for pair in zip(kept[m], outs[m][3:8]))
+        flip_to(normed_one, outs[m][2])
+        sums[m].near_add()
+
+    def norm_rows(rows, values):
+        return (values * root_of(values) * gain_two[...]).astype(jnp.bfloat16)
+
+    def join(m):
+        own, near, far = sets[m]
+
+        def add(rows):
+            values = rows_in[m][mine(rows), :].astype(jnp.float32)
+            own[rows, :] = values + (own[rows, :] + far[rows, :])
+
+        def norm_mine(rows):
+            normed_two[mine(rows), :] = norm_rows(rows, own[rows, :])
+
+        def norm_others(rows):
+            normed_two[others(rows), :] = norm_rows(rows, near[rows, :])
+
+        for_rows(half, add)
+        sums[m].near_start(own)
+        out_loads.append(load(own, outs[m][8]))
+        for_rows(half, norm_mine)
+        sums[m].near_wait()
+        for_rows(half, norm_others)
+        sums[m].near_free()
+
+    def feed(m):
+        inside, gate_pre, up_pre = hidden[m]
+        if m == 0:
+            wait_all(wide_loads)
+
+        def block(j, carry):
+            at = pl.ds(pl.multiple_of(j * 256, 256), 256)
+            gate = f32_dot(normed_two[...], gate_weight[:, at])
+            upward = f32_dot(normed_two[...], up_weight[:, at])
+            grads = dot_t(cot_rows[m][...], down_weight[at, :])
+            sigmoid = jax.nn.sigmoid(gate)
+            inside[:, at] = (gate * sigmoid * upward).astype(jnp.bfloat16)
+            gate_pre[:, at] = (
+                grads * upward * sigmoid * (1.0 + gate * (1.0 - sigmoid))
+            ).astype(jnp.bfloat16)
+            up_pre[:, at] = (grads * gate * sigmoid).astype(jnp.bfloat16)
+            return carry
+
+        lax.fori_loop(0, hidden_count // 256, block, 0)
+        out_loads.extend(load(*pair) for pair in zip(hidden[m], outs[m][9:12]))
+        wait_all(wide_outs)
+
+        def through(i, carry):
+            at = pl.ds(pl.multiple_of(i * 512, 512), 512)
+            back[:, at] = dot_t(gate_pre[...], gate_weight[at, :]) + dot_t(
+                up_pre[...], up_weight[at, :]
+            )
+            fed[:, at] = f32_dot(inside[...], down_weight[:, at])
+            return carry
+
+        lax.fori_loop(0, depth // 512, through, 0)
+        wide_outs.extend([load(back, outs[m][12]), load(fed, outs[m][13])])
+
+    attend(0)
+    sums[0].far_go()
+    attend(1)
+    for m in range(2):
+        cot_loads[m].wait()
+        flip_to(cot_rows[m], outs[m][0])
+    sums[0].far_wait()
+    sums[1].far_go()
+    join(0)
+    feed(0)
+    flip_to(normed_two, outs[0][1])
+    sums[1].far_wait()
+    join(1)
+    feed(1)
+    flip_to(normed_two, outs[1][1])
+    wait_all(flip_loads)
+    wait_all(wide_outs)
+    wait_all(out_loads)
+
+
+def front_call(lam, arrays, blocks, shapes):
+    depth, row_count, inner, hidden_count = shapes[:4]
+    bf16, f32 = jnp.bfloat16, jnp.float32
+    dma, regular = pltpu.SemaphoreType.DMA, pltpu.SemaphoreType.REGULAR
+    half = row_count // 2
+    out_shape = []
+    for m in range(2):
+        out_shape += [jax.ShapeDtypeStruct((depth, row_count), bf16)] * 3
+        out_shape += [jax.ShapeDtypeStruct((row_count, inner), bf16)] * 3
+        out_shape += [jax.ShapeDtypeStruct((row_count, inner), f32)]
+        out_shape += [jax.ShapeDtypeStruct((row_count, inner), bf16)]
+        out_shape += [jax.ShapeDtypeStruct((half, depth), f32)]
+        out_shape += [jax.ShapeDtypeStruct((row_count, hidden_count), bf16)] * 3
+        out_shape += [jax.ShapeDtypeStruct((row_count, depth), f32)] * 2
+    wide_rows = pltpu.VMEM((row_count, depth), bf16)
+    narrow = pltpu.VMEM((row_count, inner), bf16)
+    wide_half = pltpu.VMEM((half, depth), f32)
     return pl.pallas_call(
-        forward_kernel,
-        out_shape=[
-            jax.ShapeDtypeStruct((row_count, depth), jnp.bfloat16),
-            narrow,
-            narrow,
-            narrow,
-            jax.ShapeDtypeStruct((row_count, inner), jnp.float32),
-            narrow,
-        ],
-        in_specs=[pl.BlockSpec(memory_space=pltpu.SMEM)] + in_vmem(10),
-        out_specs=in_vmem(6),
-        compiler_params=pltpu.CompilerParams(vmem_limit_bytes=32 * 1024 * 1024),
+        front_kernel,
+        out_shape=out_shape,
+        in_specs=[pl.BlockSpec(memory_space=pltpu.SMEM)]
+        + [pl.BlockSpec(memory_space=pl.ANY)] * len(arrays)
+        + in_vmem(len(blocks)),
+        out_specs=[pl.BlockSpec(memory_space=pl.ANY)] * len(out_shape),
+        scratch_shapes=[wide_rows] * 6
+        + [pltpu.VMEM((depth, row_count), bf16)]
+        + [pltpu.VMEM((depth, inner), bf16)] * 3
+        + [pltpu.VMEM((inner, depth), bf16)]
+        + [pltpu.VMEM((depth, hidden_count), bf16)] * 2
+        + [pltpu.VMEM((hidden_count, depth), bf16)]
+        + [narrow, narrow, narrow, pltpu.VMEM((row_count, inner), f32), narrow] * 2
+        + [wide_half] * 7
+        + [pltpu.VMEM((row_count, hidden_count), bf16)] * 6
+        + [pltpu.VMEM((row_count, depth), f32)] * 2
+        + [dma((2, 2)), dma((2, 2)), regular((2,)), dma((64,))],
+        compiler_params=pltpu.CompilerParams(
+            collective_id=1, has_side_effects=True, vmem_limit_bytes=62 * 1024 * 1024
+        ),
         cost_estimate=pl.CostEstimate(
-            flops=12 * row_count * depth * inner, bytes_accessed=8 << 20, transcendentals=0
+            flops=4 * row_count * depth * (6 * hidden_count + 4 * inner),
+            bytes_accessed=64 << 20,
+            transcendentals=0,
         ),
-    )(lam, row_in, norm1_gain[None, :], *projections, *tables, sub_scale)
-
-
-def feed_forward(normed_two, cot_rows, gate_weight, up_weight, down_weight):
-    half = normed_two.shape[0] // 2
-    gate_pre = f32_dot(normed_two, gate_weight)
-    upward = f32_dot(normed_two, up_weight)
-    sigmoid_gate = jax.nn.sigmoid(gate_pre)
-    hidden = (gate_pre * sigmoid_gate * upward).astype(jnp.bfloat16)
-    grad_hidden = dot_t(cot_rows, down_weight)
-    grad_gate_pre = (
-        grad_hidden * upward * sigmoid_gate * (1.0 + gate_pre * (1.0 - sigmoid_gate))
-    ).astype(jnp.bfloat16)
-    grad_up_pre = (grad_hidden * gate_pre * sigmoid_gate).astype(jnp.bfloat16)
-
-    def back(at):
-        return dot_t(grad_gate_pre[at], gate_weight) + dot_t(grad_up_pre[at], up_weight)
-
-    send_back = back(slice(half, None))
-    keep_back = back(slice(0, half))
-    send_fed = f32_dot(hidden[half:], down_weight)
-    keep_fed = f32_dot(hidden[:half], down_weight)
-    return (keep_back, send_back), (keep_fed, send_fed), hidden, grad_gate_pre, grad_up_pre
+    )(lam, *arrays, *blocks)
 
 
 def on_device(
@@ -937,7 +1095,6 @@
     out_cotangent,
 ):
     dp_count = lax.axis_size("dp")
-    core = lax.axis_index("tensor") % 2
     head_count, lambda_width = lambda_param.shape
     doc_lengths = (short_lengths[0], long_lengths[0])
     map_width = lambda_width // 4
@@ -953,36 +1110,19 @@
         tables.append(
             rotary_tables(position, map_width) + (segment[:, None], segment[None, :])
         )
-    cots = [mine_first(out_cotangent[m], core) for m in range(2)]
-    inputs = [half_rows(layer_in[m], core).astype(jnp.float32) for m in range(2)]
-    front = [
-        attention_forward(layer_in[m], tables[m], lam, sub_scale, norm1_gain, projections)
-        for m in range(2)
-    ]
-    heads = [front[m][5] for m in range(2)]
-    middle, normed_two, ffn = [], [], []
-    for m in range(2):
-        keep = f32_dot(half_rows(heads[m], core), out_weight)
-        send = f32_dot(half_rows(heads[m], 1 - core), out_weight)
-        middle.append(inputs[m] + tensor_sum(keep, send))
-        scaled = middle[m] * root_of(middle[m])
-        normed_two.append((with_other(scaled) * norm2_gain).astype(jnp.bfloat16))
-        ffn.append(feed_forward(normed_two[m], cots[m], gate_weight, up_weight, down_weight))
-    turned = lambda parts: [part.T for part in parts]
-    arrays = turned(cots) + turned(normed_two) + turned([front[m][0] for m in range(2)])
-    for index in (2, 3, 4):
-        arrays += [ffn[m][index] for m in range(2)]
-    arrays += heads
-    for group, part in ((0, 0), (0, 1), (1, 0), (1, 1)):
-        arrays += [ffn[m][group][part] for m in range(2)]
-    arrays += middle + [layer_in, out_cotangent, out_weight, *projections]
-    for m in range(2):
-        arrays += front[m][1:5]
-    blocks = [*tables[0], *tables[1], sub_scale, norm1_gain[None, :], norm2_gain[None, :]]
     depth, inner = query_weight.shape
     shapes = (
         depth, layer_in.shape[1], inner, gate_weight.shape[1], head_count, sub_gain.shape[1],
     )
+    blocks = [*tables[0], *tables[1], sub_scale, norm1_gain[None, :], norm2_gain[None, :]]
+    arrays = [layer_in, out_cotangent, *projections, out_weight]
+    arrays += [gate_weight, up_weight, down_weight]
+    parts = front_call(lam, arrays, blocks, shapes)
+    pick = lambda at: [parts[at], parts[at + 14]]
+    arrays = pick(0) + pick(1) + pick(2) + pick(9) + pick(10) + pick(11) + pick(7)
+    arrays += pick(12) + pick(13) + pick(8)
+    arrays += [layer_in, out_cotangent, out_weight, *projections]
+    arrays += parts[3:7] + parts[17:21]
     grad_down, grad_gate, grad_up, grad_out, grad_qkv, layer_out, grad_in, small = back_call(
         dp_count, lam, arrays, blocks, shapes
     )

time: 573 us -> 495 us (0.86)
  Pallas kernels: 367 us -> 459 us
  waiting for transfers between devices: 63.1 us -> 0 us
  local copies, waits for them, and re-layouts: 61.6 us -> 17.8 us
  matrix products: 42.5 us -> 0 us
  other arithmetic: 21.7 us -> 11.1 us
    pallas_call x2 -> x1, Pallas kernels: 17.9 us -> 108 us  [front_call(): pl.pallas_call(front_kernel, out_shape=out_shape, in_specs=[pl.BlockSpec(...]
    ppermute x6 -> x0, waiting for transfers between devices: 63.1 us -> none  [flip(): return lax.ppermute(values, axis_name, [(i, i ^ bit) for i in range(size)])]
    dot_general x22 -> x0, matrix products: 42.5 us -> none  [the longest x12 25.8 us: f32_dot(): return jnp.dot(left, right, preferred_element_type=jnp.float32)]
    unnamed x167 -> x27, local copies, waits for them, and re-layouts: 28.3 us -> 9.06 us
    dynamic_slice x5 -> x0, local copies, waits for them, and re-layouts: 10.9 us -> none  [half_rows(): return lax.dynamic_slice_in_dim(values, which * count, count, 0)]
  transfers between devices with their start and end apart: 6 -> 0, of which waited for: 2 -> 0; matrix products, arithmetic and copies ran while one was open for 7% -> 0% of each run, Pallas kernels for 2% -> 0%
where the time goes in v5:
time: 495 us; the launch traced here: 489 us
  Pallas kernels  459 us (93%)
  local copies, waits for them, and re-layouts  17.8 us (4%)
  other arithmetic  11.1 us (2%)
    pallas_call x1, Pallas kernels, back_call(): pl.pallas_call(functools.partial(back_kernel, dp_count), out_shape=[grad(...  350 us
    pallas_call x1, Pallas kernels, front_call(): pl.pallas_call(front_kernel, out_shape=out_shape, in_specs=[pl.BlockSpec(...  108 us

profile of v5, /device:TPU:0, one launch (start us, length us, event | category | flops | bytes accessed | tf_op | source)
XLA Modules:
  0.0 488.5 jit_solution(14030341719886270197)
XLA Ops:
  0.7 0.8 reshape.124
  2.2 0.8 reduce-window.17
  3.1 0.7 convert_reduce_fusion
  3.8 0.8 reduce-window.16
  4.7 0.7 convert_reduce_fusion.1
  5.4 1.9 fusion.1
  7.3 1.0 pad_maximum_fusion.3.refs_15_.refs_40_
  8.3 1.0 pad_maximum_fusion.1.refs_11_.refs_36_
  9.3 1.0 pad_maximum_fusion.refs_10_.refs_35_
  10.3 1.0 pad_maximum_fusion.2.refs_14_.refs_39_
  11.2 0.9 copy.50.refs_12_.refs_37_
  12.1 0.9 copy.51.refs_16_.refs_41_
  14.8 108.4 %shard_map.246 = (bf16[1536,512]{1,0:T(8,128)(2,1)}, bf16[1536,512]{1,0:T(8,128)(2,1)}, bf16[1536,512]{1,0:T(8,128)(2,1)}, bf16[512,384]{1,0:T(8,128)(2,1)}, bf1...) custom-call(f32[3]{0:T(128)} %subtract_add_fusion.refs_0_, ...), custom_call_target="tpu_custom_call" | custom-call | flops 24159191040 | bytes 67108864 | tf_op jit(solution)/shard_map/pallas_call | solution.py:1051
  123.2 350.2 %shard_map.247 = (f32[192,1024]{1,0:T(8,128)}, f32[192,1024]{1,0:T(8,128)}, f32[192,1024]{1,0:T(8,128)}, f32[192,384]{1,0:T(8,128)}, f32[192,1152]{1,0:T(8,128)}...) custom-call(f32[3]{0:T(128)} %subtract_add_fusion.refs_0_, ...), custom_call_target="tpu_custom_call" | custom-call | flops 19327352832 | bytes 67108864 | tf_op jit(solution)/shard_map/pallas_call | solution.py:807
  473.4 0.8 slice_reduce_fusion
  474.4 0.7 fusion.4
  475.1 0.9 fusion.16
  476.6 2.1 fusion.15
  479.3 3.9 copy.87
  483.2 1.7 copy.88
  484.9 0.7 copy.89
  485.6 0.9 copy.90
  486.5 0.9 copy.91
  487.4 0.9 copy.92
  (35 shorter events, 4.1 us)
Async XLA Ops:
  0.6 12.3 %copy-start.7 = (f32[1536]{0:T(1024)S(1)}, f32[1536]{0:T(1024)}, u32[]{:S(2)}) copy-start(f32[1536]{0:T(1024)} %param.18) | copy-start | bytes 18436
  0.7 12.9 %copy-start.8 = (f32[1536]{0:T(1024)S(1)}, f32[1536]{0:T(1024)}, u32[]{:S(2)}) copy-start(f32[1536]{0:T(1024)} %param.25) | copy-start | bytes 18436
  0.7 13.5 %copy-start.9 = (f32[3,128]{1,0:T(4,128)S(1)}, f32[3,128]{1,0:T(4,128)}, u32[]{:S(2)}) copy-start(f32[3,128]{1,0:T(4,128)} %param.23) | copy-start | bytes 4612
  3.8 11.0 %copy-start.5 = (s32[512]{0:T(512)}, s32[512]{0:T(512)S(1)}, u32[]{:S(2)}) copy-start(s32[512]{0:T(512)S(1)} %get-tuple-element.87) | copy-start | bytes 6148
  5.4 9.4 %copy-start.6 = (s32[512]{0:T(512)}, s32[512]{0:T(512)S(1)}, u32[]{:S(2)}) copy-start(s32[512]{0:T(512)S(1)} %get-tuple-element.89) | copy-start | bytes 6148
  479.3 3.9 copy-start
  483.2 1.7 copy-start.4
  483.2 2.4 copy-start.3
  483.2 3.3 copy-start.2
  484.9 2.5 copy-start.1

commit v6 on v5

--- a/solution.py
+++ b/solution.py
@@ -201,19 +201,104 @@
     return [pl.BlockSpec(memory_space=pltpu.VMEM)] * count
 
 
+class Line:
+    def __init__(self, line, widths, total, landed, line_out, line_in, credit):
+        self.line, self.widths = line, widths
+        self.total, self.landed = total, landed
+        self.line_out, self.line_in, self.credit = line_out, line_in, credit
+        self.me = lax.axis_index("dp")
+        self.place = self.me // 2
+        self.ring = total.shape[0]
+
+    def copy(self, c, step, way, block, target):
+        width = self.widths[c]
+        return pltpu.make_async_remote_copy(
+            src_ref=self.total.at[c % self.ring, block, :, :width],
+            dst_ref=self.landed.at[way, step, c % 2, :, :width],
+            send_sem=self.line_out.at[way, step, c % 2],
+            recv_sem=self.line_in.at[way, step, c % 2],
+            device_id={"dp": target},
+            device_id_type=MESH,
+        )
+
+    def sends(self, step, way):
+        place, line = self.place, self.line
+        if way == 0:
+            block = line - 1 - step + place
+            return (place <= step) & (place < line - 1), block, self.me + 2
+        block = place + step - line + 1
+        return (place >= line - 1 - step) & (place > 0), block, self.me - 2
+
+    def gets(self, step, way):
+        place, line = self.place, self.line
+        if way == 0:
+            return (place > 0) & (place - 1 <= step), line - 2 - step + place, self.me - 2
+        gets = (place < line - 1) & (place + 1 >= line - 1 - step)
+        return gets, place + step - line + 2, self.me + 2
+
+    def start(self, c, step):
+        for way in range(2):
+            sends, block, target = self.sends(step, way)
+
+            @pl.when(sends)
+            def _():
+                if c >= 2:
+                    pl.semaphore_wait(self.credit.at[way, step], 1)
+                self.copy(c, step, way, block, target).start()
+
+    def finish(self, c, step):
+        width = self.widths[c]
+        for way in range(2):
+            gets, block, source = self.gets(step, way)
+
+            @pl.when(gets)
+            def _():
+                self.copy(c, step, way, block, source).wait_recv()
+                self.total[c % self.ring, block, :, :width] += self.landed[
+                    way, step, c % 2, :, :width
+                ]
+                if c + 2 < len(self.widths):
+                    pl.semaphore_signal(
+                        self.credit.at[way, step],
+                        inc=1,
+                        device_id={"dp": source},
+                        device_id_type=MESH,
+                    )
+
+            sends, sent, target = self.sends(step, way)
+
+            @pl.when(sends)
+            def _():
+                self.copy(c, step, way, sent, target).wait_send()
+
+
 class Reducer:
-    def __init__(self, plan, line, refs):
-        self.plan, self.line = plan, line
+    def __init__(self, plan, line_plan, line_starts, line, refs):
+        self.plan, self.line_plan, self.line_starts = plan, line_plan, line_starts
+        self.line = line
         (
-            self.send, self.held, self.total, self.landed, self.pair_out, self.pair_in,
-            self.line_out, self.line_in, self.credit, self.out_sem,
-        ) = refs
-        self.me = lax.axis_index("dp")
-        self.place, self.side = self.me // 2, self.me % 2
+            self.send, self.held, self.total, landed, self.pair_out, self.pair_in,
+            line_out, line_in, credit, self.out_sem,
+        ) = refs[:10]
+        self.first = Line(
+            line, [item.width for item in plan], self.total, landed, line_out, line_in, credit
+        )
+        self.place = self.first.place
+        self.me = self.first.me
+        self.side = self.me % 2
         self.other = self.me + 1 - 2 * self.side
         self.steps = line - 1
         self.ring = self.total.shape[0]
         self.rows = self.total.shape[2]
+        if line_plan:
+            (
+                self.line_total, landed, line_out, line_in, credit, self.last_held,
+                self.last_out, self.last_in, self.line_out_sem,
+            ) = refs[10:]
+            self.second = Line(
+                line, [item.width for item in line_plan], self.line_total, landed, line_out,
+                line_in, credit,
+            )
 
     def compute(self, c):
         item = self.plan[c]
@@ -231,6 +316,63 @@
 
         lax.fori_loop(0, self.line, block, 0)
         item.computed()
+
+    def line_compute(self, c):
+        item = self.line_plan[c]
+        left, right = item.left(), item.right()
+        slot = c % self.line_total.shape[0]
+        if c >= self.line_total.shape[0]:
+            self.line_result(c - self.line_total.shape[0]).wait()
+
+        def block(at, carry):
+            rows = pl.ds(pl.multiple_of(2 * at * self.rows, 2 * self.rows), 2 * self.rows)
+            self.line_total[slot, at] = f32_dot(left[rows, :], right[...])
+            return carry
+
+        lax.fori_loop(0, self.line, block, 0)
+        item.computed()
+
+    def side_rows(self, side):
+        return pl.ds(pl.multiple_of(side * self.rows, self.rows), self.rows)
+
+    def last_copy(self, c):
+        slot = c % self.line_total.shape[0]
+        return pltpu.make_async_remote_copy(
+            src_ref=self.line_total.at[slot, self.place, self.side_rows(1 - self.side), :],
+            dst_ref=self.last_held.at[c],
+            send_sem=self.last_out.at[c],
+            recv_sem=self.last_in.at[c],
+            device_id={"dp": self.other},
+            device_id_type=MESH,
+        )
+
+    def line_result(self, c):
+        item = self.line_plan[c]
+        slot = c % self.line_total.shape[0]
+        return pltpu.make_async_copy(
+            self.line_total.at[slot, self.place, self.side_rows(self.side), :],
+            item.out.at[:, item.first : item.first + item.width],
+            self.line_out_sem.at[slot],
+        )
+
+    def line_finish(self, slot):
+        for c, start in enumerate(self.line_starts):
+            step = slot - 1 - start
+            if 0 <= step < self.steps:
+                self.second.finish(c, step)
+            if step == self.steps:
+                self.last_copy(c).wait()
+                at = c % self.line_total.shape[0]
+                self.line_total[at, self.place, self.side_rows(self.side), :] += self.last_held[c]
+                self.line_result(c).start()
+
+    def line_begin(self, slot):
+        for c, start in enumerate(self.line_starts):
+            step = slot - start
+            if 0 <= step < self.steps:
+                self.second.start(c, step)
+            if step == self.steps:
+                self.last_copy(c).start()
 
     def pair_copy(self, c):
         width = self.plan[c].width
@@ -254,67 +396,6 @@
         lax.fori_loop(0, self.line, block, 0)
         self.pair_copy(c).wait_send()
 
-    def line_copy(self, c, step, way, block, target):
-        width = self.plan[c].width
-        return pltpu.make_async_remote_copy(
-            src_ref=self.total.at[c % self.ring, block, :, :width],
-            dst_ref=self.landed.at[way, step, c % 2, :, :width],
-            send_sem=self.line_out.at[way, step, c % 2],
-            recv_sem=self.line_in.at[way, step, c % 2],
-            device_id={"dp": target},
-            device_id_type=MESH,
-        )
-
-    def line_sends(self, step, way):
-        place, line = self.place, self.line
-        if way == 0:
-            block = line - 1 - step + place
-            return (place <= step) & (place < line - 1), block, self.me + 2
-        block = place + step - line + 1
-        return (place >= line - 1 - step) & (place > 0), block, self.me - 2
-
-    def line_gets(self, step, way):
-        place, line = self.place, self.line
-        if way == 0:
-            return (place > 0) & (place - 1 <= step), line - 2 - step + place, self.me - 2
-        gets = (place < line - 1) & (place + 1 >= line - 1 - step)
-        return gets, place + step - line + 2, self.me + 2
-
-    def line_start(self, c, step):
-        for way in range(2):
-            sends, block, target = self.line_sends(step, way)
-
-            @pl.when(sends)
-            def _():
-                if c >= 2:
-                    pl.semaphore_wait(self.credit.at[way, step], 1)
-                self.line_copy(c, step, way, block, target).start()
-
-    def line_finish(self, c, step):
-        width = self.plan[c].width
-        for way in range(2):
-            gets, block, source = self.line_gets(step, way)
-
-            @pl.when(gets)
-            def _():
-                self.line_copy(c, step, way, block, source).wait_recv()
-                self.total[c % self.ring, block, :, :width] += self.landed[
-                    way, step, c % 2, :, :width
-                ]
-                if c + 2 < len(self.plan):
-                    pl.semaphore_signal(
-                        self.credit.at[way, step],
-                        inc=1,
-                        device_id={"dp": source},
-                        device_id_type=MESH,
-                    )
-
-            sends, sent, target = self.line_sends(step, way)
-
-            @pl.when(sends)
-            def _():
-                self.line_copy(c, step, way, sent, target).wait_send()
-
     def out_copy(self, c):
         item = self.plan[c]
         return pltpu.make_async_copy(
@@ -325,20 +406,27 @@
 
     def run(self, tasks):
         count, steps = len(self.plan), self.steps
+        begun = [c for c, start in enumerate(self.line_starts) if start == 0]
         self.compute(0)
         self.pair_copy(0).start()
+        for c in begun:
+            self.line_compute(c)
+        self.line_begin(0)
         self.compute(1)
         for slot in range(count + steps + 1):
             for step in range(steps):
                 c = slot - 2 - step
                 if 0 <= c < count:
-                    self.line_finish(c, step)
+                    self.first.finish(c, step)
+            self.line_finish(slot)
             if 0 <= slot - 1 < count:
                 self.pair_finish(slot - 1)
             for step in range(steps):
                 c = slot - 1 - step
                 if 0 <= c < count:
-                    self.line_start(c, step)
+                    self.first.start(c, step)
+            if slot:
+                self.line_begin(slot)
             if slot + 1 < count:
                 self.pair_copy(slot + 1).start()
             done = slot - 1 - steps
@@ -348,10 +436,16 @@
                 if slot + 2 >= self.ring:
                     self.out_copy(slot + 2 - self.ring).wait()
                 self.compute(slot + 2)
+            for c, start in enumerate(self.line_starts):
+                if slot and start == slot + 1:
+                    self.line_compute(c)
             for task in tasks.get(slot, ()):
                 task()
         for c in range(max(0, count - self.ring), count):
             self.out_copy(c).wait()
+        if self.line_plan:
+            for c in range(len(self.line_plan) - self.line_total.shape[0], len(self.line_plan)):
+                self.line_result(c).wait()
 
 
 class Chunk:
@@ -434,6 +528,10 @@
             pl.semaphore_signal(
                 self.far_credit, inc=1, device_id={"tensor": self.far_peer}, device_id_type=MESH
             )
+
+
+def line_first(dp_count):
+    return (0, 0, 3, 6, 9, 12) if dp_count == 8 else ()
 
 
 def back_kernel(dp_count, *refs):
@@ -449,10 +547,11 @@
     tables = [take(4) for _ in range(2)]
     (sub_scale, gain_one, gain_two) = take(3)
     (grad_down, grad_gate, grad_up, grad_out, grad_qkv, layer_out, grad_in, small_out) = take(8)
-    reducer_refs = take(10)
+    reducer_refs = take(20 if line_first(dp_count) else 10)
+    line_rights = reducer_refs.pop() if line_first(dp_count) else None
     (left_a, left_b, rights, rows_qkv) = take(4)
     weights = take(4)
-    kept = [take(4) for _ in range(2)]
+    kept = take(4)
     backward_scratch = take(4)
     (grad_sub, grad_lam) = take(2)
     sets = [take(3) for _ in range(2)]
@@ -505,16 +604,27 @@
     def load_left(sources_of, left):
         return [load(sources_of[m], left.at[:, tokens[m]]) for m in range(2)]
 
+    def load_columns(source, first, width, target):
+        return [
+            load(source[m].at[:, first : first + width], target.at[tokens[m], :width])
+            for m in range(2)
+        ]
+
     def load_right(c):
         if c in sources:
-            source, first, width = sources[c]
-            right_loads[c] = [
-                load(source[m].at[:, first : first + width], rights.at[c % 2, tokens[m], :width])
-                for m in range(2)
-            ]
+            right_loads[c] = load_columns(*sources[c], rights.at[c % 2])
+
+    def load_line_right(c):
+        if c < len(line_sources):
+            line_loads[c] = load_columns(*line_sources[c], line_rights.at[c % 2])
 
     def get_left(c, left):
         wait_all(left_loads.pop(c, ()))
+        return left
+
+    def get_line_left(left):
+        if left is left_b and first_two in left_loads:
+            wait_all(left_loads.pop(first_two))
         return left
 
     def get_right(c, first, width):
@@ -523,13 +633,31 @@
             return rights.at[c % 2, :, :width]
         return rows_qkv.at[:, first : first + width]
 
+    def get_line_right(c):
+        wait_all(line_loads[c])
+        return line_rights.at[c % 2]
+
     def computed(c):
         load_right(c + 2)
         if c == last_two:
             left_loads[first_one] = load_left(one_left, left_b)
 
-    def add_group(left, source, columns, out):
-        for first in range(0, columns, reducer_width):
+    def add_group(left, source, columns, out, line_chunks=0):
+        start = line_chunks * line_width
+        for first in range(0, start, line_width):
+            c = len(line_plan)
+            line_sources.append((source, first, line_width))
+            line_plan.append(
+                Chunk(
+                    functools.partial(get_line_left, left),
+                    functools.partial(get_line_right, c),
+                    functools.partial(load_line_right, c + 2),
+                    out,
+                    first,
+                    line_width,
+                )
+            )
+        for first in range(start, columns, reducer_width):
             width = min(reducer_width, columns - first)
             c = len(plan)
             if source is not None:
@@ -545,17 +673,23 @@
                 )
             )
 
+    line_starts = line_first(dp_count)
+    line_plan, line_sources, line_loads, line_width = [], [], {}, 128
+    late = len(line_starts) // 3
     add_group(left_a, hidden, hidden[0].shape[1], grad_down)
     first_two = len(plan)
-    add_group(left_b, gate_pre, gate_pre[0].shape[1], grad_gate)
-    add_group(left_b, up_pre, up_pre[0].shape[1], grad_up)
+    add_group(left_b, gate_pre, gate_pre[0].shape[1], grad_gate, late)
+    add_group(left_b, up_pre, up_pre[0].shape[1], grad_up, late)
     last_two = len(plan) - 1
-    add_group(left_a, heads, inner, grad_out)
+    add_group(left_a, heads, inner, grad_out, late)
     first_one = len(plan)
     add_group(left_b, None, 3 * inner, grad_qkv)
 
     left_loads[0] = load_left(cot_left, left_a)
     load_right(0)
+    left_loads[first_two] = load_left(two_left, left_b)
+    load_line_right(0)
+    load_line_right(1)
     load_right(1)
     sums = [
         TensorSum(
@@ -567,9 +701,8 @@
     for m in range(2):
         own_loads[m] = load(part_back[m].at[kept_half], sets[m][0])
         sums[m].near_start(part_back[m].at[sent_half])
-    left_loads[first_two] = load_left(two_left, left_b)
     weight_loads = [load(*pair) for pair in zip(weights_in, weights)]
-    kept_loads = [[load(*pair) for pair in zip(kept_in[m], kept[m])] for m in range(2)]
+    kept_loads = [load(*pair) for pair in zip(kept_in[0], kept)]
     spare_queue = [middle[0], middle[1], middle[0], middle[1]]
     rows_queue = [cotangent.at[0], cotangent.at[1]]
     rows_queue += [layer_in.at[0], cotangent.at[0], layer_in.at[1], cotangent.at[1]]
@@ -640,11 +773,13 @@
         lax.fori_loop(0, attended.shape[1] // 128, flip_block, 0)
         if m == 0:
             wait_all(weight_loads)
-        wait_all(kept_loads[m])
+        wait_all(kept_loads)
         backward_kernel(
-            lam, attended, out_weight, *kept[m], *tables[m], sub_scale,
+            lam, attended, out_weight, *kept, *tables[m], sub_scale,
             rows_qkv.at[tokens[m], :], grad_sub, grad_lam, *backward_scratch,
         )
+        if m == 0:
+            kept_loads[:] = [load(*pair) for pair in zip(kept_in[1], kept)]
         for head in range(head_count):
             at = slice(head * head_width, (head + 1) * head_width)
             small[2:3, at] += grad_sub[head : head + 1, :]
@@ -782,7 +917,7 @@
     }
     stretch = 256 // reducer_width
     tasks = {slot * stretch: items for slot, items in order.items()}
-    Reducer(plan, line, reducer_refs).run(tasks)
+    Reducer(plan, line_plan, line_starts, line, reducer_refs).run(tasks)
     wait_all(out_loads)
 
 
@@ -792,7 +927,8 @@
     rows = depth // dp_count
     half = row_count // 2
     width = 256 if line <= 4 else 128
-    ring = line + 4
+    ring = line + 3
+    starts = line_first(dp_count)
     wide = (line, rows, width)
     bf16, f32 = jnp.bfloat16, jnp.float32
     dma, regular = pltpu.SemaphoreType.DMA, pltpu.SemaphoreType.REGULAR
@@ -824,6 +960,24 @@
             dma((2, line - 1, 2)),
             regular((2, line - 1)),
             dma((ring,)),
+        ]
+        + (
+            [
+                pltpu.VMEM((3, line, 2 * rows, 128), f32),
+                pltpu.VMEM((2, line - 1, 2, 2 * rows, 128), f32),
+                dma((2, line - 1, 2)),
+                dma((2, line - 1, 2)),
+                regular((2, line - 1)),
+                pltpu.VMEM((len(starts), rows, 128), f32),
+                dma((len(starts),)),
+                dma((len(starts),)),
+                dma((3,)),
+                pltpu.VMEM((2, 2 * row_count, 128), bf16),
+            ]
+            if starts
+            else []
+        )
+        + [
             pltpu.VMEM((depth, 2 * row_count), bf16),
             pltpu.VMEM((depth, 2 * row_count), bf16),
             pltpu.VMEM((2, 2 * row_count, width), bf16),
@@ -831,7 +985,7 @@
             pltpu.VMEM((inner, depth), bf16),
         ]
         + [pltpu.VMEM((depth, inner), bf16)] * 3
-        + [narrow, narrow, narrow, narrow_f32] * 2
+        + [narrow, narrow, narrow, narrow_f32]
         + [narrow_f32, narrow, narrow_f32, narrow_f32]
         + [pltpu.VMEM((head_count, head_width), f32)] * 2
         + [wide_half] * 10
@@ -850,7 +1004,7 @@
             dma((dp_count - 1,)),
         ],
         compiler_params=pltpu.CompilerParams(
-            collective_id=0, has_side_effects=True, vmem_limit_bytes=60 * 1024 * 1024
+            collective_id=0, has_side_effects=True, vmem_limit_bytes=62 * 1024 * 1024
         ),
         cost_estimate=pl.CostEstimate(flops=flops, bytes_accessed=64 << 20, transcendentals=0),
     )(lam, *arrays, *blocks)

time: 495 us -> 456 us (0.921)
  Pallas kernels: 459 us -> 419 us
    pallas_call x1, Pallas kernels: 350 us -> 311 us  [back_call(): pl.pallas_call(functools.partial(back_kernel, dp_count), out_shape=[grad(...]
where the time goes in v6:
time: 456 us; the launch traced here: 449 us
  Pallas kernels  419 us (92%)
  local copies, waits for them, and re-layouts  17.8 us (4%)
  other arithmetic  11.1 us (2%)
    pallas_call x1, Pallas kernels, back_call(): pl.pallas_call(functools.partial(back_kernel, dp_count), out_shape=[grad(...  311 us
    pallas_call x1, Pallas kernels, front_call(): pl.pallas_call(front_kernel, out_shape=out_shape, in_specs=[pl.BlockSpec(...  109 us

profile of v6, /device:TPU:0, one launch (start us, length us, event | category | flops | bytes accessed | tf_op | source)
XLA Modules:
  0.0 449.2 jit_solution(2259911094350213190)
XLA Ops:
  0.7 0.8 reshape.124
  2.2 0.8 reduce-window.17
  3.1 0.7 convert_reduce_fusion
  3.8 0.8 reduce-window.16
  4.7 0.7 convert_reduce_fusion.1
  5.4 1.9 fusion.1
  7.3 1.0 pad_maximum_fusion.3.refs_15_.refs_40_
  8.3 1.0 pad_maximum_fusion.1.refs_11_.refs_36_
  9.3 1.0 pad_maximum_fusion.refs_10_.refs_35_
  10.3 1.0 pad_maximum_fusion.2.refs_14_.refs_39_
  11.2 0.9 copy.50.refs_12_.refs_37_
  12.1 0.9 copy.51.refs_16_.refs_41_
  14.8 108.5 %shard_map.246 = (bf16[1536,512]{1,0:T(8,128)(2,1)}, bf16[1536,512]{1,0:T(8,128)(2,1)}, bf16[1536,512]{1,0:T(8,128)(2,1)}, bf16[512,384]{1,0:T(8,128)(2,1)}, bf1...) custom-call(f32[3]{0:T(128)} %subtract_add_fusion.refs_0_, ...), custom_call_target="tpu_custom_call" | custom-call | flops 24159191040 | bytes 67108864 | tf_op jit(solution)/shard_map/pallas_call | solution.py:1205
  123.3 310.6 %shard_map.247 = (f32[192,1024]{1,0:T(8,128)}, f32[192,1024]{1,0:T(8,128)}, f32[192,1024]{1,0:T(8,128)}, f32[192,384]{1,0:T(8,128)}, f32[192,1152]{1,0:T(8,128)}...) custom-call(f32[3]{0:T(128)} %subtract_add_fusion.refs_0_, ...), custom_call_target="tpu_custom_call" | custom-call | flops 19327352832 | bytes 67108864 | tf_op jit(solution)/shard_map/pallas_call | solution.py:943
  433.9 0.8 slice_reduce_fusion
  434.9 0.7 fusion.4
  435.5 0.9 fusion.16
  437.1 2.1 fusion.15
  439.8 3.9 copy.87
  443.7 1.7 copy.88
  445.4 0.7 copy.89
  446.1 0.9 copy.90
  447.0 0.9 copy.91
  447.9 0.9 copy.92
  (35 shorter events, 4.1 us)
Async XLA Ops:
  0.6 12.3 %copy-start.7 = (f32[1536]{0:T(1024)S(1)}, f32[1536]{0:T(1024)}, u32[]{:S(2)}) copy-start(f32[1536]{0:T(1024)} %param.18) | copy-start | bytes 18436
  0.7 12.9 %copy-start.8 = (f32[1536]{0:T(1024)S(1)}, f32[1536]{0:T(1024)}, u32[]{:S(2)}) copy-start(f32[1536]{0:T(1024)} %param.25) | copy-start | bytes 18436
  0.7 13.5 %copy-start.9 = (f32[3,128]{1,0:T(4,128)S(1)}, f32[3,128]{1,0:T(4,128)}, u32[]{:S(2)}) copy-start(f32[3,128]{1,0:T(4,128)} %param.23) | copy-start | bytes 4612
  3.8 11.0 %copy-start.5 = (s32[512]{0:T(512)}, s32[512]{0:T(512)S(1)}, u32[]{:S(2)}) copy-start(s32[512]{0:T(512)S(1)} %get-tuple-element.87) | copy-start | bytes 6148
  5.4 9.4 %copy-start.6 = (s32[512]{0:T(512)}, s32[512]{0:T(512)S(1)}, u32[]{:S(2)}) copy-start(s32[512]{0:T(512)S(1)} %get-tuple-element.89) | copy-start | bytes 6148
  439.8 3.9 copy-start
  443.7 1.7 copy-start.4
  443.7 2.4 copy-start.3
  443.7 3.3 copy-start.2
  445.4 2.5 copy-start.1

commit v7 on v6

--- a/solution.py
+++ b/solution.py
@@ -106,7 +106,7 @@
 
 def forward_kernel(
     lam, rows, gain, query_weight, key_weight, value_weight, cosine, sine, segment_column,
-    segment_row, sub_scale, normed_one, query, key, value, mixed, heads_out,
+    segment_row, sub_scale, normed_one, query, key, value, mixed, heads_out, between,
 ):
     head_count, width = sub_scale.shape
     scale = (width // 2) ** (-0.5)
@@ -123,6 +123,8 @@
         first, last = key_range(block)
         here = slice(block * block_rows, last)
         opened = open_pairs(block, segment_column, segment_row)
+        if block in between:
+            between[block]()
         for head in range(head_count):
             at = slice(head * width, (head + 1) * width)
             keys = key[first:last, at]
@@ -407,8 +409,6 @@
     def run(self, tasks):
         count, steps = len(self.plan), self.steps
         begun = [c for c, start in enumerate(self.line_starts) if start == 0]
-        self.compute(0)
-        self.pair_copy(0).start()
         for c in begun:
             self.line_compute(c)
         self.line_begin(0)
@@ -531,7 +531,7 @@
 
 
 def line_first(dp_count):
-    return (0, 0, 3, 6, 9, 12) if dp_count == 8 else ()
+    return ((0, 0, 3, 6, 9, 12), (2, 2, 2)) if dp_count == 8 else ((), (0, 0, 0))
 
 
 def back_kernel(dp_count, *refs):
@@ -547,8 +547,8 @@
     tables = [take(4) for _ in range(2)]
     (sub_scale, gain_one, gain_two) = take(3)
     (grad_down, grad_gate, grad_up, grad_out, grad_qkv, layer_out, grad_in, small_out) = take(8)
-    reducer_refs = take(20 if line_first(dp_count) else 10)
-    line_rights = reducer_refs.pop() if line_first(dp_count) else None
+    reducer_refs = take(20 if line_first(dp_count)[0] else 10)
+    line_rights = reducer_refs.pop() if line_first(dp_count)[0] else None
     (left_a, left_b, rights, rows_qkv) = take(4)
     weights = take(4)
     kept = take(4)
@@ -584,7 +584,6 @@
         )
     for peer in (core_peer, far_peer):
         pl.semaphore_signal(barrier, inc=1, device_id={"tensor": peer}, device_id_type=MESH)
-    pl.semaphore_wait(barrier, dp_count + 1)
 
     used = [0]
 
@@ -673,15 +672,14 @@
                 )
             )
 
-    line_starts = line_first(dp_count)
+    line_starts, line_counts = line_first(dp_count)
     line_plan, line_sources, line_loads, line_width = [], [], {}, 128
-    late = len(line_starts) // 3
     add_group(left_a, hidden, hidden[0].shape[1], grad_down)
     first_two = len(plan)
-    add_group(left_b, gate_pre, gate_pre[0].shape[1], grad_gate, late)
-    add_group(left_b, up_pre, up_pre[0].shape[1], grad_up, late)
+    add_group(left_b, gate_pre, gate_pre[0].shape[1], grad_gate, line_counts[0])
+    add_group(left_b, up_pre, up_pre[0].shape[1], grad_up, line_counts[1])
     last_two = len(plan) - 1
-    add_group(left_a, heads, inner, grad_out, late)
+    add_group(left_a, heads, inner, grad_out, line_counts[2])
     first_one = len(plan)
     add_group(left_b, None, 3 * inner, grad_qkv)
 
@@ -697,10 +695,7 @@
         )
         for m in range(2)
     ]
-    own_loads = {}
-    for m in range(2):
-        own_loads[m] = load(part_back[m].at[kept_half], sets[m][0])
-        sums[m].near_start(part_back[m].at[sent_half])
+    own_loads = {m: load(part_back[m].at[kept_half], sets[m][0]) for m in range(2)}
     weight_loads = [load(*pair) for pair in zip(weights_in, weights)]
     kept_loads = [load(*pair) for pair in zip(kept_in[0], kept)]
     spare_queue = [middle[0], middle[1], middle[0], middle[1]]
@@ -917,7 +912,13 @@
     }
     stretch = 256 // reducer_width
     tasks = {slot * stretch: items for slot, items in order.items()}
-    Reducer(plan, line_plan, line_starts, line, reducer_refs).run(tasks)
+    reducer = Reducer(plan, line_plan, line_starts, line, reducer_refs)
+    reducer.compute(0)
+    pl.semaphore_wait(barrier, dp_count + 1)
+    reducer.pair_copy(0).start()
+    for m in range(2):
+        sums[m].near_start(part_back[m].at[sent_half])
+    reducer.run(tasks)
     wait_all(out_loads)
 
 
@@ -928,7 +929,7 @@
     half = row_count // 2
     width = 256 if line <= 4 else 128
     ring = line + 3
-    starts = line_first(dp_count)
+    starts = line_first(dp_count)[0]
     wide = (line, rows, width)
     bf16, f32 = jnp.bfloat16, jnp.float32
     dma, regular = pltpu.SemaphoreType.DMA, pltpu.SemaphoreType.REGULAR
@@ -1010,7 +1011,178 @@
     )(lam, *arrays, *blocks)
 
 
-def front_kernel(*refs):
+def gathers_heads(dp_count):
+    return dp_count == 8
+
+
+class Gather:
+    def __init__(self, own, piece, wide, far, near, far_near, full, sems):
+        self.own, self.piece, self.wide = own, piece, wide
+        self.far, self.near, self.far_near, self.full = far, near, far_near, full
+        (
+            self.cross_sems, self.line_out, self.line_in, self.pair_out, self.pair_in,
+            self.near_sems,
+        ) = sems
+        self.me = lax.axis_index("dp")
+        self.place, self.side = self.me // 2, self.me % 2
+        self.line = self.line_out.shape[1] + 1
+        self.rows = piece.shape[0]
+        tensor = lax.axis_index("tensor")
+        self.tensor = tensor
+        self.core_peer = tensor + 1 - 2 * (tensor % 2)
+        self.far_peer = tensor + 2 - 4 * (tensor // 2)
+        self.diagonal = self.far_peer + 1 - 2 * (tensor % 2)
+
+    def slot(self, side, place):
+        start = (side * self.line + place) * self.rows
+        return self.far.at[pl.ds(pl.multiple_of(start, self.rows), self.rows)]
+
+    def remote(self, source, target, send, recv, device):
+        return pltpu.make_async_remote_copy(
+            src_ref=source, dst_ref=target, send_sem=send, recv_sem=recv, device_id=device,
+            device_id_type=MESH,
+        )
+
+    def cross(self):
+        return self.remote(
+            self.piece, self.slot(self.side, self.place), self.cross_sems.at[0],
+            self.cross_sems.at[1], {"tensor": self.far_peer},
+        )
+
+    def near_copy(self, index):
+        half = self.line * self.rows
+        if index == 0:
+            source, target = self.wide, self.near
+        else:
+            start = (self.side if index == 1 else 1 - self.side) * half
+            rows = pl.ds(pl.multiple_of(start, self.rows), half)
+            source, target = self.far.at[rows], self.far_near.at[rows]
+        return self.remote(
+            source, target, self.near_sems.at[0, index], self.near_sems.at[1, index],
+            {"tensor": self.core_peer},
+        )
+
+    def line_copy(self, way, step):
+        place = self.place - step if way == 0 else self.place + step
+        slot = self.slot(self.side, place)
+        return self.remote(
+            slot, slot, self.line_out.at[way, step], self.line_in.at[way, step],
+            {"dp": self.me + 2 - 4 * way},
+        )
+
+    def line_sends(self, way, step):
+        if way == 0:
+            return (self.place >= step) & (self.place < self.line - 1)
+        return (self.place + step <= self.line - 1) & (self.place > 0)
+
+    def line_gets(self, way, step):
+        if way == 0:
+            return self.place >= step
+        return self.place + step <= self.line - 1
+
+    def pair_copy(self, index, place):
+        slot = self.slot(self.side, place)
+        return self.remote(
+            slot, slot, self.pair_out.at[index], self.pair_in.at[index],
+            {"dp": self.me + 1 - 2 * self.side},
+        )
+
+    def pair_index(self, way, step):
+        return 1 + way * (self.line - 1) + step - 1
+
+    def begin(self):
+        count = self.own.shape[0]
+        rows = pl.ds(pl.multiple_of(self.me * self.rows, self.rows), self.rows)
+        self.piece[...] = self.own[rows, :].astype(jnp.float32)
+        self.cross().start()
+
+        def widen(rows):
+            self.wide[rows, :] = self.own[rows, :].astype(jnp.float32)
+
+        for_rows(count, widen)
+        self.near_copy(0).start()
+
+    def forward(self, step):
+        if step == 0:
+            self.cross().wait()
+            self.pair_copy(0, self.place).start()
+        for way in range(2):
+            if step:
+
+                @pl.when(self.line_gets(way, step))
+                def _():
+                    self.line_arrival(way, step).wait_recv()
+                    place = self.place - step if way == 0 else self.place + step
+                    self.pair_copy(self.pair_index(way, step), place).start()
+
+            if step < self.line - 1:
+
+                @pl.when(self.line_sends(way, step))
+                def _():
+                    self.line_copy(way, step).start()
+
+    def line_arrival(self, way, step):
+        place = self.place - step if way == 0 else self.place + step
+        slot = self.slot(self.side, place)
+        return self.remote(
+            slot, slot, self.line_out.at[way, step - 1], self.line_in.at[way, step - 1],
+            {"dp": self.me - 2 + 4 * way},
+        )
+
+    def store(self, source, tensor, first, count):
+        block = self.own.shape[0]
+
+        def narrow(rows):
+            at = pl.ds(pl.multiple_of(tensor * block + first + rows.start, row_group), row_group)
+            self.full[at, :] = source[rows, :].astype(jnp.bfloat16)
+
+        for_rows(count, narrow)
+
+    def store_far(self, source, tensor):
+        for side in range(2):
+            for place in range(self.line):
+                rows = pl.ds((side * self.line + place) * self.rows, self.rows)
+                self.store(source.at[rows], tensor, (2 * place + side) * self.rows, self.rows)
+
+    def finish_line(self):
+        self.near_copy(1).start()
+        for way in range(2):
+            for step in range(self.line - 1):
+
+                @pl.when(self.line_sends(way, step))
+                def _():
+                    self.line_copy(way, step).wait_send()
+
+        block = self.own.shape[0]
+        self.store(self.own, self.tensor, 0, block)
+        self.near_copy(0).wait()
+        self.store(self.near, self.core_peer, 0, block)
+
+    def finish(self):
+        for index in range(1 + 2 * (self.line - 1)):
+            if index == 0:
+                self.pair_copy(0, self.place).wait()
+                continue
+            way, step = (index - 1) // (self.line - 1), (index - 1) % (self.line - 1) + 1
+
+            @pl.when(self.line_gets(way, step))
+            def _():
+                place = self.place - step if way == 0 else self.place + step
+                slot = self.slot(1 - self.side, place)
+                self.pair_copy(index, place).wait_send()
+                self.remote(
+                    slot, slot, self.pair_out.at[index], self.pair_in.at[index],
+                    {"dp": self.me + 1 - 2 * self.side},
+                ).wait_recv()
+
+        self.near_copy(2).start()
+        self.store_far(self.far, self.far_peer)
+        self.near_copy(1).wait()
+        self.near_copy(2).wait()
+        self.store_far(self.far_near, self.diagonal)
+
+
+def front_kernel(dp_count, *refs):
     refs = list(refs)
     take = lambda n: [refs.pop(0) for _ in range(n)]
     (lam,) = take(1)
@@ -1022,12 +1194,19 @@
     rows_in, cot_rows = take(2), take(2)
     (normed_one, normed_two, flipped) = take(3)
     weights = take(7)
-    kept = [take(5) for _ in range(2)]
-    sets = [take(3) for _ in range(2)]
-    (projected,) = take(1)
-    hidden = [take(3) for _ in range(2)]
+    kept = take(5)
+    hidden = take(3)
     (back, fed) = take(2)
-    (near_sems, far_sems, near_credit, load_sems) = take(4)
+    (near_sems, load_sems) = take(2)
+    gathers = gathers_heads(dp_count)
+    if gathers:
+        sets = [take(2) for _ in range(2)]
+        heads_wide, heads_landed = take(2), take(2)
+        (heads_full, piece, wide, near_weight, full_weight, heads_sems) = take(6)
+        gather_sems = take(6)
+    else:
+        sets = [take(3) for _ in range(2)]
+        (projected, far_sems, near_credit) = take(3)
     assert not refs
 
     tensor = lax.axis_index("tensor")
@@ -1056,14 +1235,31 @@
     wide_loads = [load(*pair) for pair in zip(weights_in[4:], weights[4:])]
 
     barrier = pltpu.get_barrier_semaphore()
-    for peer in (tensor + 1 - 2 * core, tensor + 2 - 4 * (tensor // 2)):
+    core_peer, far_peer = tensor + 1 - 2 * core, tensor + 2 - 4 * (tensor // 2)
+    diagonal = far_peer + 1 - 2 * core
+    me = lax.axis_index("dp")
+    for peer in (core_peer, far_peer, diagonal):
         pl.semaphore_signal(barrier, inc=1, device_id={"tensor": peer}, device_id_type=MESH)
-    pl.semaphore_wait(barrier, 2)
-    sums = [
-        TensorSum(1, *sets[m], near_sems.at[m], far_sems.at[m], near_credit.at[m], None)
-        for m in range(2)
-    ]
-    out_loads, flip_loads, wide_outs = [], [], []
+    if gathers:
+        for offset in range(1, dp_count):
+            target = lax.rem(me + offset, dp_count)
+            pl.semaphore_signal(barrier, inc=1, device_id={"dp": target}, device_id_type=MESH)
+    pl.semaphore_wait(barrier, dp_count + 2 if gathers else 3)
+    if gathers:
+        sums = [
+            TensorSum(1, *sets[m], None, near_sems.at[m], None, None, None) for m in range(2)
+        ]
+        for item in sums:
+            item.near_left = 1
+        gather = Gather(
+            weights[3], piece, wide, back, near_weight, fed, full_weight, gather_sems
+        )
+    else:
+        sums = [
+            TensorSum(1, *sets[m], near_sems.at[m], far_sems.at[m], near_credit.at[m], None)
+            for m in range(2)
+        ]
+    out_loads, flip_loads, wide_outs, hidden_outs = [], [], [], []
 
     def mine(rows):
         return pl.ds(pl.multiple_of(core * half + rows.start, row_group), row_group)
@@ -1082,14 +1278,55 @@
         lax.fori_loop(0, depth // 128, block, 0)
         flip_loads.append(load(flipped, target))
 
-    def attend(m):
+    def heads_copy(m, index):
+        peer = (core_peer, far_peer, diagonal)[index]
+        which = core if index == 1 else 1 - core
+        rows = pl.ds(pl.multiple_of(which * half, half), half)
+        return pltpu.make_async_remote_copy(
+            src_ref=heads_wide[m].at[rows], dst_ref=heads_landed[m].at[index],
+            send_sem=heads_sems.at[m, 0, index], recv_sem=heads_sems.at[m, 1, index],
+            device_id={"tensor": peer}, device_id_type=MESH,
+        )
+
+    def join_heads(m):
+        own = sets[m][0]
+        inner = kept[4].shape[1]
+
+        def place_of(index):
+            return pl.ds(pl.multiple_of(index * inner, inner), inner)
+
+        rows = pl.ds(pl.multiple_of(core * half, half), half)
+        heads_full[:, place_of(tensor)] = heads_wide[m][rows, :].astype(jnp.bfloat16)
+        for index, peer in enumerate((core_peer, far_peer, diagonal)):
+            heads_copy(m, index).wait()
+            heads_full[:, place_of(peer)] = heads_landed[m][index].astype(jnp.bfloat16)
+
+        def block(i, carry):
+            at = pl.ds(pl.multiple_of(i * 512, 512), 512)
+            values = rows_in[m][rows, at].astype(jnp.float32)
+            own[:, at] = values + f32_dot(heads_full[...], full_weight[:, at])
+            return carry
+
+        lax.fori_loop(0, depth // 512, block, 0)
+
+    def attend(m, between):
         rows_loads[m].wait()
-        if m == 0:
-            wait_all(weight_loads)
+        wait_all(weight_loads)
+        wait_all(out_loads)
         forward_kernel(
-            lam, rows_in[m], gain_one, *weights[:3], *tables[m], sub_scale, normed_one, *kept[m]
-        )
-        heads = kept[m][4]
+            lam, rows_in[m], gain_one, *weights[:3], *tables[m], sub_scale, normed_one, *kept,
+            between,
+        )
+        heads = kept[4]
+        if gathers:
+            if m == 0:
+                gather.forward(0)
+            heads_wide[m][...] = heads[...].astype(jnp.float32)
+            for index in range(3):
+                heads_copy(m, index).start()
+            out_loads.extend(load(*pair) for pair in zip(kept, outs[m][3:8]))
+            flip_to(normed_one, outs[m][2])
+            return
 
         def part(which, target):
             rows = pl.ds(pl.multiple_of(which * half, half), half)
@@ -1104,38 +1341,48 @@
         part(1 - core, projected)
         sums[m].near_start(projected)
         part(core, sets[m][0])
-        out_loads.extend(load(*pair) for pair in zip(kept[m], outs[m][3:8]))
+        out_loads.extend(load(*pair) for pair in zip(kept, outs[m][3:8]))
         flip_to(normed_one, outs[m][2])
         sums[m].near_add()
 
-    def norm_rows(rows, values):
+    def norm_rows(values):
         return (values * root_of(values) * gain_two[...]).astype(jnp.bfloat16)
 
     def join(m):
-        own, near, far = sets[m]
-
-        def add(rows):
-            values = rows_in[m][mine(rows), :].astype(jnp.float32)
-            own[rows, :] = values + (own[rows, :] + far[rows, :])
-
-        def norm_mine(rows):
-            normed_two[mine(rows), :] = norm_rows(rows, own[rows, :])
-
-        def norm_others(rows):
-            normed_two[others(rows), :] = norm_rows(rows, near[rows, :])
-
-        for_rows(half, add)
+        own = sets[m][0]
+        if gathers:
+            join_heads(m)
+        else:
+            far = sets[m][2]
+
+            def add(rows):
+                values = rows_in[m][mine(rows), :].astype(jnp.float32)
+                own[rows, :] = values + (own[rows, :] + far[rows, :])
+
+            for_rows(half, add)
         sums[m].near_start(own)
         out_loads.append(load(own, outs[m][8]))
+
+    def norm(m):
+        own, near = sets[m][:2]
+
+        def norm_mine(rows):
+            normed_two[mine(rows), :] = norm_rows(own[rows, :])
+
+        def norm_others(rows):
+            normed_two[others(rows), :] = norm_rows(near[rows, :])
+
         for_rows(half, norm_mine)
         sums[m].near_wait()
         for_rows(half, norm_others)
         sums[m].near_free()
+        flip_to(normed_two, outs[m][1])
 
     def feed(m):
-        inside, gate_pre, up_pre = hidden[m]
+        inside, gate_pre, up_pre = hidden
         if m == 0:
             wait_all(wide_loads)
+        wait_all(hidden_outs)
 
         def block(j, carry):
             at = pl.ds(pl.multiple_of(j * 256, 256), 256)
@@ -1151,7 +1398,7 @@
             return carry
 
         lax.fori_loop(0, hidden_count // 256, block, 0)
-        out_loads.extend(load(*pair) for pair in zip(hidden[m], outs[m][9:12]))
+        hidden_outs.extend(load(*pair) for pair in zip(hidden, outs[m][9:12]))
         wait_all(wide_outs)
 
         def through(i, carry):
@@ -1165,27 +1412,46 @@
         lax.fori_loop(0, depth // 512, through, 0)
         wide_outs.extend([load(back, outs[m][12]), load(fed, outs[m][13])])
 
-    attend(0)
-    sums[0].far_go()
-    attend(1)
-    for m in range(2):
+    def flip_cot(m):
         cot_loads[m].wait()
         flip_to(cot_rows[m], outs[m][0])
-    sums[0].far_wait()
-    sums[1].far_go()
+
+    if gathers:
+        wait_all(weight_loads)
+        gather.begin()
+        attend(0, {})
+        attend(1, {2: lambda: gather.forward(1)})
+        flip_cot(0)
+        gather.forward(2)
+        flip_cot(1)
+        gather.forward(3)
+        gather.finish_line()
+        gather.finish()
+    else:
+        attend(0, {})
+        sums[0].far_go()
+        attend(1, {})
+        flip_cot(0)
+        flip_cot(1)
+        sums[0].far_wait()
+        sums[1].far_go()
     join(0)
+    if gathers:
+        join(1)
+    norm(0)
     feed(0)
-    flip_to(normed_two, outs[0][1])
-    sums[1].far_wait()
-    join(1)
+    if not gathers:
+        sums[1].far_wait()
+        join(1)
+    norm(1)
     feed(1)
-    flip_to(normed_two, outs[1][1])
     wait_all(flip_loads)
+    wait_all(hidden_outs)
     wait_all(wide_outs)
     wait_all(out_loads)
 
 
-def front_call(lam, arrays, blocks, shapes):
+def front_call(dp_count, lam, arrays, blocks, shapes):
     depth, row_count, inner, hidden_count = shapes[:4]
     bf16, f32 = jnp.bfloat16, jnp.float32
     dma, regular = pltpu.SemaphoreType.DMA, pltpu.SemaphoreType.REGULAR
@@ -1202,8 +1468,29 @@
     wide_rows = pltpu.VMEM((row_count, depth), bf16)
     narrow = pltpu.VMEM((row_count, inner), bf16)
     wide_half = pltpu.VMEM((half, depth), f32)
+    if gathers_heads(dp_count):
+        steps = dp_count // 2 - 1
+        extra = [wide_half] * 4
+        extra += [pltpu.VMEM((row_count, inner), f32)] * 2
+        extra += [pltpu.VMEM((3, half, inner), f32)] * 2
+        extra += [
+            pltpu.VMEM((half, depth), bf16),
+            pltpu.VMEM((inner // dp_count, depth), f32),
+            pltpu.VMEM((inner, depth), f32),
+            pltpu.VMEM((inner, depth), f32),
+            pltpu.VMEM((depth, depth), bf16),
+            dma((2, 2, 3)),
+            dma((2,)),
+            dma((2, steps)),
+            dma((2, steps)),
+            dma((1 + 2 * steps,)),
+            dma((1 + 2 * steps,)),
+            dma((2, 3)),
+        ]
+    else:
+        extra = [wide_half] * 7 + [dma((2, 2)), regular((2,))]
     return pl.pallas_call(
-        front_kernel,
+        functools.partial(front_kernel, dp_count),
         out_shape=out_shape,
         in_specs=[pl.BlockSpec(memory_space=pltpu.SMEM)]
         + [pl.BlockSpec(memory_space=pl.ANY)] * len(arrays)
@@ -1215,11 +1502,11 @@
         + [pltpu.VMEM((inner, depth), bf16)]
         + [pltpu.VMEM((depth, hidden_count), bf16)] * 2
         + [pltpu.VMEM((hidden_count, depth), bf16)]
-        + [narrow, narrow, narrow, pltpu.VMEM((row_count, inner), f32), narrow] * 2
-        + [wide_half] * 7
-        + [pltpu.VMEM((row_count, hidden_count), bf16)] * 6
+        + [narrow, narrow, narrow, pltpu.VMEM((row_count, inner), f32), narrow]
+        + [pltpu.VMEM((row_count, hidden_count), bf16)] * 3
         + [pltpu.VMEM((row_count, depth), f32)] * 2
-        + [dma((2, 2)), dma((2, 2)), regular((2,)), dma((64,))],
+        + [dma((2, 2)), dma((64,))]
+        + extra,
         compiler_params=pltpu.CompilerParams(
             collective_id=1, has_side_effects=True, vmem_limit_bytes=62 * 1024 * 1024
         ),
@@ -1271,7 +1558,7 @@
     blocks = [*tables[0], *tables[1], sub_scale, norm1_gain[None, :], norm2_gain[None, :]]
     arrays = [layer_in, out_cotangent, *projections, out_weight]
     arrays += [gate_weight, up_weight, down_weight]
-    parts = front_call(lam, arrays, blocks, shapes)
+    parts = front_call(dp_count, lam, arrays, blocks, shapes)
     pick = lambda at: [parts[at], parts[at + 14]]
     arrays = pick(0) + pick(1) + pick(2) + pick(9) + pick(10) + pick(11) + pick(7)
     arrays += pick(12) + pick(13) + pick(8)

time: 456 us -> 428 us (0.939)
  Pallas kernels: 419 us -> 395 us
    pallas_call x1, Pallas kernels: 109 us -> 87.3 us  [front_call(): pl.pallas_call(functools.partial(front_kernel, dp_count), out_shape=out_s...]
where the time goes in v7:
time: 428 us; the launch traced here: 424 us
  Pallas kernels  395 us (92%)
  local copies, waits for them, and re-layouts  17.8 us (4%)
  other arithmetic  11.1 us (3%)
    pallas_call x1, Pallas kernels, back_call(): pl.pallas_call(functools.partial(back_kernel, dp_count), out_shape=[grad(...  307 us
    pallas_call x1, Pallas kernels, front_call(): pl.pallas_call(functools.partial(front_kernel, dp_count), out_shape=out_s...  87.3 us
    unnamed x27, local copies, waits for them, and re-layouts  9.06 us

profile of v7, /device:TPU:0, one launch (start us, length us, event | category | flops | bytes accessed | tf_op | source)
XLA Modules:
  0.0 424.5 jit_solution(1680228985701218181)
XLA Ops:
  0.7 0.8 reshape.124
  2.2 0.8 reduce-window.17
  3.1 0.7 convert_reduce_fusion
  3.8 0.8 reduce-window.16
  4.7 0.7 convert_reduce_fusion.1
  5.4 1.9 fusion.1
  7.3 1.0 pad_maximum_fusion.3.refs_15_.refs_40_
  8.3 1.0 pad_maximum_fusion.1.refs_11_.refs_36_
  9.3 1.0 pad_maximum_fusion.refs_10_.refs_35_
  10.3 1.0 pad_maximum_fusion.2.refs_14_.refs_39_
  11.2 0.9 copy.50.refs_12_.refs_37_
  12.1 0.9 copy.51.refs_16_.refs_41_
  14.8 87.3 %shard_map.246 = (bf16[1536,512]{1,0:T(8,128)(2,1)}, bf16[1536,512]{1,0:T(8,128)(2,1)}, bf16[1536,512]{1,0:T(8,128)(2,1)}, bf16[512,384]{1,0:T(8,128)(2,1)}, bf1...) custom-call(f32[3]{0:T(128)} %subtract_add_fusion.refs_0_, ...), custom_call_target="tpu_custom_call" | custom-call | flops 24159191040 | bytes 67108864 | tf_op jit(solution)/shard_map/pallas_call | solution.py:1492
  102.0 307.3 %shard_map.247 = (f32[192,1024]{1,0:T(8,128)}, f32[192,1024]{1,0:T(8,128)}, f32[192,1024]{1,0:T(8,128)}, f32[192,384]{1,0:T(8,128)}, f32[192,1152]{1,0:T(8,128)}...) custom-call(f32[3]{0:T(128)} %subtract_add_fusion.refs_0_, ...), custom_call_target="tpu_custom_call" | custom-call | flops 19327352832 | bytes 67108864 | tf_op jit(solution)/shard_map/pallas_call | solution.py:944
  409.4 0.8 slice_reduce_fusion
  410.4 0.7 fusion.4
  411.0 0.9 fusion.16
  412.6 2.1 fusion.15
  415.3 3.9 copy.87
  419.2 1.7 copy.88
  420.9 0.7 copy.89
  421.6 0.9 copy.90
  422.5 0.9 copy.91
  423.4 0.9 copy.92
  (35 shorter events, 4.1 us)
Async XLA Ops:
  0.6 12.3 %copy-start.7 = (f32[1536]{0:T(1024)S(1)}, f32[1536]{0:T(1024)}, u32[]{:S(2)}) copy-start(f32[1536]{0:T(1024)} %param.18) | copy-start | bytes 18436
  0.7 12.9 %copy-start.8 = (f32[1536]{0:T(1024)S(1)}, f32[1536]{0:T(1024)}, u32[]{:S(2)}) copy-start(f32[1536]{0:T(1024)} %param.25) | copy-start | bytes 18436
  0.7 13.5 %copy-start.9 = (f32[3,128]{1,0:T(4,128)S(1)}, f32[3,128]{1,0:T(4,128)}, u32[]{:S(2)}) copy-start(f32[3,128]{1,0:T(4,128)} %param.23) | copy-start | bytes 4612
  3.8 11.0 %copy-start.5 = (s32[512]{0:T(512)}, s32[512]{0:T(512)S(1)}, u32[]{:S(2)}) copy-start(s32[512]{0:T(512)S(1)} %get-tuple-element.87) | copy-start | bytes 6148
  5.4 9.4 %copy-start.6 = (s32[512]{0:T(512)}, s32[512]{0:T(512)S(1)}, u32[]{:S(2)}) copy-start(s32[512]{0:T(512)S(1)} %get-tuple-element.89) | copy-start | bytes 6148
  415.3 3.9 copy-start
  419.2 1.7 copy-start.4
  419.2 2.4 copy-start.3
  419.2 3.3 copy-start.2
  420.9 2.5 copy-start.1

commit v8 on v7

--- a/solution.py
+++ b/solution.py
@@ -20,24 +20,60 @@
 MESH = pl.DeviceIdType.MESH
 
 
-def doc_tables(lengths, row_count):
-    doc_ends = jnp.cumsum(lengths, dtype=jnp.int32)
-    places = jnp.arange(row_count, dtype=jnp.int32)
-    passed = (places[:, None] >= doc_ends[None, :]).astype(jnp.int32)
-    segment = jnp.sum(passed, axis=1, dtype=jnp.int32)
-    starts = jnp.sum(passed * lengths[None, :], axis=1, dtype=jnp.int32)
-    return (places - starts, segment)
-
-
-def rotary_tables(position, map_width):
+def documents(lengths, places):
+    end, segment, start = 0, 0, 0
+    for k in range(lengths.shape[1]):
+        length = lengths[0, k]
+        end = end + length
+        passed = (places >= end).astype(jnp.int32)
+        segment = segment + passed
+        start = start + passed * length
+    return segment, start
+
+
+def segments(lengths, column, row):
+    column[...] = documents(lengths, lax.broadcasted_iota(jnp.int32, column.shape, 0))[0]
+    row[...] = documents(lengths, lax.broadcasted_iota(jnp.int32, row.shape, 1))[0]
+
+
+def rotary_tables(lengths, cosines, sines, map_width):
     half_width = map_width // 2
-    frequency = rotary_base ** (-2.0 * jnp.arange(half_width, dtype=jnp.float32) / map_width)
-    angles = position.astype(jnp.float32)[:, None] * frequency[None, :]
-    cosine, sine = jnp.cos(angles), jnp.sin(angles)
-    return (
-        jnp.concatenate([cosine] * 4, axis=1),
-        jnp.concatenate([-sine, sine, -sine, sine], axis=1),
-    )
+    row_count, width = cosines[0].shape
+    lane = lax.broadcasted_iota(jnp.int32, (block_rows, width), 1)
+    frequency = jnp.zeros((block_rows, width), jnp.float32)
+    for k in range(half_width):
+        value = rotary_base ** (-2.0 * k / map_width)
+        frequency = jnp.where(lane % half_width == k, value, frequency)
+
+    def block(i, carry):
+        rows = pl.ds(pl.multiple_of(i * block_rows, block_rows), block_rows)
+        places = lax.broadcasted_iota(jnp.int32, (block_rows, width), 0) + i * block_rows
+        starts = [documents(item, places)[1] for item in lengths]
+        start = jnp.where(lane < half_width, starts[0], starts[1])
+        angles = (places - start).astype(jnp.float32) * frequency
+
+        def spread(values, m):
+            base = jnp.where(lane // half_width == m, values, 0.0)
+            return sum(
+                (pltpu.roll(base, k * half_width, 1) for k in range(1, width // half_width)), base
+            )
+
+        cosine, sine = jnp.cos(angles), jnp.sin(angles)
+        for m in range(2):
+            cosines[m][rows, :] = spread(cosine, m)
+            signed = spread(sine, m)
+            sines[m][rows, :] = jnp.where(lane % map_width < half_width, -signed, signed)
+        return carry
+
+    lax.fori_loop(0, row_count // block_rows, block, 0)
+
+
+def lambda_terms(param):
+    width = param.shape[1] // 4
+    part = lambda k: param[:, k * width : (k + 1) * width]
+    first = jnp.exp(jnp.sum(part(0) * part(1), axis=-1, keepdims=True))
+    second = jnp.exp(jnp.sum(part(2) * part(3), axis=-1, keepdims=True))
+    return first, second, first - second + lambda_base
 
 
 def turn(values, cosine, sine):
@@ -129,7 +165,7 @@
             at = slice(head * width, (head + 1) * width)
             keys = key[first:last, at]
             maps = [softmax_map(map_of(query[here, at], c), keys, opened, scale) for c in range(2)]
-            combined = (maps[0] - lam[head] * maps[1]).astype(jnp.bfloat16)
+            combined = (maps[0] - lam[head : head + 1, :] * maps[1]).astype(jnp.bfloat16)
             out = f32_dot(combined, value[first:last, at])
             mixed[here, at] = out
             heads_out[here, at] = (out * root_of(out) * sub_scale[head : head + 1, :]).astype(
@@ -171,7 +207,7 @@
             queries = [map_of(query[here, at], c) for c in range(2)]
             maps = [softmax_map(queries[c], keys, opened, scale) for c in range(2)]
             mixes = grad_mixed[here, at]
-            combined = (maps[0] - lam[head] * maps[1]).astype(jnp.bfloat16)
+            combined = (maps[0] - lam[head : head + 1, :] * maps[1]).astype(jnp.bfloat16)
             grad_value[first:last, at] += dot_rows(combined, mixes)
             grads = dot_t(mixes, value[first:last, at])
             first_sum = jnp.sum(grads * maps[0], axis=-1, keepdims=True)
@@ -179,7 +215,7 @@
             lam_sums[head] = lam_sums[head] + jnp.sum(second_sum, axis=0, keepdims=True)
             score_grads = [
                 (maps[0] * (grads - first_sum)).astype(jnp.bfloat16),
-                (maps[1] * (-lam[head] * (grads - second_sum))).astype(jnp.bfloat16),
+                (maps[1] * (-lam[head : head + 1, :] * (grads - second_sum))).astype(jnp.bfloat16),
             ]
             grad_query = f32_dot(score_grads[0], map_of(keys, 0)) + f32_dot(
                 score_grads[1], map_of(keys, 1)
@@ -398,13 +434,28 @@
         lax.fori_loop(0, self.line, block, 0)
         self.pair_copy(c).wait_send()
 
-    def out_copy(self, c):
+    def out_copies(self, c):
         item = self.plan[c]
-        return pltpu.make_async_copy(
-            self.total.at[c % self.ring, self.place, :, : item.width],
-            item.out.at[:, item.first : item.first + item.width],
-            self.out_sem.at[c % self.ring],
-        )
+        outs = item.out if isinstance(item.out, list) else [item.out]
+        size = outs[0].shape[1]
+        first, last = item.first, item.first + item.width
+        while first < last:
+            count = min(last, (first // size + 1) * size) - first
+            at = first - item.first
+            yield pltpu.make_async_copy(
+                self.total.at[c % self.ring, self.place, :, at : at + count],
+                outs[first // size].at[:, first % size : first % size + count],
+                self.out_sem.at[c % self.ring, at // 128],
+            )
+            first += count
+
+    def out_start(self, c):
+        for copy in self.out_copies(c):
+            copy.start()
+
+    def out_wait(self, c):
+        for copy in self.out_copies(c):
+            copy.wait()
 
     def run(self, tasks):
         count, steps = len(self.plan), self.steps
@@ -431,10 +482,10 @@
                 self.pair_copy(slot + 1).start()
             done = slot - 1 - steps
             if 0 <= done < count:
-                self.out_copy(done).start()
+                self.out_start(done)
             if slot + 2 < count:
                 if slot + 2 >= self.ring:
-                    self.out_copy(slot + 2 - self.ring).wait()
+                    self.out_wait(slot + 2 - self.ring)
                 self.compute(slot + 2)
             for c, start in enumerate(self.line_starts):
                 if slot and start == slot + 1:
@@ -442,7 +493,7 @@
             for task in tasks.get(slot, ()):
                 task()
         for c in range(max(0, count - self.ring), count):
-            self.out_copy(c).wait()
+            self.out_wait(c)
         if self.line_plan:
             for c in range(len(self.line_plan) - self.line_total.shape[0], len(self.line_plan)):
                 self.line_result(c).wait()
@@ -537,16 +588,19 @@
 def back_kernel(dp_count, *refs):
     refs = list(refs)
     take = lambda n: [refs.pop(0) for _ in range(n)]
-    (lam,) = take(1)
+    lengths = take(2)
     cot_left, two_left, one_left = [take(2) for _ in range(3)]
     hidden, gate_pre, up_pre, heads = [take(2) for _ in range(4)]
     part_back, part_fed, middle = [take(2) for _ in range(3)]
     (layer_in, cotangent) = take(2)
     weights_in = take(4)
     kept_in = [take(4) for _ in range(2)]
-    tables = [take(4) for _ in range(2)]
-    (sub_scale, gain_one, gain_two) = take(3)
-    (grad_down, grad_gate, grad_up, grad_out, grad_qkv, layer_out, grad_in, small_out) = take(8)
+    tables_in = [take(2) for _ in range(2)]
+    (lambda_param, sub_gain, gain_one, gain_two) = take(4)
+    (grad_down, grad_gate, grad_up, grad_out) = take(4)
+    grad_qkv = take(3)
+    (layer_out, grad_in) = take(2)
+    small_outs = take(4)
     reducer_refs = take(20 if line_first(dp_count)[0] else 10)
     line_rights = reducer_refs.pop() if line_first(dp_count)[0] else None
     (left_a, left_b, rights, rows_qkv) = take(4)
@@ -558,6 +612,8 @@
     through = take(2)
     (spare, projected, attended, rows_in, rows_out) = take(5)
     (small, small_near, small_landed) = take(3)
+    small_blocks = take(4)
+    tables = take(4)
     (near_sems, far_sems, near_credit, far_credit) = take(4)
     (load_sems, small_near_sems, small_send, small_recv) = take(4)
     assert not refs
@@ -570,7 +626,9 @@
     line = dp_count // 2
     half = middle[0].shape[0]
     row_count = 2 * half
-    head_count, head_width = sub_scale.shape
+    head_count, head_width = sub_gain.shape
+    sub_scale = sub_gain[...] * (1.0 - lambda_base)
+    first_exp, second_exp, lam = lambda_terms(lambda_param)
     out_weight, projections = weights[0], weights[1:]
     inner = out_weight.shape[0]
     kept_half = pl.ds(pl.multiple_of(core * half, half), half)
@@ -697,7 +755,11 @@
     ]
     own_loads = {m: load(part_back[m].at[kept_half], sets[m][0]) for m in range(2)}
     weight_loads = [load(*pair) for pair in zip(weights_in, weights)]
-    kept_loads = [load(*pair) for pair in zip(kept_in[0], kept)]
+    def load_kept(m):
+        pairs = zip([*kept_in[m], *tables_in[m]], [*kept, *tables[:2]])
+        return [load(*pair) for pair in pairs]
+
+    kept_loads = load_kept(0)
     spare_queue = [middle[0], middle[1], middle[0], middle[1]]
     rows_queue = [cotangent.at[0], cotangent.at[1]]
     rows_queue += [layer_in.at[0], cotangent.at[0], layer_in.at[1], cotangent.at[1]]
@@ -769,12 +831,13 @@
         if m == 0:
             wait_all(weight_loads)
         wait_all(kept_loads)
+        segments(lengths[m], *tables[2:])
         backward_kernel(
-            lam, attended, out_weight, *kept, *tables[m], sub_scale,
+            lam, attended, out_weight, *kept, *tables, sub_scale,
             rows_qkv.at[tokens[m], :], grad_sub, grad_lam, *backward_scratch,
         )
         if m == 0:
-            kept_loads[:] = [load(*pair) for pair in zip(kept_in[1], kept)]
+            kept_loads[:] = load_kept(1)
         for head in range(head_count):
             at = slice(head * head_width, (head + 1) * head_width)
             small[2:3, at] += grad_sub[head : head + 1, :]
@@ -892,8 +955,35 @@
         total = small[...]
         for offset in range(1, dp_count):
             total = total + small_landed[offset - 1]
-        small_near[...] = total
-        out_loads.append(load(small_near, small_out))
+
+        def own_block(values, target):
+            count = target.shape[1]
+            shift = lax.rem((dp_count - me) * count, count * dp_count)
+            return pltpu.roll(values, shift, 1)[: target.shape[0], :count]
+
+        norm_blocks, lambda_block, sub_block = small_blocks[:2], small_blocks[2], small_blocks[3]
+        for row in range(2):
+            norm_blocks[row][...] = own_block(total, norm_blocks[row][...])
+            total = pltpu.roll(total, 7, 0)
+        total = pltpu.roll(total, 2, 0)
+        part = head_width // 2
+        for head in range(head_count):
+            at = slice(head * head_width, (head + 1) * head_width)
+            sub_block[head : head + 1, :] = own_block(
+                jnp.broadcast_to(total[2:3, at], (8, head_width)), sub_block[0:1, :]
+            )
+            grad = total[3:4, head * head_width : head * head_width + 1]
+            param = lambda_param[head : head + 1, :]
+            first = grad * first_exp[head : head + 1, :]
+            second = grad * second_exp[head : head + 1, :]
+            piece = lambda k: param[:, k * part : (k + 1) * part]
+            full = jnp.concatenate(
+                [first * piece(1), first * piece(0), -second * piece(3), -second * piece(2)], axis=1
+            )
+            lambda_block[head : head + 1, :] = own_block(
+                jnp.broadcast_to(full, (8, 4 * part)), lambda_block[0:1, :]
+            )
+        out_loads.extend(load(*pair) for pair in zip(small_blocks, small_outs))
 
     order = {
         0: [lambda: exchange(0)],
@@ -922,7 +1012,7 @@
     wait_all(out_loads)
 
 
-def back_call(dp_count, lam, arrays, blocks, shapes):
+def back_call(dp_count, lengths, arrays, blocks, shapes):
     depth, row_count, inner, hidden_count, head_count, head_width = shapes
     line = dp_count // 2
     rows = depth // dp_count
@@ -940,16 +1030,20 @@
     small = pltpu.VMEM((8, depth), f32)
     grad = lambda columns: jax.ShapeDtypeStruct((rows, columns), f32)
     rows_shape = jax.ShapeDtypeStruct((2, row_count, depth), bf16)
+    small_shapes = [jax.ShapeDtypeStruct((1, rows), f32)] * 2
+    for count in (2 * head_width, head_width):
+        small_shapes.append(jax.ShapeDtypeStruct((head_count, count // dp_count), f32))
     flops = 2 * 2 * row_count * depth * (3 * hidden_count + 8 * inner)
     return pl.pallas_call(
         functools.partial(back_kernel, dp_count),
         out_shape=[grad(hidden_count)] * 3
-        + [grad(inner), grad(3 * inner), rows_shape, rows_shape]
-        + [jax.ShapeDtypeStruct((8, depth), f32)],
-        in_specs=[pl.BlockSpec(memory_space=pltpu.SMEM)]
+        + [grad(inner)] * 4
+        + [rows_shape] * 2
+        + small_shapes,
+        in_specs=[pl.BlockSpec(memory_space=pltpu.SMEM)] * 2
         + [pl.BlockSpec(memory_space=pl.ANY)] * len(arrays)
         + in_vmem(len(blocks)),
-        out_specs=[pl.BlockSpec(memory_space=pl.ANY)] * 8,
+        out_specs=[pl.BlockSpec(memory_space=pl.ANY)] * 13,
         scratch_shapes=[
             pltpu.VMEM((send_slots,) + wide, f32),
             pltpu.VMEM((held_slots,) + wide, f32),
@@ -960,7 +1054,7 @@
             dma((2, line - 1, 2)),
             dma((2, line - 1, 2)),
             regular((2, line - 1)),
-            dma((ring,)),
+            dma((ring, 2)),
         ]
         + (
             [
@@ -995,6 +1089,11 @@
             small,
             small,
             pltpu.VMEM((dp_count - 1, 8, depth), f32),
+            *[pltpu.VMEM(item.shape, f32) for item in small_shapes],
+            pltpu.VMEM((row_count, head_width), f32),
+            pltpu.VMEM((row_count, head_width), f32),
+            pltpu.VMEM((row_count, 1), jnp.int32),
+            pltpu.VMEM((1, row_count), jnp.int32),
             dma((2, 2)),
             dma((2, 2)),
             regular((2,)),
@@ -1008,7 +1107,7 @@
             collective_id=0, has_side_effects=True, vmem_limit_bytes=62 * 1024 * 1024
         ),
         cost_estimate=pl.CostEstimate(flops=flops, bytes_accessed=64 << 20, transcendentals=0),
-    )(lam, *arrays, *blocks)
+    )(*lengths, *arrays, *blocks)
 
 
 def gathers_heads(dp_count):
@@ -1185,12 +1284,13 @@
 def front_kernel(dp_count, *refs):
     refs = list(refs)
     take = lambda n: [refs.pop(0) for _ in range(n)]
-    (lam,) = take(1)
+    lengths = take(2)
     layer_in, cotangent = take(2)
     weights_in = take(7)
-    tables = [take(4) for _ in range(2)]
-    (sub_scale, gain_one, gain_two) = take(3)
-    outs = [take(14) for _ in range(2)]
+    (lambda_param, sub_gain, gain_one, gain_two) = take(4)
+    outs = [take(16) for _ in range(2)]
+    cosines, sines = take(2), take(2)
+    (segment_column, segment_row) = take(2)
     rows_in, cot_rows = take(2), take(2)
     (normed_one, normed_two, flipped) = take(3)
     weights = take(7)
@@ -1234,6 +1334,8 @@
     cot_loads = [load(cotangent.at[m], cot_rows[m]) for m in range(2)]
     wide_loads = [load(*pair) for pair in zip(weights_in[4:], weights[4:])]
 
+    sub_scale = sub_gain[...] * (1.0 - lambda_base)
+    lam = lambda_terms(lambda_param)[2]
     barrier = pltpu.get_barrier_semaphore()
     core_peer, far_peer = tensor + 1 - 2 * core, tensor + 2 - 4 * (tensor // 2)
     diagonal = far_peer + 1 - 2 * core
@@ -1259,6 +1361,7 @@
             TensorSum(1, *sets[m], near_sems.at[m], far_sems.at[m], near_credit.at[m], None)
             for m in range(2)
         ]
+    rotary_tables(lengths, cosines, sines, lambda_param.shape[1] // 4)
     out_loads, flip_loads, wide_outs, hidden_outs = [], [], [], []
 
     def mine(rows):
@@ -1313,8 +1416,11 @@
         rows_loads[m].wait()
         wait_all(weight_loads)
         wait_all(out_loads)
+        segments(lengths[m], segment_column, segment_row)
+        out_loads.extend([load(cosines[m], outs[m][14]), load(sines[m], outs[m][15])])
         forward_kernel(
-            lam, rows_in[m], gain_one, *weights[:3], *tables[m], sub_scale, normed_one, *kept,
+            lam, rows_in[m], gain_one, *weights[:3], cosines[m], sines[m], segment_column,
+            segment_row, sub_scale, normed_one, *kept,
             between,
         )
         heads = kept[4]
@@ -1451,8 +1557,8 @@
     wait_all(out_loads)
 
 
-def front_call(dp_count, lam, arrays, blocks, shapes):
-    depth, row_count, inner, hidden_count = shapes[:4]
+def front_call(dp_count, lengths, arrays, blocks, shapes):
+    depth, row_count, inner, hidden_count, head_count, head_width = shapes
     bf16, f32 = jnp.bfloat16, jnp.float32
     dma, regular = pltpu.SemaphoreType.DMA, pltpu.SemaphoreType.REGULAR
     half = row_count // 2
@@ -1465,6 +1571,7 @@
         out_shape += [jax.ShapeDtypeStruct((half, depth), f32)]
         out_shape += [jax.ShapeDtypeStruct((row_count, hidden_count), bf16)] * 3
         out_shape += [jax.ShapeDtypeStruct((row_count, depth), f32)] * 2
+        out_shape += [jax.ShapeDtypeStruct((row_count, head_width), f32)] * 2
     wide_rows = pltpu.VMEM((row_count, depth), bf16)
     narrow = pltpu.VMEM((row_count, inner), bf16)
     wide_half = pltpu.VMEM((half, depth), f32)
@@ -1492,11 +1599,13 @@
     return pl.pallas_call(
         functools.partial(front_kernel, dp_count),
         out_shape=out_shape,
-        in_specs=[pl.BlockSpec(memory_space=pltpu.SMEM)]
+        in_specs=[pl.BlockSpec(memory_space=pltpu.SMEM)] * 2
         + [pl.BlockSpec(memory_space=pl.ANY)] * len(arrays)
         + in_vmem(len(blocks)),
         out_specs=[pl.BlockSpec(memory_space=pl.ANY)] * len(out_shape),
-        scratch_shapes=[wide_rows] * 6
+        scratch_shapes=[pltpu.VMEM((row_count, head_width), f32)] * 4
+        + [pltpu.VMEM((row_count, 1), jnp.int32), pltpu.VMEM((1, row_count), jnp.int32)]
+        + [wide_rows] * 6
         + [pltpu.VMEM((depth, row_count), bf16)]
         + [pltpu.VMEM((depth, inner), bf16)] * 3
         + [pltpu.VMEM((inner, depth), bf16)]
@@ -1515,7 +1624,7 @@
             bytes_accessed=64 << 20,
             transcendentals=0,
         ),
-    )(lam, *arrays, *blocks)
+    )(*lengths, *arrays, *blocks)
 
 
 def on_device(
@@ -1536,68 +1645,34 @@
     out_cotangent,
 ):
     dp_count = lax.axis_size("dp")
-    head_count, lambda_width = lambda_param.shape
-    doc_lengths = (short_lengths[0], long_lengths[0])
-    map_width = lambda_width // 4
-    projections = (query_weight, key_weight, value_weight)
-    lambda_parts = lambda_param.reshape(head_count, 4, map_width)
-    first_exp = jnp.exp(jnp.sum(lambda_parts[:, 0] * lambda_parts[:, 1], axis=-1))
-    second_exp = jnp.exp(jnp.sum(lambda_parts[:, 2] * lambda_parts[:, 3], axis=-1))
-    lam = first_exp - second_exp + lambda_base
-    sub_scale = sub_gain * (1.0 - lambda_base)
-    tables = []
-    for m in range(2):
-        position, segment = doc_tables(doc_lengths[m], layer_in.shape[1])
-        tables.append(
-            rotary_tables(position, map_width) + (segment[:, None], segment[None, :])
-        )
+    projections = [query_weight, key_weight, value_weight]
     depth, inner = query_weight.shape
-    shapes = (
-        depth, layer_in.shape[1], inner, gate_weight.shape[1], head_count, sub_gain.shape[1],
-    )
-    blocks = [*tables[0], *tables[1], sub_scale, norm1_gain[None, :], norm2_gain[None, :]]
+    shapes = (depth, layer_in.shape[1], inner, gate_weight.shape[1], *sub_gain.shape)
+    lengths = [short_lengths, long_lengths]
+    blocks = [lambda_param, sub_gain, norm1_gain[None, :], norm2_gain[None, :]]
     arrays = [layer_in, out_cotangent, *projections, out_weight]
     arrays += [gate_weight, up_weight, down_weight]
-    parts = front_call(dp_count, lam, arrays, blocks, shapes)
-    pick = lambda at: [parts[at], parts[at + 14]]
+    parts = front_call(dp_count, lengths, arrays, blocks, shapes)
+    pick = lambda at: [parts[at], parts[at + 16]]
     arrays = pick(0) + pick(1) + pick(2) + pick(9) + pick(10) + pick(11) + pick(7)
     arrays += pick(12) + pick(13) + pick(8)
     arrays += [layer_in, out_cotangent, out_weight, *projections]
-    arrays += parts[3:7] + parts[17:21]
-    grad_down, grad_gate, grad_up, grad_out, grad_qkv, layer_out, grad_in, small = back_call(
-        dp_count, lam, arrays, blocks, shapes
-    )
-    grad_query, grad_key, grad_value = jnp.split(grad_qkv, 3, axis=1)
-    per_head = lambda row: row[:inner].reshape(head_count, -1)
-    grad_lam = per_head(small[3])[:, :1]
-    first_scale = grad_lam * first_exp[:, None]
-    second_scale = grad_lam * second_exp[:, None]
-    lambda_grad = jnp.concatenate(
-        [
-            first_scale * lambda_parts[:, 1],
-            first_scale * lambda_parts[:, 0],
-            -second_scale * lambda_parts[:, 3],
-            -second_scale * lambda_parts[:, 2],
-        ],
-        axis=1,
-    )
-    index = lax.axis_index("dp")
-
-    def block_of(values):
-        size = values.shape[-1] // dp_count
-        return lax.dynamic_slice_in_dim(values, index * size, size, values.ndim - 1)
-
+    arrays += parts[3:7] + parts[19:23] + parts[14:16] + parts[30:32]
+    (
+        grad_down, grad_gate, grad_up, grad_out, grad_query, grad_key, grad_value, layer_out,
+        grad_in, grad_norm1, grad_norm2, grad_lambda, grad_sub,
+    ) = back_call(dp_count, lengths, arrays, blocks, shapes)
     return (
         layer_out,
         grad_in,
-        block_of(small[0]),
+        grad_norm1.reshape(-1),
         grad_query,
         grad_key,
         grad_value,
-        block_of(lambda_grad),
-        block_of(per_head(small[2])),
+        grad_lambda,
+        grad_sub,
         grad_out.T,
-        block_of(small[1]),
+        grad_norm2.reshape(-1),
         grad_gate,
         grad_up,
         grad_down.T,

time: 428 us -> 417 us (0.974)
  other arithmetic: 11.1 us -> 0 us
    concatenate x5 -> x0, other arithmetic: 4.57 us -> none  [the longest x2 1.95 us: rotary_tables(): jnp.concatenate([-sine, sine, -sine, sine], axis=1)]
    unnamed x27 -> x37, local copies, waits for them, and re-layouts: 9.06 us -> 13.4 us
where the time goes in v8:
time: 417 us; the launch traced here: 411 us
  Pallas kernels  394 us (94%)
  local copies, waits for them, and re-layouts  16 us (4%)
    pallas_call x1, Pallas kernels, back_call(): pl.pallas_call(functools.partial(back_kernel, dp_count), out_shape=[grad(...  305 us
    pallas_call x1, Pallas kernels, front_call(): pl.pallas_call(functools.partial(front_kernel, dp_count), out_shape=out_s...  89.1 us
    unnamed x37, local copies, waits for them, and re-layouts  13.4 us

profile of v8, /device:TPU:0, one launch (start us, length us, event | category | flops | bytes accessed | tf_op | source)
XLA Modules:
  0.0 411.3 jit_solution(3890423449047181721)
XLA Ops:
  0.6 1.3 broadcast_in_dim.6.refs_13_.refs_42_
  1.9 1.3 broadcast_in_dim.7.refs_14_.refs_43_
  3.2 89.1 %shard_map.246 = (bf16[1536,512]{1,0:T(8,128)(2,1)}, bf16[1536,512]{1,0:T(8,128)(2,1)}, bf16[1536,512]{1,0:T(8,128)(2,1)}, bf16[512,384]{1,0:T(8,128)(2,1)}, bf1...) custom-call(s32[1,4]{1,0:T(1,128)} %refs_0_.3, ...), custom_call_target="tpu_custom_call" | custom-call | flops 24159191040 | bytes 67108864 | tf_op jit(solution)/shard_map/pallas_call | solution.py:1599
  92.3 305.4 %shard_map.247 = (f32[192,1024]{1,0:T(8,128)}, f32[192,1024]{1,0:T(8,128)}, f32[192,1024]{1,0:T(8,128)}, f32[192,384]{1,0:T(8,128)}, f32[192,384]{1,0:T(8,128)},...) custom-call(s32[1,4]{1,0:T(1,128)} %refs_0_.3, ...), custom_call_target="tpu_custom_call" | custom-call | flops 19327352832 | bytes 67108864 | tf_op jit(solution)/shard_map/pallas_call | solution.py:1037
  397.7 0.0 copy-start
  397.7 3.9 copy.41
  401.6 0.0 copy-done
  401.6 0.0 copy-start.5
  401.7 1.7 copy.42
  403.3 0.6 copy.43
  403.9 0.0 copy-done.7
  403.9 0.7 copy.44
  404.6 0.0 copy-done.6
  404.6 0.7 copy.45
  405.3 0.7 copy.46
  406.1 0.6 copy.47
  406.6 0.0 copy-done.8
  406.6 0.6 copy.48
  407.2 0.7 copy.49
  407.9 0.6 copy.50
  408.5 0.9 copy.51
  409.4 0.0 copy-done.2
  409.4 0.9 copy.52
  410.3 0.9 copy.53
  (17 shorter events, 0.0 us)
Async XLA Ops:
  397.7 3.9 copy-start
  401.6 1.7 copy-start.11
  401.6 2.3 copy-start.7
  401.6 3.0 copy-start.6
  401.6 3.7 copy-start.5
  401.6 4.4 %copy-start.9 = (f32[3,32]{1,0:T(4,128)S(1)}, f32[3,32]{1,0:T(4,128)}, u32[]{:S(2)}) copy-start(f32[3,32]{1,0:T(4,128)} %get-tuple-element.122) | copy-start | bytes 1156
  401.6 5.0 %copy-start.8 = (f32[3,16]{1,0:T(4,128)S(1)}, f32[3,16]{1,0:T(4,128)}, u32[]{:S(2)}) copy-start(f32[3,16]{1,0:T(4,128)} %get-tuple-element.123) | copy-start | bytes 580
  401.6 5.6 %copy-start.4 = (f32[192,384]{1,0:T(8,128)S(1)}, f32[192,384]{1,0:T(8,128)}, u32[]{:S(2)}) copy-start(f32[192,384]{1,0:T(8,128)} %get-tuple-element.98) | copy-start | bytes 884740
  401.6 6.3 %copy-start.10 = (f32[1,192]{1,0:T(1,128)S(1)}, f32[1,192]{1,0:T(1,128)}, u32[]{:S(2)}) copy-start(f32[1,192]{1,0:T(1,128)} %get-tuple-element.99) | copy-start | bytes 2308
  401.7 6.8 %copy-start.3 = (f32[192,1024]{1,0:T(8,128)S(1)}, f32[192,1024]{1,0:T(8,128)}, u32[]{:S(2)}) copy-start(f32[192,1024]{1,0:T(8,128)} %get-tuple-element.126) | copy-start | bytes 2359300
  403.3 6.0 %copy-start.2 = (f32[192,1024]{1,0:T(8,128)S(1)}, f32[192,1024]{1,0:T(8,128)}, u32[]{:S(2)}) copy-start(f32[192,1024]{1,0:T(8,128)} %get-tuple-element.127) | copy-start | bytes 2359300
  403.3 6.9 %copy-start.1 = (f32[192,1024]{1,0:T(8,128)S(1)}, f32[192,1024]{1,0:T(8,128)}, u32[]{:S(2)}) copy-start(f32[192,1024]{1,0:T(8,128)} %get-tuple-element.102) | copy-start | bytes 2359300
